TPU v7x, 32 devices: a whole 2x2x4 slice. The times are simulated.
32 devices in a mesh: dom: 2 (over y), chol: 4 (over z), walk: 4 (over x, core).
Axes of the slice: x: 2, y: 2, z: 4, core: 2. Of those that a mesh axis runs over, the one named last changes fastest.
Arguments:
- chol_vectors: bfloat16 [32, 100, 1000], P('chol', None, 'walk'), may hold values from -0.0047302246 to 0.0047302246
- green_blocks: bfloat16 [8, 4, 100, 1000], P(('dom', 'walk'), 'chol'), parts along dimension 0, may hold values from -6 to 6
- phase_codes: int32 [8, 4], P(('dom', 'walk')), parts along dimension 0, may hold values from 0 to 7
- occupations: int32 [8, 4, 100], P(('dom', 'walk'), 'chol'), parts along dimension 0, may hold values from 0 to 99, each once within a row
Outputs:
- chol_grad: float32 [64, 100, 1000], P(('dom', 'chol'), None, 'walk'), parts along dimension 0
- energies: float32 [8, 4], P(('dom', 'walk'), 'chol'), parts along dimension 0
There are 2 independent parts, one for each index of `dom`. A program takes and returns all parts, laid end to end along the dimension named above; an argument that names none is the same for every part. Nothing has to cross between parts.
Inputs may be any that keep to these rules, and one draw needn't show every extreme that they name: Each walker's row of occupations is a permutation of 0 to 99.
All inputs are finite; a program needn't handle non-finite values.
Results may differ from a plain program's by a relative error of at most 0.0029.
Values may be sent and summed in bfloat16 or wider, within the bound.
No kernel may reach another device: no remote copies, remote signals or barrier semaphores. Data moves between devices by JAX's collectives and lax.ppermute only.
A program may use at most 128 MiB of HBM per device.

v0:
```python
import jax
import jax.numpy as jnp
from jax import lax
from jax.sharding import PartitionSpec as P


def body(chol_vectors, green_blocks, phase_codes, occupations):
    full_slab = lax.all_gather(chol_vectors, "walk", axis=2, tiled=True)
    nocc = green_blocks.shape[2]
    onehot = (
        occupations[0][:, :, None] == jnp.arange(nocc, dtype=jnp.int32)[None, None, :]
    ).astype(jnp.bfloat16)
    theta = jnp.einsum(
        "wjs,wsp->wjp", onehot, green_blocks[0], preferred_element_type=jnp.float32
    ).astype(jnp.bfloat16)
    weight = jnp.cos(jnp.pi * phase_codes[0].astype(jnp.float32) / 4.0)
    piece = lax.all_gather(theta, "chol", axis=0, tiled=True)
    tmat = jnp.einsum("gip,wjp->gwij", full_slab, piece, preferred_element_type=jnp.float32)
    energy = -0.5 * jnp.einsum("gwij,gwji->w", tmat, tmat)
    cotan = (-weight[None, :, None, None] * tmat).astype(jnp.bfloat16)
    grad_acc = jnp.einsum("gwji,wjp->gip", cotan, piece, preferred_element_type=jnp.float32)
    energy_acc = energy
    grad_acc, energy_acc = (grad_acc, energy_acc)
    energies = lax.psum_scatter(energy_acc, "chol", scatter_dimension=0, tiled=True)[None, :]
    summed = lax.psum(grad_acc, "walk")
    width = chol_vectors.shape[2]
    chol_grad = lax.dynamic_slice_in_dim(summed, lax.axis_index("walk") * width, width, 2)
    return (chol_grad, energies)


def solution(mesh):
    placed = (
        P("chol", None, "walk"),
        P(("dom", "walk"), "chol", None, None),
        P(("dom", "walk"), None),
        P(("dom", "walk"), "chol", None),
    )
    return jax.shard_map(
        body,
        mesh=mesh,
        in_specs=placed,
        out_specs=(P(("dom", "chol"), None, "walk"), P(("dom", "walk"), "chol")),
        check_vma=False,
    )
```

profile of v0, /device:TPU:0, one launch (start us, length us, event | category | flops | bytes accessed | tf_op | source)
XLA Modules:
  0.0 127.5 jit_solution(1747782089062413354)
XLA Ops:
  7.2 0.0 copy-start
  7.2 0.0 copy-start.1
  7.2 0.0 all-gather.4.cloned.1.call-start
  7.2 2.3 %copy.12 = bf16[8,100,250]{1,0,2:T(8,128)(2,1)} copy(bf16[8,100,250]{2,0,1:T(8,128)(2,1)} %param.4) | data formatting | bytes 800000 | tf_op args[0]
  9.6 0.0 all-gather.4.cloned.1.call-update
  9.6 0.0 all-reduce.3.cloned.1.call-start
  9.6 0.0 copy-done
  9.7 0.9 fusion.4
  10.6 0.0 copy-done.1
  10.6 22.1 %all-gather.1 = bf16[4,100,1000]{2,1,0:T(8,128)(2,1)S(1)} all-gather(bf16[1,100,1000]{2,1,0:T(8,128)(2,1)S(1)} %fusion.4), channel_id=2, replica_groups=mesh['dom'=2,'chol'=4,'walk'=4] {'chol'}, dimensions={0}, use_global_device_ids=true | all-gather | bytes 1000000 | tf_op jit(solution)/shard_map/all_gather | solution.py:17
  32.7 2.5 %all-gather.4.cloned.1.call-done = bf16[8,100,1000]{1,0,2:T(8,128)(2,1)} async-done(((bf16[8,100,250]{1,0,2:T(8,128)(2,1)}), bf16[8,100,1000]{1,0,2:T(8,128)(2,1)}) %all-gather.4.cloned.1.call-update) | async-done | bytes 1600016 | tf_op jit(solution)/shard_map/all_gather | solution.py:8
  35.2 4.4 %copy.13 = bf16[8,100,1000]{2,1,0:T(8,128)(2,1)} copy(bf16[8,100,1000]{1,0,2:T(8,128)(2,1)} %all-gather.4.cloned.1.call-done) | data formatting | bytes 3200000 | tf_op jit(solution)/shard_map/all_gather | solution.py:8
  39.6 2.5 %fusion.2 = f32[4,100,8,100]{3,1,2,0:T(8,128)S(1)} fusion(bf16[8,100,1000]{2,1,0:T(8,128)(2,1)} %copy.13, bf16[4,100,1000]{2,1,0:T(8,128)(2,1)S(1)} %all-gather.1), kind=kOutput, calls=%fused_computation.5 | convolution fusion | flops 640000000 | bytes 3680000 | tf_op jit(solution)/shard_map/gip,wjp->gwij/dot_general | solution.py:18
  42.1 2.9 %convolution_bitcast_fusion = f32[8,100,1000]{2,1,0:T(8,128)} fusion(f32[4,100,8,100]{3,1,2,0:T(8,128)S(1)} %fusion.2, bf16[4,100,1000]{2,1,0:T(8,128)(2,1)S(1)} %all-gather.1, f32[4]{0:T(128)S(1)} %negate_bitcast_fusion), kind=kOutput, calls=%fused_computation | convolution fusion | flops 640640000 | bytes 5280016 | tf_op jit(solution)/shard_map/gwji,wjp->gip/dot_general | solution.py:21
  45.1 0.0 all-reduce.3.cloned.1.call-update
  45.1 1.8 %copy.21 = f32[4,8,100,100]{3,2,1,0:T(8,128)} copy(f32[4,8,100,100]{2,3,1,0:T(8,128)S(1)} %bitcast.37) | data formatting | bytes 2560000
  46.9 0.0 copy-start.2
  46.9 1.8 %fusion = f32[4]{0:T(128)S(1)} fusion(f32[4,8,100,100]{3,2,1,0:T(8,128)} %copy.21, f32[4,100,8,100]{3,1,2,0:T(8,128)S(1)} %fusion.2), kind=kLoop, calls=%fused_computation.2 | loop fusion | flops 639996 | bytes 2560016 | tf_op jit(solution)/shard_map/gwij,gwji->w/dot_general | solution.py:19
  48.7 0.0 copy-done.2
  48.7 0.6 dynamic-slice
  49.3 11.7 %all-reduce = f32[4]{0:T(128)S(1)} all-reduce(f32[4]{0:T(128)S(1)} %broadcast_multiply_fusion), channel_id=3, replica_groups=mesh['dom'=2,'chol'=4,'walk'=4] {'chol'}, use_global_device_ids=true, to_apply=%region_1.0.clone | all-reduce | flops 4 | bytes 32
  60.9 1.2 dynamic-slice.1
  62.1 55.8 %all-reduce.3.cloned.1.call-done = f32[8,100,1000]{2,1,0:T(8,128)} async-done(((f32[8,100,1000]{2,1,0:T(8,128)}), f32[8,100,1000]{2,1,0:T(8,128)}) %all-reduce.3.cloned.1.call-update) | async-done | bytes 3200016 | tf_op jit(solution)/shard_map/psum | solution.py:25
  118.0 1.6 %constant_dynamic-slice_fusion = f32[8,100,250]{2,1,0:T(8,128)S(1)} fusion(f32[8,100,1000]{2,1,0:T(8,128)} %all-reduce.3.cloned.1.call-done, s32[]{:T(128)S(6)} %select_n.3), kind=kLoop, calls=%fused_computation.18 | loop fusion | bytes 1600004 | tf_op jit(solution)/shard_map/dynamic_slice | solution.py:27
  119.6 1.1 copy.14
  (2 shorter events, 0.0 us)
Async XLA Ops:
  7.2 2.5 %copy-start = (bf16[1,1,100,1000]{3,2,1,0:T(8,128)(2,1)S(1)}, bf16[1,1,100,1000]{3,2,1,0:T(8,128)(2,1)}, u32[]{:S(2)}) copy-start(bf16[1,1,100,1000]{3,2,1,0:T(8,128)(2,1)} %param.5) | copy-start | bytes 600004
  7.2 3.4 %copy-start.1 = (s32[1,4]{1,0:T(1,128)S(1)}, s32[1,4]{1,0:T(1,128)}, u32[]{:S(2)}) copy-start(s32[1,4]{1,0:T(1,128)} %param.6) | copy-start | bytes 52
  7.2 28.0 %all-gather.4.cloned.1.call-start = ((), (), s32[]{:S(2)}) async-start(), calls=%async_computation | async-start | bytes 2560000 | tf_op jit(solution)/shard_map/all_gather | solution.py:8
  9.6 108.4 %all-reduce.3.cloned.1.call-start = ((), (), s32[]{:S(2)}) async-start(), calls=%async_computation.1 | async-start | bytes 6815744 | tf_op jit(solution)/shard_map/psum | solution.py:25
  46.9 1.8 %copy-start.2 = (u32[32]{0:T(128)S(1)}, u32[32]{0:T(128)}, u32[]{:S(2)}) copy-start(u32[32]{0:T(128)} %constant.24) | copy-start | bytes 388
Sparse Core Ops, SparseCore 0:
  10.2 24.9 all-gather.3
  45.2 72.6 all-reduce.2
where the time goes:
time: 128 us
  waiting for transfers between devices  58.3 us (46%)
  blocking collectives  33.8 us (26%)
  between operations  14.1 us (11%)
  local copies, waits for them, and re-layouts  13.1 us (10%)
  matrix products  6.36 us (5%)
  other arithmetic  1.84 us (1%)
    psum x1, waiting for transfers between devices, body(): summed = lax.psum(grad_acc, 'walk')  55.8 us
    all_gather x1, blocking collectives, body(): piece = lax.all_gather(theta, 'chol', axis=0, tiled=True)  22.1 us
    unnamed x1, blocking collectives  11.7 us
    unnamed x11, local copies, waits for them, and re-layouts  7.08 us
    all_gather x1, local copies, waits for them, and re-layouts, body(): full_slab = lax.all_gather(chol_vectors, 'walk', axis=2, tiled=True)  4.41 us
    dot_general x1, matrix products, body(): jnp.einsum('gwji,wjp->gip', cotan, piece, preferred_element_type=jnp.floa...  2.93 us
  transfers between devices with their start and end apart: 2, of which 2 were waited for; matrix products, arithmetic and copies ran while one was open for 5% of the time, Pallas kernels for 0%

commit v1 on v0

v1 whole, which is shorter than its diff:
```python
import functools

import jax
import jax.numpy as jnp
from jax import lax
from jax.experimental import pallas as pl
from jax.experimental.pallas import tpu as pltpu
from jax.sharding import PartitionSpec as P

LANES = 128
GRANT = 48 * 1024 * 1024


def ceil_to(value, step):
    return -(-value // step) * step


def prep_theta(occ_ref, code_ref, green_ref, out_ref, *, width, padded):
    nocc, norb = green_ref.shape
    rows = out_ref.shape[0]
    pick = (lax.broadcasted_iota(jnp.int32, (nocc, nocc), 0) == occ_ref[...]).astype(jnp.bfloat16)
    theta = lax.dot_general(pick, green_ref[...], (((0,), (0,)), ((), ())), preferred_element_type=jnp.float32)
    mine = lax.broadcasted_iota(jnp.int32, code_ref.shape, 1) == lax.axis_index("chol")
    code = jnp.sum(jnp.where(mine, code_ref[...], 0).astype(jnp.float32), axis=1, keepdims=True)
    out_ref[...] = jnp.zeros_like(out_ref)
    for k in range(norb // width):
        out_ref[:nocc, padded * k:padded * k + width] = theta[:, width * k:width * (k + 1)].astype(jnp.bfloat16)
    out_ref[:, width:width + 1] = jnp.broadcast_to(code, (rows, 1)).astype(jnp.bfloat16)


def prep_chol(chol_ref, same_ref, other_ref):
    half, nocc = same_ref.shape[0], chol_ref.shape[1]
    width = chol_ref.shape[2]
    h = lax.rem(lax.axis_index("walk"), 2)
    for ref, start in ((same_ref, h * half), (other_ref, (1 - h) * half)):
        ref[...] = jnp.zeros_like(ref)
        for g in range(half):
            ref[g, :nocc, :width] = chol_ref[start + g]


def main(*refs, walkers, half, rows, width, padded):
    thetas, refs = refs[:walkers], refs[walkers:]
    chols, refs = refs[:4], refs[4:]
    own_ref, core_ref, xsame_ref, xother_ref, energy_ref, theta_s, chol_s, cotan_s = refs
    k = lax.axis_index("walk")
    theta_s[...] = jnp.zeros_like(theta_s)
    chol_s[...] = jnp.zeros_like(chol_s)
    for w in range(walkers):
        theta_s[w * LANES:w * LANES + rows, :] = thetas[w][...]
    for s in range(4):
        place = pl.ds(pl.multiple_of((k ^ s) * padded, padded), padded)
        for g in range(half):
            chol_s[g * LANES:g * LANES + rows, place] = chols[s][g]
    tmat = lax.dot_general(
        theta_s[...], chol_s[...], (((1,), (1,)), ((), ())), preferred_element_type=jnp.float32
    )
    for w in range(walkers):
        code = thetas[w][0:8, padded - LANES:padded].astype(jnp.float32)
        lane = lax.broadcasted_iota(jnp.int32, (8, LANES), 1) == width - (padded - LANES)
        code = jnp.sum(jnp.where(lane, code, 0.0), axis=1, keepdims=True)[0:1]
        weight = jnp.cos(jnp.pi * code / 4.0)
        total = jnp.zeros((LANES, LANES), jnp.float32)
        for g in range(half):
            block = tmat[w * LANES:(w + 1) * LANES, g * LANES:(g + 1) * LANES]
            total += block * block.T
            cotan_s[g * LANES:(g + 1) * LANES, w * LANES:(w + 1) * LANES] = (-weight * block).astype(jnp.bfloat16)
        energy_ref[w:w + 1, :] = -0.5 * jnp.sum(total, axis=0, keepdims=True)
    for ref, s in ((xsame_ref, 2), (xother_ref, 3), (core_ref, 1), (own_ref, 0)):
        place = pl.ds(pl.multiple_of((k ^ s) * padded, padded), padded)
        grad = jnp.dot(cotan_s[...], theta_s[:, place], preferred_element_type=jnp.float32)
        for g in range(half):
            ref[g] = grad[g * LANES:g * LANES + rows].astype(ref.dtype)


def finish(own_ref, core_ref, xsame_ref, xother_ref, out_ref):
    half = own_ref.shape[0]
    nocc, width = out_ref.shape[1:]
    h = lax.rem(lax.axis_index("walk"), 2)
    for g in range(half):
        out_ref[h * half + g] = (own_ref[g] + xsame_ref[g].astype(jnp.float32))[:nocc, :width]
        out_ref[(1 - h) * half + g] = (core_ref[g] + xother_ref[g].astype(jnp.float32))[:nocc, :width]


def call(kernel, outs, *operands, scratch=()):
    return pl.pallas_call(
        kernel,
        out_shape=outs,
        in_specs=[pl.BlockSpec(memory_space=pltpu.VMEM)] * len(operands),
        out_specs=jax.tree.map(lambda _: pl.BlockSpec(memory_space=pltpu.VMEM), outs),
        scratch_shapes=scratch,
        compiler_params=pltpu.CompilerParams(vmem_limit_bytes=GRANT),
    )(*operands)


def swap(x, axis, size, flip):
    return lax.ppermute(x, axis, [(i, i ^ flip) for i in range(size)])


def body(chol_vectors, green_blocks, phase_codes, occupations, *, nchol, nwalk):
    gdev, nocc, width = chol_vectors.shape
    norb = green_blocks.shape[3]
    half = gdev // 2
    rows = ceil_to(nocc, 8)
    padded = ceil_to(width, LANES)
    bf16, f32 = jnp.bfloat16, jnp.float32

    theta = call(
        functools.partial(prep_theta, width=width, padded=padded),
        jax.ShapeDtypeStruct((rows, padded * nwalk), bf16),
        occupations.reshape(1, nocc),
        phase_codes,
        green_blocks.reshape(nocc, norb),
    )
    piece = jax.ShapeDtypeStruct((half, rows, padded), bf16)
    same, other = call(prep_chol, (piece, piece), chol_vectors)

    thetas = [theta] + [swap(theta, "chol", nchol, d) for d in range(1, nchol)]
    chols = [same, swap(other, "walk", nwalk, 1), swap(same, "walk", nwalk, 2), swap(other, "walk", nwalk, 3)]
    partners = [swap(t, "walk", nwalk, 1) for t in thetas]

    wide = jax.ShapeDtypeStruct((half, rows, padded), f32)
    step = 4
    grads = None
    energy = [[], []]
    for first in range(0, nchol, step):
        group = thetas[first:first + step] + partners[first:first + step]
        walkers = len(group)
        last = nchol <= step
        kind = piece if last else wide
        *terms, e = call(
            functools.partial(main, walkers=walkers, half=half, rows=rows, width=width, padded=padded),
            (wide, wide, kind, kind, jax.ShapeDtypeStruct((walkers, LANES), f32)),
            *group,
            *chols,
            scratch=[
                pltpu.VMEM((walkers * LANES, padded * nwalk), bf16),
                pltpu.VMEM((half * LANES, padded * nwalk), bf16),
                pltpu.VMEM((half * LANES, walkers * LANES), bf16),
            ],
        )
        grads = terms if grads is None else [a + b for a, b in zip(grads, terms)]
        energy[0].append(e[:walkers // 2])
        energy[1].append(e[walkers // 2:])
    own, core, xsame, xother = grads
    xsame = swap(xsame.astype(bf16), "walk", nwalk, 2)
    xother = swap(xother.astype(bf16), "walk", nwalk, 3)
    core = swap(core, "walk", nwalk, 1)

    mine, theirs = (jnp.concatenate(e) if len(e) > 1 else e[0] for e in energy)
    part = mine + swap(theirs, "walk", nwalk, 1)
    flip = nchol // 2
    while flip:
        part = part[:flip] + swap(part[flip:], "chol", nchol, flip)
        flip //= 2
    energies = jnp.sum(part).reshape(1, 1)

    chol_grad = call(finish, jax.ShapeDtypeStruct((gdev, nocc, width), f32), own, core, xsame, xother)
    return chol_grad, energies


def solution(mesh):
    placed = (
        P("chol", None, "walk"),
        P(("dom", "walk"), "chol", None, None),
        P(("dom", "walk"), None),
        P(("dom", "walk"), "chol", None),
    )
    return jax.shard_map(
        functools.partial(body, nchol=mesh.shape["chol"], nwalk=mesh.shape["walk"]),
        mesh=mesh,
        in_specs=placed,
        out_specs=(P(("dom", "chol"), None, "walk"), P(("dom", "walk"), "chol")),
        check_vma=False,
    )
```

time: 128 us -> 45.6 us (0.36)
  blocking collectives: 33.8 us -> 0 us
  waiting for transfers between devices: 58.3 us -> 27.2 us
  between operations: 14.1 us -> 0.71 us
  starting transfers between devices: 0.08 us -> 10.5 us
  local copies, waits for them, and re-layouts: 13.1 us -> 2.83 us
  matrix products: 6.36 us -> 0 us
  Pallas kernels: 0 us -> 3.25 us
    psum x1 -> x0, waiting for transfers between devices: 55.8 us -> none  [body(): summed = lax.psum(grad_acc, 'walk')]
    ppermute x0 -> x16, waiting for transfers between devices: none -> 27.2 us  [swap(): return lax.ppermute(x, axis, [(i, i ^ flip) for i in range(size)])]
    all_gather x1 -> x0, blocking collectives: 22.1 us -> none  [body(): piece = lax.all_gather(theta, 'chol', axis=0, tiled=True)]
    unnamed x1 -> x0, blocking collectives: 11.7 us -> none
    ppermute x0 -> x16, starting transfers between devices: none -> 10.5 us  [swap(): return lax.ppermute(x, axis, [(i, i ^ flip) for i in range(size)])]
    dot_general x3 -> x0, matrix products: 6.36 us -> none  [the longest x1 2.93 us: body(): jnp.einsum('gwji,wjp->gip', cotan, piece, preferred_element_type=jnp.floa...]
    all_gather x1 -> x0, local copies, waits for them, and re-layouts: 4.41 us -> none  [body(): full_slab = lax.all_gather(chol_vectors, 'walk', axis=2, tiled=True)]
    unnamed x11 -> x10, local copies, waits for them, and re-layouts: 7.08 us -> 2.81 us
  transfers between devices with their start and end apart: 2 -> 16, of which waited for: 2 -> 9; matrix products, arithmetic and copies ran while one was open for 5% -> 2% of each run, Pallas kernels for 0% -> 0%
where the time goes in v1:
time: 45.6 us; the launch traced here: 45.1 us
  waiting for transfers between devices  27.2 us (60%)
  starting transfers between devices  10.5 us (23%)
  Pallas kernels  3.25 us (7%)
  local copies, waits for them, and re-layouts  2.83 us (6%)
  between operations  0.71 us (2%)
  other arithmetic  0.61 us (1%)
    ppermute x16, waiting for transfers between devices, swap(): return lax.ppermute(x, axis, [(i, i ^ flip) for i in range(size)])  27.2 us
    ppermute x16, starting transfers between devices, swap(): return lax.ppermute(x, axis, [(i, i ^ flip) for i in range(size)])  10.5 us
    pallas_call x4, Pallas kernels, call(): pl.pallas_call(kernel, out_shape=outs, in_specs=[pl.BlockSpec(memory_spac...  3.25 us
    unnamed x10, local copies, waits for them, and re-layouts  2.81 us
  transfers between devices with their start and end apart: 16, of which 9 were waited for; matrix products, arithmetic and copies ran while one was open for 2% of the time, Pallas kernels for 0%

profile of v1, /device:TPU:0, one launch (start us, length us, event | category | flops | bytes accessed | tf_op | source)
XLA Modules:
  0.0 45.1 jit_solution(12442236140803418160)
XLA Ops:
  0.6 0.0 copy-start.1
  0.6 0.0 copy-start.2
  0.7 0.6 %copy-done.1 = s32[1,1,100]{2,1,0:T(1,128)S(1)} copy-done((s32[1,1,100]{2,1,0:T(1,128)S(1)}, s32[1,1,100]{2,1,0:T(1,128)}, u32[]{:S(2)}) %copy-start.1) | copy-done | bytes 424
  1.3 0.0 copy-done.2
  1.3 0.0 copy-start
  1.3 0.9 %copy-done = bf16[1,1,100,1000]{3,2,1,0:T(8,128)(2,1)S(1)} copy-done((bf16[1,1,100,1000]{3,2,1,0:T(8,128)(2,1)S(1)}, bf16[1,1,100,1000]{3,2,1,0:T(8,128)(2,1)}, u32[]{:S(2)}) %copy-start) | copy-done | bytes 200024
  2.2 0.0 copy-start.3
  2.2 0.3 shard_map.59.refs_0_
  2.6 0.5 %collective-permute-start.3 = (bf16[104,1024]{1,0:T(8,128)(2,1)S(1)}, bf16[104,1024]{1,0:T(8,128)(2,1)S(1)}, u32[]{:S(2)}, u32[]{:S(2)}) collective-permute-start(bf16[104,1024]{1,0:T(8,128)(2,1)S(1)} %shard_map.59.refs_0_), channel_id=1, source_target_pairs={{0,1},{1,0},{2,3},{3,2},{4,5},{5,4},{6,7},{7,6},{8,9},{9,8},{10,11... | collective-permute-start | bytes 638984 | tf_op jit(solution)/shard_map/ppermute | solution.py:96
  3.1 4.7 %collective-permute-start.2 = (bf16[104,1024]{1,0:T(8,128)(2,1)S(1)}, bf16[104,1024]{1,0:T(8,128)(2,1)S(1)}, u32[]{:S(2)}, u32[]{:S(2)}) collective-permute-start(bf16[104,1024]{1,0:T(8,128)(2,1)S(1)} %shard_map.59.refs_0_), channel_id=1, source_target_pairs={{0,12},{4,8},{8,4},{12,0},{1,13},{5,9},{9,5},{13,1},{2,14},{6,10},... | collective-permute-start | bytes 638984 | tf_op jit(solution)/shard_map/ppermute | solution.py:96
  7.8 0.0 collective-permute-start.1
  7.8 0.6 %collective-permute-start = (bf16[104,1024]{1,0:T(8,128)(2,1)S(1)}, bf16[104,1024]{1,0:T(8,128)(2,1)S(1)}, u32[]{:S(2)}, u32[]{:S(2)}) collective-permute-start(bf16[104,1024]{1,0:T(8,128)(2,1)S(1)} %shard_map.59.refs_0_), channel_id=1, source_target_pairs={{0,4},{4,0},{8,12},{12,8},{1,5},{5,1},{9,13},{13,9},{2,6},{6,2},{1... | collective-permute-start | bytes 638984 | tf_op jit(solution)/shard_map/ppermute | solution.py:96
  8.4 0.0 copy-done.3
  8.4 0.1 copy.6.chol_ref
  8.5 0.1 shard_map.60
  8.6 1.7 %collective-permute-start.8 = (bf16[4,104,256]{2,1,0:T(8,128)(2,1)S(1)}, bf16[4,104,256]{2,1,0:T(8,128)(2,1)S(1)}, u32[]{:S(2)}, u32[]{:S(2)}) collective-permute-start(bf16[4,104,256]{2,1,0:T(8,128)(2,1)S(1)} %get-tuple-element.9.refs_8_), channel_id=1, source_target_pairs={{0,2},{1,3},{2,0},{3,1},{4,6},{5,7},{6,4},{7,5},{8,10},{9,11},{10,... | collective-permute-start | bytes 638984 | tf_op jit(solution)/shard_map/ppermute | solution.py:96
  10.3 0.0 collective-permute-done.3.refs_4_
  10.3 0.0 collective-permute-start.9
  10.3 3.7 %collective-permute-done.2.refs_3_ = bf16[104,1024]{1,0:T(8,128)(2,1)S(1)} collective-permute-done((bf16[104,1024]{1,0:T(8,128)(2,1)S(1)}, bf16[104,1024]{1,0:T(8,128)(2,1)S(1)}, u32[]{:S(2)}, u32[]{:S(2)}) %collective-permute-start.2) | collective-permute-done | bytes 213024 | tf_op jit(solution)/shard_map/ppermute | solution.py:96
  14.0 0.0 collective-permute-start.7
  14.0 12.5 %collective-permute-done.1.refs_2_ = bf16[104,1024]{1,0:T(8,128)(2,1)S(1)} collective-permute-done((bf16[104,1024]{1,0:T(8,128)(2,1)S(1)}, bf16[104,1024]{1,0:T(8,128)(2,1)S(1)}, u32[]{:S(2)}, u32[]{:S(2)}) %collective-permute-start.1) | collective-permute-done | bytes 213024 | tf_op jit(solution)/shard_map/ppermute | solution.py:96
  26.5 0.0 collective-permute-start.6
  26.5 0.0 collective-permute-done.refs_1_
  26.5 0.5 %collective-permute-start.5 = (bf16[104,1024]{1,0:T(8,128)(2,1)S(1)}, bf16[104,1024]{1,0:T(8,128)(2,1)S(1)}, u32[]{:S(2)}, u32[]{:S(2)}) collective-permute-start(bf16[104,1024]{1,0:T(8,128)(2,1)S(1)} %collective-permute-done.1.refs_2_), channel_id=1, source_target_pairs={{0,1},{1,0},{2,3},{3,2},{4,5},{5,4},{6,7},{7,6},{8,9},{9,8},{10,11... | collective-permute-start | bytes 638984 | tf_op jit(solution)/shard_map/ppermute | solution.py:96
  27.0 0.0 collective-permute-done.8.refs_10_
  27.0 0.1 collective-permute-start.4
  27.1 0.0 collective-permute-done.9.refs_11_
  27.1 0.0 collective-permute-done.7.refs_9_
  27.1 0.9 %collective-permute-done.6.refs_7_ = bf16[104,1024]{1,0:T(8,128)(2,1)S(1)} collective-permute-done((bf16[104,1024]{1,0:T(8,128)(2,1)S(1)}, bf16[104,1024]{1,0:T(8,128)(2,1)S(1)}, u32[]{:S(2)}, u32[]{:S(2)}) %collective-permute-start.6) | collective-permute-done | bytes 213024 | tf_op jit(solution)/shard_map/ppermute | solution.py:96
  27.9 0.3 collective-permute-done.5.refs_6_
  28.3 0.3 collective-permute-done.4.refs_5_
  28.6 2.8 %shard_map.61 = (f32[4,104,256]{2,1,0:T(8,128)S(1)}, f32[4,104,256]{2,1,0:T(8,128)S(1)}, bf16[4,104,256]{2,1,0:T(8,128)(2,1)S(1)}, bf16[4,104,256]{2,1,0:T(8,128)(2,1)S(1)}, f32[8,128]{1,0:T(8,128)S(1)}) custom-call(bf16[104,1024]{1,0:T(8,128)(2,1)S(1)} %shard_map.59.refs_0_, bf16[104,1024]{1,0:T(8,128)(2,1)S(1)} %collective-permute-done.refs_1_, ...), custom_call_target="tpu_custom_call" | custom-call | tf_op jit(solution)/shard_map/pallas_call | solution.py:85
  31.4 0.3 collective-permute-start.13
  31.6 0.3 collective-permute-start.10
  31.9 0.6 %collective-permute-done.13 = f32[4,128]{1,0:T(4,128)S(1)} collective-permute-done((f32[4,128]{1,0:T(4,128)S(1)}, f32[4,128]{1,0:T(4,128)S(1)}, u32[]{:S(2)}, u32[]{:S(2)}) %collective-permute-start.13) | collective-permute-done | bytes 2080 | tf_op jit(solution)/shard_map/ppermute | solution.py:96
  32.6 0.0 collective-permute-start.14
  32.6 1.5 %collective-permute-start.11 = (bf16[4,104,256]{2,1,0:T(8,128)(2,1)S(1)}, bf16[4,104,256]{2,1,0:T(8,128)(2,1)S(1)}, u32[]{:S(2)}, u32[]{:S(2)}) collective-permute-start(bf16[4,104,256]{2,1,0:T(8,128)(2,1)S(1)} %get-tuple-element.13), channel_id=1, source_target_pairs={{0,2},{1,3},{2,0},{3,1},{4,6},{5,7},{6,4},{7,5},{8,10},{9,11},{10,... | collective-permute-start | bytes 638984 | tf_op jit(solution)/shard_map/ppermute | solution.py:96
  34.1 0.1 collective-permute-start.12
  34.2 2.8 %collective-permute-done.14 = f32[2,128]{1,0:T(2,128)S(1)} collective-permute-done((f32[2,128]{1,0:T(2,128)S(1)}, f32[2,128]{1,0:T(2,128)S(1)}, u32[]{:S(2)}, u32[]{:S(2)}) %collective-permute-start.14) | collective-permute-done | bytes 1056 | tf_op jit(solution)/shard_map/ppermute | solution.py:96
  37.1 0.2 collective-permute-start.15
  37.2 3.4 %collective-permute-done.15 = f32[1,128]{1,0:T(1,128)S(1)} collective-permute-done((f32[1,128]{1,0:T(1,128)S(1)}, f32[1,128]{1,0:T(1,128)S(1)}, u32[]{:S(2)}, u32[]{:S(2)}) %collective-permute-start.15) | collective-permute-done | bytes 544 | tf_op jit(solution)/shard_map/ppermute | solution.py:96
  40.6 0.6 %add_reduce_fusion = f32[]{:T(128)} fusion(f32[1,128]{1,0:T(1,128)S(1)} %collective-permute-done.15, f32[2,128]{1,0:T(2,128)S(1)} %slice_add_fusion.1), kind=kLoop, calls=%fused_computation.2 | loop fusion | flops 255 | bytes 1028 | tf_op jit(solution)/shard_map/reduce_sum | solution.py:155
  41.2 0.0 collective-permute-done.11.xsame_ref
  41.2 2.6 %collective-permute-done.12.xother_ref = bf16[4,104,256]{2,1,0:T(8,128)(2,1)S(1)} collective-permute-done((bf16[4,104,256]{2,1,0:T(8,128)(2,1)S(1)}, bf16[4,104,256]{2,1,0:T(8,128)(2,1)S(1)}, u32[]{:S(2)}, u32[]{:S(2)}) %collective-permute-start.12) | collective-permute-done | bytes 213024 | tf_op jit(solution)/shard_map/ppermute | solution.py:96
  43.9 0.0 collective-permute-done.10.core_ref
  43.9 0.1 shard_map.62
  43.9 1.1 %copy.7 = f32[8,100,250]{2,0,1:T(8,128)} copy(f32[8,100,250]{2,1,0:T(8,128)S(1)} %shard_map.62) | data formatting | bytes 1600000
  (5 shorter events, 0.0 us)
Async XLA Ops:
  0.6 0.7 %copy-start.1 = (s32[1,1,100]{2,1,0:T(1,128)S(1)}, s32[1,1,100]{2,1,0:T(1,128)}, u32[]{:S(2)}) copy-start(s32[1,1,100]{2,1,0:T(1,128)} %param.7) | copy-start | bytes 1204
  0.6 0.7 %copy-start.2 = (s32[1,4]{1,0:T(1,128)S(1)}, s32[1,4]{1,0:T(1,128)}, u32[]{:S(2)}) copy-start(s32[1,4]{1,0:T(1,128)} %code_ref.1) | copy-start | bytes 52
  1.3 0.9 %copy-start = (bf16[1,1,100,1000]{3,2,1,0:T(8,128)(2,1)S(1)}, bf16[1,1,100,1000]{3,2,1,0:T(8,128)(2,1)}, u32[]{:S(2)}) copy-start(bf16[1,1,100,1000]{3,2,1,0:T(8,128)(2,1)} %param.5) | copy-start | bytes 600004
  2.2 6.2 %copy-start.3 = (bf16[8,100,250]{2,0,1:T(8,128)(2,1)S(1)}, bf16[8,100,250]{2,0,1:T(8,128)(2,1)}, u32[]{:S(2)}) copy-start(bf16[8,100,250]{2,0,1:T(8,128)(2,1)} %param.4) | copy-start | bytes 1200004
  2.6 7.7 %collective-permute-start.3 = (bf16[104,1024]{1,0:T(8,128)(2,1)S(1)}, bf16[104,1024]{1,0:T(8,128)(2,1)S(1)}, u32[]{:S(2)}, u32[]{:S(2)}) collective-permute-start(bf16[104,1024]{1,0:T(8,128)(2,1)S(1)} %shard_map.59.refs_0_), channel_id=1, source_target_pairs={{0,1},{1,0},{2,3},{3,2},{4,5},{5,4},{6,7},{7,6},{8,9},{9,8},{10,11... | collective-permute-start | bytes 638984 | tf_op jit(solution)/shard_map/ppermute | solution.py:96
  3.1 10.9 %collective-permute-start.2 = (bf16[104,1024]{1,0:T(8,128)(2,1)S(1)}, bf16[104,1024]{1,0:T(8,128)(2,1)S(1)}, u32[]{:S(2)}, u32[]{:S(2)}) collective-permute-start(bf16[104,1024]{1,0:T(8,128)(2,1)S(1)} %shard_map.59.refs_0_), channel_id=1, source_target_pairs={{0,12},{4,8},{8,4},{12,0},{1,13},{5,9},{9,5},{13,1},{2,14},{6,10},... | collective-permute-start | bytes 638984 | tf_op jit(solution)/shard_map/ppermute | solution.py:96
  7.8 18.7 %collective-permute-start.1 = (bf16[104,1024]{1,0:T(8,128)(2,1)S(1)}, bf16[104,1024]{1,0:T(8,128)(2,1)S(1)}, u32[]{:S(2)}, u32[]{:S(2)}) collective-permute-start(bf16[104,1024]{1,0:T(8,128)(2,1)S(1)} %shard_map.59.refs_0_), channel_id=1, source_target_pairs={{0,8},{4,12},{8,0},{12,4},{1,9},{5,13},{9,1},{13,5},{2,10},{6,14},... | collective-permute-start | bytes 638984 | tf_op jit(solution)/shard_map/ppermute | solution.py:96
  7.8 18.7 %collective-permute-start = (bf16[104,1024]{1,0:T(8,128)(2,1)S(1)}, bf16[104,1024]{1,0:T(8,128)(2,1)S(1)}, u32[]{:S(2)}, u32[]{:S(2)}) collective-permute-start(bf16[104,1024]{1,0:T(8,128)(2,1)S(1)} %shard_map.59.refs_0_), channel_id=1, source_target_pairs={{0,4},{4,0},{8,12},{12,8},{1,5},{5,1},{9,13},{13,9},{2,6},{6,2},{1... | collective-permute-start | bytes 638984 | tf_op jit(solution)/shard_map/ppermute | solution.py:96
  8.6 18.4 %collective-permute-start.8 = (bf16[4,104,256]{2,1,0:T(8,128)(2,1)S(1)}, bf16[4,104,256]{2,1,0:T(8,128)(2,1)S(1)}, u32[]{:S(2)}, u32[]{:S(2)}) collective-permute-start(bf16[4,104,256]{2,1,0:T(8,128)(2,1)S(1)} %get-tuple-element.9.refs_8_), channel_id=1, source_target_pairs={{0,2},{1,3},{2,0},{3,1},{4,6},{5,7},{6,4},{7,5},{8,10},{9,11},{10,... | collective-permute-start | bytes 638984 | tf_op jit(solution)/shard_map/ppermute | solution.py:96
  10.3 16.8 %collective-permute-start.9 = (bf16[4,104,256]{2,1,0:T(8,128)(2,1)S(1)}, bf16[4,104,256]{2,1,0:T(8,128)(2,1)S(1)}, u32[]{:S(2)}, u32[]{:S(2)}) collective-permute-start(bf16[4,104,256]{2,1,0:T(8,128)(2,1)S(1)} %get-tuple-element.10), channel_id=1, source_target_pairs={{0,3},{1,2},{2,1},{3,0},{4,7},{5,6},{6,5},{7,4},{8,11},{9,10},{10,... | collective-permute-start | bytes 638984 | tf_op jit(solution)/shard_map/ppermute | solution.py:96
  14.0 13.1 %collective-permute-start.7 = (bf16[4,104,256]{2,1,0:T(8,128)(2,1)S(1)}, bf16[4,104,256]{2,1,0:T(8,128)(2,1)S(1)}, u32[]{:S(2)}, u32[]{:S(2)}) collective-permute-start(bf16[4,104,256]{2,1,0:T(8,128)(2,1)S(1)} %get-tuple-element.10), channel_id=1, source_target_pairs={{0,1},{1,0},{2,3},{3,2},{4,5},{5,4},{6,7},{7,6},{8,9},{9,8},{10,11... | collective-permute-start | bytes 638984 | tf_op jit(solution)/shard_map/ppermute | solution.py:96
  26.5 1.5 %collective-permute-start.6 = (bf16[104,1024]{1,0:T(8,128)(2,1)S(1)}, bf16[104,1024]{1,0:T(8,128)(2,1)S(1)}, u32[]{:S(2)}, u32[]{:S(2)}) collective-permute-start(bf16[104,1024]{1,0:T(8,128)(2,1)S(1)} %collective-permute-done.2.refs_3_), channel_id=1, source_target_pairs={{0,1},{1,0},{2,3},{3,2},{4,5},{5,4},{6,7},{7,6},{8,9},{9,8},{10,11... | collective-permute-start | bytes 638984 | tf_op jit(solution)/shard_map/ppermute | solution.py:96
  26.5 1.8 %collective-permute-start.5 = (bf16[104,1024]{1,0:T(8,128)(2,1)S(1)}, bf16[104,1024]{1,0:T(8,128)(2,1)S(1)}, u32[]{:S(2)}, u32[]{:S(2)}) collective-permute-start(bf16[104,1024]{1,0:T(8,128)(2,1)S(1)} %collective-permute-done.1.refs_2_), channel_id=1, source_target_pairs={{0,1},{1,0},{2,3},{3,2},{4,5},{5,4},{6,7},{7,6},{8,9},{9,8},{10,11... | collective-permute-start | bytes 638984 | tf_op jit(solution)/shard_map/ppermute | solution.py:96
  27.0 1.6 %collective-permute-start.4 = (bf16[104,1024]{1,0:T(8,128)(2,1)S(1)}, bf16[104,1024]{1,0:T(8,128)(2,1)S(1)}, u32[]{:S(2)}, u32[]{:S(2)}) collective-permute-start(bf16[104,1024]{1,0:T(8,128)(2,1)S(1)} %collective-permute-done.refs_1_), channel_id=1, source_target_pairs={{0,1},{1,0},{2,3},{3,2},{4,5},{5,4},{6,7},{7,6},{8,9},{9,8},{10,11... | collective-permute-start | bytes 638984 | tf_op jit(solution)/shard_map/ppermute | solution.py:96
  31.4 1.2 %collective-permute-start.13 = (f32[4,128]{1,0:T(4,128)S(1)}, f32[4,128]{1,0:T(4,128)S(1)}, u32[]{:S(2)}, u32[]{:S(2)}) collective-permute-start(f32[4,128]{1,0:T(4,128)S(1)} %slice.19), channel_id=1, source_target_pairs={{0,1},{1,0},{2,3},{3,2},{4,5},{5,4},{6,7},{7,6},{8,9},{9,8},{10,11... | collective-permute-start | bytes 6152 | tf_op jit(solution)/shard_map/ppermute | solution.py:96
  31.6 12.2 %collective-permute-start.10 = (f32[4,104,256]{2,1,0:T(8,128)S(1)}, f32[4,104,256]{2,1,0:T(8,128)S(1)}, u32[]{:S(2)}, u32[]{:S(2)}) collective-permute-start(f32[4,104,256]{2,1,0:T(8,128)S(1)} %get-tuple-element.12), channel_id=1, source_target_pairs={{0,1},{1,0},{2,3},{3,2},{4,5},{5,4},{6,7},{7,6},{8,9},{9,8},{10,11... | collective-permute-start | bytes 1277960 | tf_op jit(solution)/shard_map/ppermute | solution.py:96
  32.6 4.5 %collective-permute-start.14 = (f32[2,128]{1,0:T(2,128)S(1)}, f32[2,128]{1,0:T(2,128)S(1)}, u32[]{:S(2)}, u32[]{:S(2)}) collective-permute-start(f32[2,128]{1,0:T(2,128)S(1)} %slice.21), channel_id=1, source_target_pairs={{0,8},{4,12},{8,0},{12,4},{1,9},{5,13},{9,1},{13,5},{2,10},{6,14},... | collective-permute-start | bytes 3080 | tf_op jit(solution)/shard_map/ppermute | solution.py:96
  32.6 8.6 %collective-permute-start.11 = (bf16[4,104,256]{2,1,0:T(8,128)(2,1)S(1)}, bf16[4,104,256]{2,1,0:T(8,128)(2,1)S(1)}, u32[]{:S(2)}, u32[]{:S(2)}) collective-permute-start(bf16[4,104,256]{2,1,0:T(8,128)(2,1)S(1)} %get-tuple-element.13), channel_id=1, source_target_pairs={{0,2},{1,3},{2,0},{3,1},{4,6},{5,7},{6,4},{7,5},{8,10},{9,11},{10,... | collective-permute-start | bytes 638984 | tf_op jit(solution)/shard_map/ppermute | solution.py:96
  34.1 9.7 %collective-permute-start.12 = (bf16[4,104,256]{2,1,0:T(8,128)(2,1)S(1)}, bf16[4,104,256]{2,1,0:T(8,128)(2,1)S(1)}, u32[]{:S(2)}, u32[]{:S(2)}) collective-permute-start(bf16[4,104,256]{2,1,0:T(8,128)(2,1)S(1)} %get-tuple-element.14), channel_id=1, source_target_pairs={{0,3},{1,2},{2,1},{3,0},{4,7},{5,6},{6,5},{7,4},{8,11},{9,10},{10,... | collective-permute-start | bytes 638984 | tf_op jit(solution)/shard_map/ppermute | solution.py:96
  37.1 3.5 %collective-permute-start.15 = (f32[1,128]{1,0:T(1,128)S(1)}, f32[1,128]{1,0:T(1,128)S(1)}, u32[]{:S(2)}, u32[]{:S(2)}) collective-permute-start(f32[1,128]{1,0:T(1,128)S(1)} %slice.23), channel_id=1, source_target_pairs={{0,4},{4,0},{8,12},{12,8},{1,5},{5,1},{9,13},{13,9},{2,6},{6,2},{1... | collective-permute-start | bytes 1544 | tf_op jit(solution)/shard_map/ppermute | solution.py:96

commit v2 on v0

v2 whole, which is shorter than its diff:
```python
import functools

import jax
import jax.numpy as jnp
from jax import lax
from jax.experimental import pallas as pl
from jax.experimental.pallas import tpu as pltpu
from jax.sharding import PartitionSpec as P

LANES = 128
GRANT = 16 * 1024 * 1024
HBM = pltpu.MemorySpace.HBM
VMEM = pltpu.MemorySpace.VMEM
bf16, f32 = jnp.bfloat16, jnp.float32


def ceil_to(value, step):
    return -(-value // step) * step


def prep_theta(occ_hbm, code_hbm, green_hbm, out_ref, occ_ref, code_ref, green_ref, sems, *, width, padded):
    copies = [
        pltpu.make_async_copy(src, dst, sems.at[i])
        for i, (src, dst) in enumerate(((occ_hbm, occ_ref), (code_hbm, code_ref), (green_hbm, green_ref)))
    ]
    for copy in copies:
        copy.start()
    out_ref[...] = jnp.zeros_like(out_ref)
    for copy in copies:
        copy.wait()
    nocc, norb = green_ref.shape
    rows = out_ref.shape[0]
    pick = (lax.broadcasted_iota(jnp.int32, (nocc, nocc), 0) == occ_ref[...]).astype(bf16)
    theta = lax.dot_general(pick, green_ref[...], (((0,), (0,)), ((), ())), preferred_element_type=f32)
    mine = lax.broadcasted_iota(jnp.int32, code_ref.shape, 1) == lax.axis_index("chol")
    code = jnp.sum(jnp.where(mine, code_ref[...], 0).astype(f32), axis=1, keepdims=True)
    for k in range(norb // width):
        out_ref[:nocc, padded * k:padded * k + width] = theta[:, width * k:width * (k + 1)].astype(bf16)
    out_ref[:, width:width + 1] = jnp.broadcast_to(code, (rows, 1)).astype(bf16)


def prep_chol(chol_ref, theta_ref, cross_ref, pair_ref):
    gdev, nocc, width = chol_ref.shape
    half = gdev // 2
    padded = cross_ref.shape[2] // half
    h = lax.rem(lax.axis_index("walk"), 2)
    cross_ref[...] = jnp.zeros_like(cross_ref)
    for i, start in enumerate((h * half, (1 - h) * half)):
        for g in range(half):
            cross_ref[i, :nocc, g * padded:g * padded + width] = chol_ref[start + g]
    pair_ref[0] = theta_ref[...]
    pair_ref[1] = jnp.zeros(pair_ref.shape[1:], pair_ref.dtype)
    pair_ref[1, :nocc] = cross_ref[1]


def second(pair_ref, out_ref):
    out_ref[...] = jnp.zeros_like(out_ref)
    out_ref[:pair_ref.shape[1]] = pair_ref[1]


def join(a_ref, b_ref, out_ref):
    out_ref[...] = a_ref[...] + b_ref[...]


def place_chol(own_ref, pair_ref, same_ref, other_ref, out_ref, *, half, rows, padded):
    out_ref[...] = jnp.zeros_like(out_ref)
    for s, ref in enumerate((own_ref.at[0], pair_ref.at[1], same_ref.at[0], other_ref)):
        for g in range(half):
            block = ref[:, g * padded:(g + 1) * padded]
            out_ref[g * LANES:g * LANES + block.shape[0], column(s, padded)] = block


def weights(theta, width, padded):
    code = theta[0:8, padded - LANES:padded].astype(f32)
    lane = lax.broadcasted_iota(jnp.int32, (8, LANES), 1) == width - (padded - LANES)
    code = jnp.sum(jnp.where(lane, code, 0.0), axis=1, keepdims=True)[0:1]
    return jnp.cos(jnp.pi * code / 4.0)


def column(s, padded):
    return pl.ds(pl.multiple_of((lax.axis_index("walk") ^ s) * padded, padded), padded)


def place_theta(thetas, theta_s):
    theta_s[...] = jnp.zeros_like(theta_s)
    for w, ref in enumerate(thetas):
        theta = ref[0] if len(ref.shape) == 3 else ref[...]
        theta_s[w * LANES:w * LANES + theta.shape[0], :] = theta


def first_walkers(*refs, walkers, half, rows, width, padded):
    *thetas, chol_s, own_ref, core_ref, same_ref, other_ref, energy_ref, theta_s, cotan_s = refs
    place_theta(thetas, theta_s)
    tmat = lax.dot_general(theta_s[...], chol_s[...], (((1,), (1,)), ((), ())), preferred_element_type=f32)
    for w in range(walkers):
        weight = weights(theta_s[w * LANES:w * LANES + 16, :], width, padded)
        total = jnp.zeros((LANES, LANES), f32)
        for g in range(half):
            block = tmat[w * LANES:(w + 1) * LANES, g * LANES:(g + 1) * LANES]
            total += block * block.T
            cotan_s[g * LANES:(g + 1) * LANES, w * LANES:(w + 1) * LANES] = (-weight * block).astype(bf16)
        energy_ref[w:w + 1, :] = -0.5 * jnp.sum(total, axis=0, keepdims=True)
    for s, ref in enumerate((own_ref, core_ref, same_ref, other_ref)):
        ref[...] = jnp.dot(cotan_s[...], theta_s[:, column(s, padded)], preferred_element_type=f32)


def last_walkers(
    mine, theirs, chol_s, same_part, other_part, same_ref, other_ref, tmat_ref, theta_s, cotan_s,
    *, walkers, half, rows, width, padded
):
    place_theta([mine, theirs], theta_s)
    tmat = lax.dot_general(theta_s[...], chol_s[...], (((1,), (1,)), ((), ())), preferred_element_type=f32)
    tmat_ref[...] = tmat
    for w in range(walkers):
        weight = weights(theta_s[w * LANES:w * LANES + 16, :], width, padded)
        for g in range(half):
            block = tmat[w * LANES:(w + 1) * LANES, g * LANES:(g + 1) * LANES]
            cotan_s[g * LANES:(g + 1) * LANES, w * LANES:(w + 1) * LANES] = (-weight * block).astype(bf16)
    for ref, part, s in ((same_ref, same_part, 2), (other_ref, other_part, 3)):
        grad = part[...] + jnp.dot(cotan_s[...], theta_s[:, column(s, padded)], preferred_element_type=f32)
        for g in range(half):
            ref[g] = grad[g * LANES:g * LANES + rows].astype(bf16)


def chip_walkers(
    tmat_ref, theta_s, cotan_s, own_part, core_part, first_ref, own_ref, core_ref, energy_ref,
    *, nocc, half, rows, padded
):
    for ref, part, s in ((core_ref, core_part, 1), (own_ref, own_part, 0)):
        grad = part[...] + jnp.dot(cotan_s[...], theta_s[:, column(s, padded)], preferred_element_type=f32)
        for g in range(half):
            ref[g] = grad[g * LANES:g * LANES + rows]
    early = first_ref.shape[0] // 2
    for w in range(2 * early):
        energy = first_ref[w:w + 1, :]
        if w < early:
            energy_ref[w:w + 1, :] = energy
        else:
            core_ref[w - early, nocc:nocc + 1, :LANES] = energy
    for w in range(2):
        total = jnp.zeros((LANES, LANES), f32)
        for g in range(half):
            block = tmat_ref[w * LANES:(w + 1) * LANES, g * LANES:(g + 1) * LANES]
            total += block * block.T
        energy = -0.5 * jnp.sum(total, axis=0, keepdims=True)
        if w == 0:
            energy_ref[early:early + 1, :] = energy
        else:
            core_ref[early, nocc:nocc + 1, :LANES] = energy


def pick_energies(energy_ref, core_ref, *out_refs, nocc):
    for w, ref in enumerate(out_refs):
        ref[...] = energy_ref[w:w + 1, :] + core_ref[w, nocc:nocc + 1, :LANES]


def finish(*refs):
    *refs, out_hbm, energy_hbm, out_ref, energy_ref, sems = refs
    own_ref, same_ref, other_ref, core_ref, *energy_refs = refs
    half, rows = own_ref.shape[:2]
    nocc, gdev, width = out_ref.shape
    h = lax.rem(lax.axis_index("walk"), 2)
    energy = sum(ref[...] for ref in energy_refs)
    energy_ref[...] = jnp.sum(energy, axis=1, keepdims=True)
    copies = [pltpu.make_async_copy(energy_ref, energy_hbm, sems.at[0])]
    copies[0].start()
    for n, start in enumerate(range(0, rows, 32), start=1):
        stop = min(start + 32, rows)
        mine = own_ref[:, start:stop, :] + same_ref[:, start:stop, :].astype(f32)
        theirs = core_ref[:half, start:stop, :] + other_ref[:, start:stop, :].astype(f32)
        low = jnp.where(h == 0, mine, theirs)
        high = jnp.where(h == 0, theirs, mine)
        both = jnp.swapaxes(jnp.concatenate([low, high], axis=0), 0, 1)
        stop = min(stop, nocc)
        out_ref[start:stop] = both[:stop - start, :, :width]
        copies.append(pltpu.make_async_copy(out_ref.at[start:stop], out_hbm.at[start:stop], sems.at[n]))
        copies[-1].start()
    for copy in copies:
        copy.wait()


def call(kernel, outs, *operands, scratch=(), ins=VMEM, out=VMEM, grant=GRANT):
    return pl.pallas_call(
        kernel,
        out_shape=outs,
        in_specs=[pl.BlockSpec(memory_space=ins)] * len(operands),
        out_specs=jax.tree.map(lambda _: pl.BlockSpec(memory_space=out), outs),
        scratch_shapes=scratch,
        compiler_params=pltpu.CompilerParams(vmem_limit_bytes=grant),
    )(*operands)


def body(chol_vectors, green_blocks, phase_codes, occupations, *, nchol, nwalk):
    gdev, nocc, width = chol_vectors.shape
    norb = green_blocks.shape[3]
    half = gdev // 2
    rows = ceil_to(nocc + 1, 8)
    padded = ceil_to(width, LANES)
    wide = padded * nwalk
    sizes = dict(half=half, rows=rows, padded=padded)

    def swap(x, flip):
        return lax.ppermute(x, "walk", [(i, i ^ flip) for i in range(nwalk)])

    def turn(x, pairs):
        return lax.ppermute(x, "chol", pairs)

    def struct(*shape, dtype=bf16):
        return jax.ShapeDtypeStruct(shape, dtype)

    theta = call(
        functools.partial(prep_theta, width=width, padded=padded),
        struct(rows, wide),
        occupations.reshape(1, nocc),
        phase_codes,
        green_blocks.reshape(nocc, norb),
        scratch=[
            pltpu.VMEM((1, nocc), jnp.int32),
            pltpu.VMEM(phase_codes.shape, jnp.int32),
            pltpu.VMEM((nocc, norb), bf16),
            pltpu.SemaphoreType.DMA((3,)),
        ],
        ins=HBM,
    )
    block = struct(rows, wide)
    cross, pair = call(prep_chol, (struct(2, nocc, wide), struct(2, rows, wide)), chol_vectors, theta)

    if nchol == 4:
        there = [(0, 2), (2, 3), (3, 1), (1, 0)]
        back = [(b, a) for a, b in there]
        paths = [there, back, [(i, 3 - i) for i in range(4)]]
        first = turn(theta, there)
        early = [first, turn(theta, back)]
        last = turn(theta, [(1, 2), (2, 1)]), turn(first, [(1, 0), (2, 3)])
    else:
        paths = [[(i, (i + d) % nchol) for i in range(nchol)] for d in range(1, nchol)]
        *early, last = [turn(theta, path) for path in paths]

    paired = swap(pair, 1)
    crossed = swap(cross, 2)
    chol = call(
        functools.partial(place_chol, **sizes),
        struct(half * LANES, wide),
        cross,
        paired,
        crossed,
        swap(call(second, block, crossed), 1),
    )
    term = struct(half * LANES, padded, dtype=f32)
    mine = [theta] + early
    theirs = [paired] + [swap(t, 1) for t in early]
    grads, energies = None, []
    for start in range(0, nchol - 1, 3):
        group = mine[start:start + 3] + theirs[start:start + 3]
        walkers = len(group)
        *terms, energy = call(
            functools.partial(first_walkers, walkers=walkers, width=width, **sizes),
            (term,) * 4 + (struct(walkers, LANES, dtype=f32),),
            *group,
            chol,
            scratch=[pltpu.VMEM((walkers * LANES, wide), bf16), pltpu.VMEM((half * LANES, walkers * LANES), bf16)],
        )
        grads = terms if grads is None else [a + b for a, b in zip(grads, terms)]
        energies += [(energy[:walkers // 2], energy[walkers // 2:])]
    if len(energies) > 1:
        energy = jnp.concatenate([e[i] for i in (0, 1) for e in energies])
    if nchol == 4:
        held = last
        last = call(join, block, *held)

    walkers = 2
    same, other, tmat, theta_s, cotan_s = call(
        functools.partial(last_walkers, walkers=walkers, width=width, **sizes),
        (
            struct(half, rows, padded),
            struct(half, rows, padded),
            struct(walkers * LANES, half * LANES, dtype=f32),
            struct(walkers * LANES, wide),
            struct(half * LANES, walkers * LANES),
        ),
        last,
        swap(last, 1),
        chol,
        grads[2],
        grads[3],
    )
    same, other = swap(same, 2), swap(other, 3)
    tall = max(half, nchol)
    own, core, energy = call(
        functools.partial(chip_walkers, nocc=nocc, **sizes),
        (struct(half, rows, padded, dtype=f32), struct(tall, rows, padded, dtype=f32), struct(nchol, LANES, dtype=f32)),
        tmat,
        theta_s,
        cotan_s,
        grads[0],
        grads[1],
        energy,
    )
    core = swap(core, 1)
    part, *parts = call(
        functools.partial(pick_energies, nocc=nocc), (struct(1, LANES, dtype=f32),) * nchol, energy, core
    )
    parts = [turn(p, [(b, a) for a, b in path]) for p, path in zip(parts, paths)]
    chol_grad, energies = call(
        finish,
        (struct(nocc, gdev, width, dtype=f32), struct(1, 1, dtype=f32)),
        own,
        same,
        other,
        core,
        part,
        *parts,
        out=HBM,
        scratch=[
            pltpu.VMEM((nocc, gdev, width), f32),
            pltpu.VMEM((1, 1), f32),
            pltpu.SemaphoreType.DMA((1 - (-rows // 32),)),
        ],
    )
    return jnp.swapaxes(chol_grad, 0, 1), energies


def solution(mesh):
    placed = (
        P("chol", None, "walk"),
        P(("dom", "walk"), "chol", None, None),
        P(("dom", "walk"), None),
        P(("dom", "walk"), "chol", None),
    )
    return jax.shard_map(
        functools.partial(body, nchol=mesh.shape["chol"], nwalk=mesh.shape["walk"]),
        mesh=mesh,
        in_specs=placed,
        out_specs=(P(("dom", "chol"), None, "walk"), P(("dom", "walk"), "chol")),
        check_vma=False,
    )
```

time: 128 us -> 38.6 us (0.30)
  waiting for transfers between devices: 58.3 us -> 15 us
  blocking collectives: 33.8 us -> 0 us
  starting transfers between devices: 0.08 us -> 15.8 us
  between operations: 14.1 us -> 0.79 us
  local copies, waits for them, and re-layouts: 13.1 us -> 1.67 us
  matrix products: 6.36 us -> 0 us
  Pallas kernels: 0 us -> 4.9 us
  other arithmetic: 1.84 us -> 0 us
    psum x1 -> x0, waiting for transfers between devices: 55.8 us -> none  [body(): summed = lax.psum(grad_acc, 'walk')]
    all_gather x1 -> x0, blocking collectives: 22.1 us -> none  [body(): piece = lax.all_gather(theta, 'chol', axis=0, tiled=True)]
    ppermute x0 -> x16, starting transfers between devices: none -> 15.8 us  [the longest x7 11.5 us: turn(): return lax.ppermute(x, 'chol', pairs)]
    ppermute x0 -> x16, waiting for transfers between devices: none -> 15 us  [the longest x9 8.55 us: swap(): return lax.ppermute(x, 'walk', [(i, i ^ flip) for i in range(nwalk)])]
    unnamed x1 -> x0, blocking collectives: 11.7 us -> none
    dot_general x3 -> x0, matrix products: 6.36 us -> none  [the longest x1 2.93 us: body(): jnp.einsum('gwji,wjp->gip', cotan, piece, preferred_element_type=jnp.floa...]
    unnamed x11 -> x9, local copies, waits for them, and re-layouts: 7.08 us -> 1.67 us
    pallas_call x0 -> x10, Pallas kernels: none -> 4.9 us  [call(): pl.pallas_call(kernel, out_shape=outs, in_specs=[pl.BlockSpec(memory_spac...]
  transfers between devices with their start and end apart: 2 -> 16, of which waited for: 2 -> 5; matrix products, arithmetic and copies ran while one was open for 5% -> 0% of each run, Pallas kernels for 0% -> 6%
where the time goes in v2:
time: 38.6 us; the launch traced here: 38.2 us
  starting transfers between devices  15.8 us (41%)
  waiting for transfers between devices  15 us (39%)
  Pallas kernels  4.9 us (13%)
  local copies, waits for them, and re-layouts  1.67 us (4%)
  between operations  0.79 us (2%)
    ppermute x7, starting transfers between devices, turn(): return lax.ppermute(x, 'chol', pairs)  11.5 us
    ppermute x9, waiting for transfers between devices, swap(): return lax.ppermute(x, 'walk', [(i, i ^ flip) for i in range(nwalk)])  8.55 us
    ppermute x7, waiting for transfers between devices, turn(): return lax.ppermute(x, 'chol', pairs)  6.46 us
    pallas_call x10, Pallas kernels, call(): pl.pallas_call(kernel, out_shape=outs, in_specs=[pl.BlockSpec(memory_spac...  4.9 us
    ppermute x9, starting transfers between devices, swap(): return lax.ppermute(x, 'walk', [(i, i ^ flip) for i in range(nwalk)])  4.35 us
    unnamed x9, local copies, waits for them, and re-layouts  1.67 us
  transfers between devices with their start and end apart: 16, of which 5 were waited for; matrix products, arithmetic and copies ran while one was open for 0% of the time, Pallas kernels for 6%

profile of v2, /device:TPU:0, one launch (start us, length us, event | category | flops | bytes accessed | tf_op | source)
XLA Modules:
  0.0 38.2 jit_solution(3713931798410077885)
XLA Ops:
  0.6 0.0 copy-start.1
  0.6 0.0 copy-start.2
  0.7 0.6 %copy-done.1 = s32[1,1,100]{2,1,0:T(1,128)S(1)} copy-done((s32[1,1,100]{2,1,0:T(1,128)S(1)}, s32[1,1,100]{2,1,0:T(1,128)}, u32[]{:S(2)}) %copy-start.1) | copy-done | bytes 424
  1.3 0.0 copy-done.2
  1.3 0.0 copy-start
  1.3 0.9 %copy-done = bf16[1,1,100,1000]{3,2,1,0:T(8,128)(2,1)S(1)} copy-done((bf16[1,1,100,1000]{3,2,1,0:T(8,128)(2,1)S(1)}, bf16[1,1,100,1000]{3,2,1,0:T(8,128)(2,1)}, u32[]{:S(2)}) %copy-start) | copy-done | bytes 200024
  2.2 0.0 copy-start.3
  2.2 0.7 %shard_map.59.theta_ref.refs_0_ = bf16[104,1024]{1,0:T(8,128)(2,1)S(1)} custom-call(s32[1,100]{1,0:T(1,128)S(1)} %bitcast.4, s32[1,4]{1,0:T(1,128)S(1)} %copy-done.2, bf16[100,1000]{1,0:T(8,128)(2,1)S(1)} %bitcast.3), custom_call_target="tpu_custom_call" | custom-call | tf_op jit(solution)/shard_map/pallas_call | solution.py:183
  2.9 4.1 %collective-permute-start.1 = (bf16[104,1024]{1,0:T(8,128)(2,1)S(1)}, bf16[104,1024]{1,0:T(8,128)(2,1)S(1)}, u32[]{:S(2)}, u32[]{:S(2)}) collective-permute-start(bf16[104,1024]{1,0:T(8,128)(2,1)S(1)} %shard_map.59.theta_ref.refs_0_), channel_id=1, source_target_pairs={{0,8},{8,12},{12,4},{4,0},{1,9},{9,13},{13,5},{5,1},{2,10},{10,14}... | collective-permute-start | bytes 638984 | tf_op jit(solution)/shard_map/ppermute | solution.py:206
  7.0 0.0 copy-done.3
  7.0 0.1 copy.6.chol_ref
  7.1 0.1 shard_map.61
  7.2 1.6 %collective-permute-start.5 = (bf16[2,100,1024]{2,1,0:T(8,128)(2,1)S(1)}, bf16[2,100,1024]{2,1,0:T(8,128)(2,1)S(1)}, u32[]{:S(2)}, u32[]{:S(2)}) collective-permute-start(bf16[2,100,1024]{2,1,0:T(8,128)(2,1)S(1)} %get-tuple-element.23.own_ref), channel_id=1, source_target_pairs={{0,2},{1,3},{2,0},{3,1},{4,6},{5,7},{6,4},{7,5},{8,10},{9,11},{10,... | collective-permute-start | bytes 1228808 | tf_op jit(solution)/shard_map/ppermute | solution.py:203
  8.7 0.0 collective-permute-start.7
  8.7 0.0 collective-permute-start.4
  8.7 0.7 %collective-permute-start = (bf16[104,1024]{1,0:T(8,128)(2,1)S(1)}, bf16[104,1024]{1,0:T(8,128)(2,1)S(1)}, u32[]{:S(2)}, u32[]{:S(2)}) collective-permute-start(bf16[104,1024]{1,0:T(8,128)(2,1)S(1)} %shard_map.59.theta_ref.refs_0_), channel_id=1, source_target_pairs={{4,8},{8,4},{5,9},{9,5},{6,10},{10,6},{7,11},{11,7},{20,24},{24,20... | collective-permute-start | bytes 638984 | tf_op jit(solution)/shard_map/ppermute | solution.py:206
  9.4 3.2 %collective-permute-done.1.refs_1_ = bf16[104,1024]{1,0:T(8,128)(2,1)S(1)} collective-permute-done((bf16[104,1024]{1,0:T(8,128)(2,1)S(1)}, bf16[104,1024]{1,0:T(8,128)(2,1)S(1)}, u32[]{:S(2)}, u32[]{:S(2)}) %collective-permute-start.1) | collective-permute-done | bytes 213024 | tf_op jit(solution)/shard_map/ppermute | solution.py:206
  12.6 1.3 %collective-permute-start.2 = (bf16[104,1024]{1,0:T(8,128)(2,1)S(1)}, bf16[104,1024]{1,0:T(8,128)(2,1)S(1)}, u32[]{:S(2)}, u32[]{:S(2)}) collective-permute-start(bf16[104,1024]{1,0:T(8,128)(2,1)S(1)} %collective-permute-done.1.refs_1_), channel_id=1, source_target_pairs={{4,0},{8,12},{5,1},{9,13},{6,2},{10,14},{7,3},{11,15},{20,16},{24,... | collective-permute-start | bytes 638984 | tf_op jit(solution)/shard_map/ppermute | solution.py:206
  13.9 4.6 %collective-permute-done.5.pair_ref.same_ref = bf16[2,100,1024]{2,1,0:T(8,128)(2,1)S(1)} collective-permute-done((bf16[2,100,1024]{2,1,0:T(8,128)(2,1)S(1)}, bf16[2,100,1024]{2,1,0:T(8,128)(2,1)S(1)}, u32[]{:S(2)}, u32[]{:S(2)}) %collective-permute-start.5) | collective-permute-done | bytes 409632 | tf_op jit(solution)/shard_map/ppermute | solution.py:203
  18.5 0.0 collective-permute-start.8
  18.5 0.0 collective-permute-done.7.refs_2_
  18.6 0.6 %collective-permute-start.6 = (bf16[104,1024]{1,0:T(8,128)(2,1)S(1)}, bf16[104,1024]{1,0:T(8,128)(2,1)S(1)}, u32[]{:S(2)}, u32[]{:S(2)}) collective-permute-start(bf16[104,1024]{1,0:T(8,128)(2,1)S(1)} %shard_map.62), channel_id=1, source_target_pairs={{0,1},{1,0},{2,3},{3,2},{4,5},{5,4},{6,7},{7,6},{8,9},{9,8},{10,11... | collective-permute-start | bytes 638984 | tf_op jit(solution)/shard_map/ppermute | solution.py:203
  19.1 0.0 collective-permute-done.a_ref
  19.1 0.1 collective-permute-start.9
  19.2 3.2 %collective-permute-done.2.b_ref = bf16[104,1024]{1,0:T(8,128)(2,1)S(1)} collective-permute-done((bf16[104,1024]{1,0:T(8,128)(2,1)S(1)}, bf16[104,1024]{1,0:T(8,128)(2,1)S(1)}, u32[]{:S(2)}, u32[]{:S(2)}) %collective-permute-start.2) | collective-permute-done | bytes 213024 | tf_op jit(solution)/shard_map/ppermute | solution.py:206
  22.5 0.1 collective-permute-start.3
  22.5 0.0 collective-permute-done.4.pair_ref.refs_3_
  22.5 0.0 collective-permute-done.6.other_ref
  22.6 0.2 shard_map.63.refs_6_.chol_s
  22.7 0.0 collective-permute-done.9.refs_5_
  22.7 0.0 collective-permute-done.8.refs_4_
  22.7 1.9 %shard_map.64 = (f32[512,256]{1,0:T(8,128)S(1)}, f32[512,256]{1,0:T(8,128)S(1)}, f32[512,256]{1,0:T(8,128)S(1)}, f32[512,256]{1,0:T(8,128)S(1)}, f32[6,128]{1,0:T(8,128)S(1)}) custom-call(bf16[104,1024]{1,0:T(8,128)(2,1)S(1)} %shard_map.59.theta_ref.refs_0_, bf16[104,1024]{1,0:T(8,128)(2,1)S(1)} %collective-permute-done.1.refs_1_, ...), custom_call_target="tpu_custom_call" | custom-call | tf_op jit(solution)/shard_map/pallas_call | solution.py:183
  24.6 0.0 collective-permute-done.3.theirs
  24.7 0.7 %shard_map.65 = (bf16[4,104,256]{2,1,0:T(8,128)(2,1)S(1)}, bf16[4,104,256]{2,1,0:T(8,128)(2,1)S(1)}, f32[256,512]{1,0:T(8,128)S(1)}, bf16[256,1024]{1,0:T(8,128)(2,1)S(1)}, bf16[512,256]{1,0:T(8,128)(2,1)S(1)}) custom-call(bf16[104,1024]{1,0:T(8,128)(2,1)S(1)} %shard_map.60.mine, bf16[104,1024]{1,0:T(8,128)(2,1)S(1)} %collective-permute-done.3.theirs, ...), custom_call_target="tpu_custom_call" | custom-call | tf_op jit(solution)/shard_map/pallas_call | solution.py:183
  25.4 0.3 shard_map.66
  25.7 0.5 %collective-permute-start.12 = (f32[4,104,256]{2,1,0:T(8,128)S(1)}, f32[4,104,256]{2,1,0:T(8,128)S(1)}, u32[]{:S(2)}, u32[]{:S(2)}) collective-permute-start(f32[4,104,256]{2,1,0:T(8,128)S(1)} %get-tuple-element.36), channel_id=1, source_target_pairs={{0,1},{1,0},{2,3},{3,2},{4,5},{5,4},{6,7},{7,6},{8,9},{9,8},{10,11... | collective-permute-start | bytes 1277960 | tf_op jit(solution)/shard_map/ppermute | solution.py:203
  26.3 1.5 %collective-permute-start.10 = (bf16[4,104,256]{2,1,0:T(8,128)(2,1)S(1)}, bf16[4,104,256]{2,1,0:T(8,128)(2,1)S(1)}, u32[]{:S(2)}, u32[]{:S(2)}) collective-permute-start(bf16[4,104,256]{2,1,0:T(8,128)(2,1)S(1)} %get-tuple-element.34), channel_id=1, source_target_pairs={{0,2},{1,3},{2,0},{3,1},{4,6},{5,7},{6,4},{7,5},{8,10},{9,11},{10,... | collective-permute-start | bytes 638984 | tf_op jit(solution)/shard_map/ppermute | solution.py:203
  27.8 0.0 collective-permute-start.11
  27.8 0.0 collective-permute-done.12.core_ref.refs_3_
  27.8 1.6 %collective-permute-start.13 = (f32[1,128]{1,0:T(1,128)S(1)}, f32[1,128]{1,0:T(1,128)S(1)}, u32[]{:S(2)}, u32[]{:S(2)}) collective-permute-start(f32[1,128]{1,0:T(1,128)S(1)} %get-tuple-element.39), channel_id=1, source_target_pairs={{8,0},{12,8},{4,12},{0,4},{9,1},{13,9},{5,13},{1,5},{10,2},{14,10}... | collective-permute-start | bytes 1544 | tf_op jit(solution)/shard_map/ppermute | solution.py:206
  29.4 1.4 %collective-permute-start.14 = (f32[1,128]{1,0:T(1,128)S(1)}, f32[1,128]{1,0:T(1,128)S(1)}, u32[]{:S(2)}, u32[]{:S(2)}) collective-permute-start(f32[1,128]{1,0:T(1,128)S(1)} %get-tuple-element.40), channel_id=1, source_target_pairs={{0,8},{8,12},{12,4},{4,0},{1,9},{9,13},{13,5},{5,1},{2,10},{10,14}... | collective-permute-start | bytes 1544 | tf_op jit(solution)/shard_map/ppermute | solution.py:206
  30.7 2.5 %collective-permute-start.15 = (f32[1,128]{1,0:T(1,128)S(1)}, f32[1,128]{1,0:T(1,128)S(1)}, u32[]{:S(2)}, u32[]{:S(2)}) collective-permute-start(f32[1,128]{1,0:T(1,128)S(1)} %get-tuple-element.41), channel_id=1, source_target_pairs={{12,0},{8,4},{4,8},{0,12},{13,1},{9,5},{5,9},{1,13},{14,2},{10,6},... | collective-permute-start | bytes 1544 | tf_op jit(solution)/shard_map/ppermute | solution.py:206
  33.2 1.1 %collective-permute-done.10.refs_1_ = bf16[4,104,256]{2,1,0:T(8,128)(2,1)S(1)} collective-permute-done((bf16[4,104,256]{2,1,0:T(8,128)(2,1)S(1)}, bf16[4,104,256]{2,1,0:T(8,128)(2,1)S(1)}, u32[]{:S(2)}, u32[]{:S(2)}) %collective-permute-start.10) | collective-permute-done | bytes 213024 | tf_op jit(solution)/shard_map/ppermute | solution.py:203
  34.4 2.8 %collective-permute-done.11.refs_2_ = bf16[4,104,256]{2,1,0:T(8,128)(2,1)S(1)} collective-permute-done((bf16[4,104,256]{2,1,0:T(8,128)(2,1)S(1)}, bf16[4,104,256]{2,1,0:T(8,128)(2,1)S(1)}, u32[]{:S(2)}, u32[]{:S(2)}) %collective-permute-start.11) | collective-permute-done | bytes 213024 | tf_op jit(solution)/shard_map/ppermute | solution.py:203
  37.2 0.0 collective-permute-done.13.refs_5_
  37.2 0.0 collective-permute-done.14.refs_6_
  37.2 0.0 collective-permute-done.15.refs_7_
  37.2 1.0 %shard_map.68 = (f32[100,8,250]{2,1,0:T(8,128)}, f32[1,1]{1,0:T(1,128)}) custom-call(f32[4,104,256]{2,1,0:T(8,128)S(1)} %get-tuple-element.33.refs_0_, bf16[4,104,256]{2,1,0:T(8,128)(2,1)S(1)} %collective-permute-done.10.refs_1_, bf16[4,104,256]{2,1,0:T(8,128)(2,1)S(1)} %collective-permute-done.11.refs_2_, ...), custom_call_target="tpu_custom_call" | custom-call | tf_op jit(solution)/shard_map/pallas_call | solution.py:183
  (3 shorter events, 0.0 us)
Async XLA Ops:
  0.6 0.7 %copy-start.1 = (s32[1,1,100]{2,1,0:T(1,128)S(1)}, s32[1,1,100]{2,1,0:T(1,128)}, u32[]{:S(2)}) copy-start(s32[1,1,100]{2,1,0:T(1,128)} %param.7) | copy-start | bytes 1204
  0.6 0.7 %copy-start.2 = (s32[1,4]{1,0:T(1,128)S(1)}, s32[1,4]{1,0:T(1,128)}, u32[]{:S(2)}) copy-start(s32[1,4]{1,0:T(1,128)} %code_hbm.1) | copy-start | bytes 52
  1.3 0.9 %copy-start = (bf16[1,1,100,1000]{3,2,1,0:T(8,128)(2,1)S(1)}, bf16[1,1,100,1000]{3,2,1,0:T(8,128)(2,1)}, u32[]{:S(2)}) copy-start(bf16[1,1,100,1000]{3,2,1,0:T(8,128)(2,1)} %param.5) | copy-start | bytes 600004
  2.2 4.8 %copy-start.3 = (bf16[8,100,250]{2,0,1:T(8,128)(2,1)S(1)}, bf16[8,100,250]{2,0,1:T(8,128)(2,1)}, u32[]{:S(2)}) copy-start(bf16[8,100,250]{2,0,1:T(8,128)(2,1)} %param.4) | copy-start | bytes 1200004
  2.9 9.7 %collective-permute-start.1 = (bf16[104,1024]{1,0:T(8,128)(2,1)S(1)}, bf16[104,1024]{1,0:T(8,128)(2,1)S(1)}, u32[]{:S(2)}, u32[]{:S(2)}) collective-permute-start(bf16[104,1024]{1,0:T(8,128)(2,1)S(1)} %shard_map.59.theta_ref.refs_0_), channel_id=1, source_target_pairs={{0,8},{8,12},{12,4},{4,0},{1,9},{9,13},{13,5},{5,1},{2,10},{10,14}... | collective-permute-start | bytes 638984 | tf_op jit(solution)/shard_map/ppermute | solution.py:206
  7.2 11.3 %collective-permute-start.5 = (bf16[2,100,1024]{2,1,0:T(8,128)(2,1)S(1)}, bf16[2,100,1024]{2,1,0:T(8,128)(2,1)S(1)}, u32[]{:S(2)}, u32[]{:S(2)}) collective-permute-start(bf16[2,100,1024]{2,1,0:T(8,128)(2,1)S(1)} %get-tuple-element.23.own_ref), channel_id=1, source_target_pairs={{0,2},{1,3},{2,0},{3,1},{4,6},{5,7},{6,4},{7,5},{8,10},{9,11},{10,... | collective-permute-start | bytes 1228808 | tf_op jit(solution)/shard_map/ppermute | solution.py:203
  8.7 9.8 %collective-permute-start.7 = (bf16[104,1024]{1,0:T(8,128)(2,1)S(1)}, bf16[104,1024]{1,0:T(8,128)(2,1)S(1)}, u32[]{:S(2)}, u32[]{:S(2)}) collective-permute-start(bf16[104,1024]{1,0:T(8,128)(2,1)S(1)} %shard_map.59.theta_ref.refs_0_), channel_id=1, source_target_pairs={{8,0},{12,8},{4,12},{0,4},{9,1},{13,9},{5,13},{1,5},{10,2},{14,10}... | collective-permute-start | bytes 638984 | tf_op jit(solution)/shard_map/ppermute | solution.py:206
  8.7 13.8 %collective-permute-start.4 = (bf16[2,104,1024]{2,1,0:T(8,128)(2,1)S(1)}, bf16[2,104,1024]{2,1,0:T(8,128)(2,1)S(1)}, u32[]{:S(2)}, u32[]{:S(2)}) collective-permute-start(bf16[2,104,1024]{2,1,0:T(8,128)(2,1)S(1)} %get-tuple-element.24), channel_id=1, source_target_pairs={{0,1},{1,0},{2,3},{3,2},{4,5},{5,4},{6,7},{7,6},{8,9},{9,8},{10,11... | collective-permute-start | bytes 1277960 | tf_op jit(solution)/shard_map/ppermute | solution.py:203
  8.7 10.4 %collective-permute-start = (bf16[104,1024]{1,0:T(8,128)(2,1)S(1)}, bf16[104,1024]{1,0:T(8,128)(2,1)S(1)}, u32[]{:S(2)}, u32[]{:S(2)}) collective-permute-start(bf16[104,1024]{1,0:T(8,128)(2,1)S(1)} %shard_map.59.theta_ref.refs_0_), channel_id=1, source_target_pairs={{4,8},{8,4},{5,9},{9,5},{6,10},{10,6},{7,11},{11,7},{20,24},{24,20... | collective-permute-start | bytes 638984 | tf_op jit(solution)/shard_map/ppermute | solution.py:206
  12.6 9.8 %collective-permute-start.2 = (bf16[104,1024]{1,0:T(8,128)(2,1)S(1)}, bf16[104,1024]{1,0:T(8,128)(2,1)S(1)}, u32[]{:S(2)}, u32[]{:S(2)}) collective-permute-start(bf16[104,1024]{1,0:T(8,128)(2,1)S(1)} %collective-permute-done.1.refs_1_), channel_id=1, source_target_pairs={{4,0},{8,12},{5,1},{9,13},{6,2},{10,14},{7,3},{11,15},{20,16},{24,... | collective-permute-start | bytes 638984 | tf_op jit(solution)/shard_map/ppermute | solution.py:206
  18.5 4.2 %collective-permute-start.8 = (bf16[104,1024]{1,0:T(8,128)(2,1)S(1)}, bf16[104,1024]{1,0:T(8,128)(2,1)S(1)}, u32[]{:S(2)}, u32[]{:S(2)}) collective-permute-start(bf16[104,1024]{1,0:T(8,128)(2,1)S(1)} %collective-permute-done.1.refs_1_), channel_id=1, source_target_pairs={{0,1},{1,0},{2,3},{3,2},{4,5},{5,4},{6,7},{7,6},{8,9},{9,8},{10,11... | collective-permute-start | bytes 638984 | tf_op jit(solution)/shard_map/ppermute | solution.py:203
  18.6 4.0 %collective-permute-start.6 = (bf16[104,1024]{1,0:T(8,128)(2,1)S(1)}, bf16[104,1024]{1,0:T(8,128)(2,1)S(1)}, u32[]{:S(2)}, u32[]{:S(2)}) collective-permute-start(bf16[104,1024]{1,0:T(8,128)(2,1)S(1)} %shard_map.62), channel_id=1, source_target_pairs={{0,1},{1,0},{2,3},{3,2},{4,5},{5,4},{6,7},{7,6},{8,9},{9,8},{10,11... | collective-permute-start | bytes 638984 | tf_op jit(solution)/shard_map/ppermute | solution.py:203
  19.1 3.6 %collective-permute-start.9 = (bf16[104,1024]{1,0:T(8,128)(2,1)S(1)}, bf16[104,1024]{1,0:T(8,128)(2,1)S(1)}, u32[]{:S(2)}, u32[]{:S(2)}) collective-permute-start(bf16[104,1024]{1,0:T(8,128)(2,1)S(1)} %collective-permute-done.7.refs_2_), channel_id=1, source_target_pairs={{0,1},{1,0},{2,3},{3,2},{4,5},{5,4},{6,7},{7,6},{8,9},{9,8},{10,11... | collective-permute-start | bytes 638984 | tf_op jit(solution)/shard_map/ppermute | solution.py:203
  22.5 2.2 %collective-permute-start.3 = (bf16[104,1024]{1,0:T(8,128)(2,1)S(1)}, bf16[104,1024]{1,0:T(8,128)(2,1)S(1)}, u32[]{:S(2)}, u32[]{:S(2)}) collective-permute-start(bf16[104,1024]{1,0:T(8,128)(2,1)S(1)} %shard_map.60.mine), channel_id=1, source_target_pairs={{0,1},{1,0},{2,3},{3,2},{4,5},{5,4},{6,7},{7,6},{8,9},{9,8},{10,11... | collective-permute-start | bytes 638984 | tf_op jit(solution)/shard_map/ppermute | solution.py:203
  25.7 2.1 %collective-permute-start.12 = (f32[4,104,256]{2,1,0:T(8,128)S(1)}, f32[4,104,256]{2,1,0:T(8,128)S(1)}, u32[]{:S(2)}, u32[]{:S(2)}) collective-permute-start(f32[4,104,256]{2,1,0:T(8,128)S(1)} %get-tuple-element.36), channel_id=1, source_target_pairs={{0,1},{1,0},{2,3},{3,2},{4,5},{5,4},{6,7},{7,6},{8,9},{9,8},{10,11... | collective-permute-start | bytes 1277960 | tf_op jit(solution)/shard_map/ppermute | solution.py:203
  26.3 8.1 %collective-permute-start.10 = (bf16[4,104,256]{2,1,0:T(8,128)(2,1)S(1)}, bf16[4,104,256]{2,1,0:T(8,128)(2,1)S(1)}, u32[]{:S(2)}, u32[]{:S(2)}) collective-permute-start(bf16[4,104,256]{2,1,0:T(8,128)(2,1)S(1)} %get-tuple-element.34), channel_id=1, source_target_pairs={{0,2},{1,3},{2,0},{3,1},{4,6},{5,7},{6,4},{7,5},{8,10},{9,11},{10,... | collective-permute-start | bytes 638984 | tf_op jit(solution)/shard_map/ppermute | solution.py:203
  27.8 9.4 %collective-permute-start.11 = (bf16[4,104,256]{2,1,0:T(8,128)(2,1)S(1)}, bf16[4,104,256]{2,1,0:T(8,128)(2,1)S(1)}, u32[]{:S(2)}, u32[]{:S(2)}) collective-permute-start(bf16[4,104,256]{2,1,0:T(8,128)(2,1)S(1)} %get-tuple-element.35), channel_id=1, source_target_pairs={{0,3},{1,2},{2,1},{3,0},{4,7},{5,6},{6,5},{7,4},{8,11},{9,10},{10,... | collective-permute-start | bytes 638984 | tf_op jit(solution)/shard_map/ppermute | solution.py:203
  27.8 9.4 %collective-permute-start.13 = (f32[1,128]{1,0:T(1,128)S(1)}, f32[1,128]{1,0:T(1,128)S(1)}, u32[]{:S(2)}, u32[]{:S(2)}) collective-permute-start(f32[1,128]{1,0:T(1,128)S(1)} %get-tuple-element.39), channel_id=1, source_target_pairs={{8,0},{12,8},{4,12},{0,4},{9,1},{13,9},{5,13},{1,5},{10,2},{14,10}... | collective-permute-start | bytes 1544 | tf_op jit(solution)/shard_map/ppermute | solution.py:206
  29.4 7.8 %collective-permute-start.14 = (f32[1,128]{1,0:T(1,128)S(1)}, f32[1,128]{1,0:T(1,128)S(1)}, u32[]{:S(2)}, u32[]{:S(2)}) collective-permute-start(f32[1,128]{1,0:T(1,128)S(1)} %get-tuple-element.40), channel_id=1, source_target_pairs={{0,8},{8,12},{12,4},{4,0},{1,9},{9,13},{13,5},{5,1},{2,10},{10,14}... | collective-permute-start | bytes 1544 | tf_op jit(solution)/shard_map/ppermute | solution.py:206
  30.7 6.4 %collective-permute-start.15 = (f32[1,128]{1,0:T(1,128)S(1)}, f32[1,128]{1,0:T(1,128)S(1)}, u32[]{:S(2)}, u32[]{:S(2)}) collective-permute-start(f32[1,128]{1,0:T(1,128)S(1)} %get-tuple-element.41), channel_id=1, source_target_pairs={{12,0},{8,4},{4,8},{0,12},{13,1},{9,5},{5,9},{1,13},{14,2},{10,6},... | collective-permute-start | bytes 1544 | tf_op jit(solution)/shard_map/ppermute | solution.py:206

commit v3 on v2

v3 whole, which is shorter than its diff:
```python
import functools

import jax
import jax.numpy as jnp
from jax import lax
from jax.experimental import pallas as pl
from jax.experimental.pallas import tpu as pltpu
from jax.sharding import PartitionSpec as P

LANES = 128
GRANT = 16 * 1024 * 1024
PREP = 56 * 1024 * 1024
HBM = pltpu.MemorySpace.HBM
VMEM = pltpu.MemorySpace.VMEM
bf16, f32 = jnp.bfloat16, jnp.float32


def ceil_to(value, step):
    return -(-value // step) * step


def prep_theta(occ_hbm, green_hbm, out_ref, occ_ref, green_ref, sems, *, width, padded):
    copies = [pltpu.make_async_copy(green_hbm, green_ref, sems.at[0]), pltpu.make_async_copy(occ_hbm, occ_ref, sems.at[1])]
    for copy in copies:
        copy.start()
    out_ref[...] = jnp.zeros_like(out_ref)
    nocc, norb = green_ref.shape
    fold = norb // width // 2
    copies[1].wait()
    pick = (lax.broadcasted_iota(jnp.int32, (nocc, nocc), 0) == occ_ref[...]).astype(bf16)
    copies[0].wait()
    theta = lax.dot_general(pick, green_ref[...], (((0,), (0,)), ((), ())), preferred_element_type=f32)
    for k in range(norb // width):
        row, lane = k // fold * nocc, k % fold * padded
        out_ref[row:row + nocc, lane:lane + width] = theta[:, width * k:width * (k + 1)].astype(bf16)


def prep_chol(chol_ref, theta_ref, code_ref, pair_ref):
    gdev, nocc, width = chol_ref.shape
    half = gdev // 2
    padded = pair_ref.shape[2] // (half // 2)
    pair_ref[0] = theta_ref[...]
    pair_ref[1] = jnp.zeros(pair_ref.shape[1:], bf16)
    fold_half(chol_ref, pair_ref.at[1], 1 - lax.rem(lax.axis_index("walk"), 2), padded)
    nchol = code_ref.shape[1]
    shape = (ceil_to(nchol, 8), nchol)
    diagonal = lax.broadcasted_iota(jnp.int32, shape, 0) == lax.broadcasted_iota(jnp.int32, shape, 1)
    codes = jnp.sum(jnp.where(diagonal, code_ref[...], 0).astype(f32), axis=1, keepdims=True)
    lane = pair_ref.shape[2] - padded + width
    pair_ref[1, :shape[0], lane:lane + 1] = codes.astype(bf16)


def fold_half(chol_ref, out_ref, which, padded):
    gdev, nocc, width = chol_ref.shape
    half = gdev // 2
    for g in range(half):
        row, lane = g // (half // 2) * nocc, g % (half // 2) * padded
        out_ref[row:row + nocc, lane:lane + width] = chol_ref[which * half + g]


def relay(crossed_ref, out_ref, *, padded):
    out_ref[...] = jnp.zeros_like(out_ref)
    fold_half(crossed_ref, out_ref, 1 - lax.rem(lax.axis_index("walk"), 2), padded)


def join(a_ref, b_ref, out_ref):
    out_ref[...] = a_ref[...] + b_ref[...]


def place_chol(
    own_ref, pair_ref, same_ref, other_ref, code_ref, out_ref, weight_ref, *, sources, half, nocc, width, padded
):
    out_ref[...] = jnp.zeros_like(out_ref)
    h = lax.rem(lax.axis_index("walk"), 2)
    for g in range(half):
        row, lane = g // (half // 2) * nocc, g % (half // 2) * padded
        rows = slice(g * LANES, g * LANES + nocc)
        for s, ref in ((0, own_ref), (2, same_ref)):
            out_ref[rows, column(s, padded)] = jnp.pad(ref[h * half + g], ((0, 0), (0, padded - width)))
        for s, ref in ((1, pair_ref.at[1]), (3, other_ref)):
            out_ref[rows, column(s, padded)] = ref[row:row + nocc, lane:lane + padded]
    nchol = code_ref.shape[1]
    me = lax.axis_index("chol")
    lane = pair_ref.shape[2] - padded + width
    theirs = pair_ref[1, :ceil_to(nchol, 16), lane:lane + 1].astype(f32)
    mine = code_ref[...].astype(f32)
    codes = jnp.zeros(weight_ref.shape, f32)
    at = lax.broadcasted_iota(jnp.int32, codes.shape, 0)
    for n, path in enumerate(sources):
        source = sum(jnp.where(me == i, s, 0) for i, s in enumerate(path))
        for group, (values, axis) in enumerate(((mine, 1), (theirs, 0))):
            here = lax.broadcasted_iota(jnp.int32, values.shape, axis) == source
            code = jnp.sum(jnp.where(here, values, 0.0), axis=axis, keepdims=True)
            codes = jnp.where(at == group * nchol + n, code, codes)
    weight_ref[...] = -jnp.cos(jnp.pi * codes / 4.0)


def column(s, padded):
    return pl.ds(pl.multiple_of((lax.axis_index("walk") ^ s) * padded, padded), padded)


def place_theta(thetas, theta_s, nocc):
    theta_s[...] = jnp.zeros_like(theta_s)
    for w, ref in enumerate(thetas):
        theta = ref[0] if len(ref.shape) == 3 else ref[...]
        wide = theta.shape[1]
        for i in range(2):
            theta_s[w * LANES:w * LANES + nocc, i * wide:(i + 1) * wide] = theta[i * nocc:(i + 1) * nocc]


def first_walkers(*refs, first, walkers, half, nocc, padded):
    *thetas, chol_s, weight_ref, own_ref, core_ref, same_ref, other_ref, energy_ref, theta_s, cotan_s = refs
    place_theta(thetas, theta_s, nocc)
    tmat = lax.dot_general(theta_s[...], chol_s[...], (((1,), (1,)), ((), ())), preferred_element_type=f32)
    n = walkers // 2
    for w in range(walkers):
        row = w // n * (weight_ref.shape[0] // 2) + first + w % n
        weight = weight_ref[row:row + 1, :]
        total = jnp.zeros((LANES, LANES), f32)
        for g in range(half):
            block = tmat[w * LANES:(w + 1) * LANES, g * LANES:(g + 1) * LANES]
            total += block * block.T
            cotan_s[g * LANES:(g + 1) * LANES, w * LANES:(w + 1) * LANES] = (weight * block).astype(bf16)
        energy_ref[w:w + 1, :] = -0.5 * jnp.sum(total, axis=0, keepdims=True)
    for s, ref in enumerate((own_ref, core_ref, same_ref, other_ref)):
        ref[...] = jnp.dot(cotan_s[...], theta_s[:, column(s, padded)], preferred_element_type=f32)


def last_walkers(
    mine, theirs, chol_s, weight_ref, same_part, other_part, same_ref, other_ref, tmat_ref, theta_s, cotan_s,
    *, half, nocc, padded
):
    place_theta([mine, theirs], theta_s, nocc)
    tmat = lax.dot_general(theta_s[...], chol_s[...], (((1,), (1,)), ((), ())), preferred_element_type=f32)
    tmat_ref[...] = tmat
    for w in range(2):
        row = (w + 1) * (weight_ref.shape[0] // 2) - 1
        weight = weight_ref[row:row + 1, :]
        for g in range(half):
            block = tmat[w * LANES:(w + 1) * LANES, g * LANES:(g + 1) * LANES]
            cotan_s[g * LANES:(g + 1) * LANES, w * LANES:(w + 1) * LANES] = (weight * block).astype(bf16)
    for ref, part, s in ((same_ref, same_part, 2), (other_ref, other_part, 3)):
        grad = part[...] + jnp.dot(cotan_s[...], theta_s[:, column(s, padded)], preferred_element_type=f32)
        store_grad(grad, ref, half, nocc)


def store_grad(grad, ref, half, nocc):
    for g in range(half):
        if len(ref.shape) == 2:
            ref[g * nocc:(g + 1) * nocc] = grad[g * LANES:g * LANES + nocc].astype(ref.dtype)
        else:
            ref[g] = grad[g * LANES:g * LANES + ref.shape[1]].astype(ref.dtype)


def chip_walkers(
    tmat_ref, theta_s, cotan_s, own_part, core_part, first_ref, own_ref, core_ref, energy_ref,
    *, nocc, half, rows, padded
):
    for ref, part, s in ((core_ref, core_part, 1), (own_ref, own_part, 0)):
        grad = part[...] + jnp.dot(cotan_s[...], theta_s[:, column(s, padded)], preferred_element_type=f32)
        for g in range(half):
            ref[g] = grad[g * LANES:g * LANES + rows]
    early = first_ref.shape[0] // 2
    for w in range(2 * early):
        energy = first_ref[w:w + 1, :]
        if w < early:
            energy_ref[w:w + 1, :] = energy
        else:
            core_ref[w - early, nocc:nocc + 1, :LANES] = energy
    for w in range(2):
        total = jnp.zeros((LANES, LANES), f32)
        for g in range(half):
            block = tmat_ref[w * LANES:(w + 1) * LANES, g * LANES:(g + 1) * LANES]
            total += block * block.T
        energy = -0.5 * jnp.sum(total, axis=0, keepdims=True)
        if w == 0:
            energy_ref[early:early + 1, :] = energy
        else:
            core_ref[early, nocc:nocc + 1, :LANES] = energy


def pick_energies(energy_ref, core_ref, *out_refs, nocc):
    for w, ref in enumerate(out_refs):
        ref[...] = energy_ref[w:w + 1, :] + core_ref[w, nocc:nocc + 1, :LANES]


def finish(*refs):
    *refs, out_hbm, energy_hbm, out_ref, energy_ref, sems = refs
    own_ref, same_ref, other_ref, core_ref, *energy_refs = refs
    half, rows = own_ref.shape[:2]
    nocc, gdev, width = out_ref.shape
    h = lax.rem(lax.axis_index("walk"), 2)
    energy = sum(ref[...] for ref in energy_refs)
    energy_ref[...] = jnp.sum(energy, axis=1, keepdims=True)
    copies = [pltpu.make_async_copy(energy_ref, energy_hbm, sems.at[0])]
    copies[0].start()
    for n, start in enumerate(range(0, nocc, 32), start=1):
        stop = min(start + 32, nocc)

        def arrived(ref):
            return jnp.stack([ref[g * nocc + start:g * nocc + stop, :].astype(f32) for g in range(half)])

        mine = own_ref[:, start:stop, :] + arrived(same_ref)
        theirs = core_ref[:half, start:stop, :] + arrived(other_ref)
        low = jnp.where(h == 0, mine, theirs)
        high = jnp.where(h == 0, theirs, mine)
        both = jnp.swapaxes(jnp.concatenate([low, high], axis=0), 0, 1)
        out_ref[start:stop] = both[:, :, :width]
        copies.append(pltpu.make_async_copy(out_ref.at[start:stop], out_hbm.at[start:stop], sems.at[n]))
        copies[-1].start()
    for copy in copies:
        copy.wait()


def call(kernel, outs, *operands, scratch=(), ins=VMEM, out=VMEM, grant=GRANT):
    return pl.pallas_call(
        kernel,
        out_shape=outs,
        in_specs=[pl.BlockSpec(memory_space=ins)] * len(operands),
        out_specs=jax.tree.map(lambda _: pl.BlockSpec(memory_space=out), outs),
        scratch_shapes=scratch,
        compiler_params=pltpu.CompilerParams(vmem_limit_bytes=grant),
    )(*operands)


def body(chol_vectors, green_blocks, phase_codes, occupations, *, nchol, nwalk):
    gdev, nocc, width = chol_vectors.shape
    norb = green_blocks.shape[3]
    half = gdev // 2
    rows = ceil_to(nocc + 1, 8)
    padded = ceil_to(width, LANES)
    wide = padded * nwalk
    sizes = dict(half=half, padded=padded)

    def swap(x, flip):
        return lax.ppermute(x, "walk", [(i, i ^ flip) for i in range(nwalk)])

    def turn(x, pairs):
        return lax.ppermute(x, "chol", pairs)

    def struct(*shape, dtype=bf16):
        return jax.ShapeDtypeStruct(shape, dtype)

    block = struct(2 * nocc, wide // 2)
    theta = call(
        functools.partial(prep_theta, width=width, padded=padded),
        pltpu.VMEM(block.shape, bf16),
        occupations.reshape(1, nocc),
        green_blocks.reshape(nocc, norb),
        scratch=[pltpu.VMEM((1, nocc), jnp.int32), pltpu.VMEM((nocc, norb), bf16), pltpu.SemaphoreType.DMA((2,))],
        ins=HBM,
        grant=PREP,
    )
    pair = call(prep_chol, struct(2, *block.shape), chol_vectors, theta, phase_codes)

    if nchol == 4:
        there = [(0, 2), (2, 3), (3, 1), (1, 0)]
        back = [(b, a) for a, b in there]
        paths = [there, back, [(i, 3 - i) for i in range(4)]]
        first = turn(theta, there)
        early = [first, turn(theta, back)]
        last = turn(theta, [(1, 2), (2, 1)]), turn(first, [(1, 0), (2, 3)])
    else:
        paths = [[(i, (i + d) % nchol) for i in range(nchol)] for d in range(1, nchol)]
        *early, last = [turn(theta, path) for path in paths]
    sources = [list(range(nchol))] + [[a for a, _ in sorted(path, key=lambda p: p[1])] for path in paths]

    paired = swap(pair, 1)
    crossed = swap(chol_vectors, 2)
    relayed = swap(call(functools.partial(relay, padded=padded), block, crossed), 1)
    chol, weight = call(
        functools.partial(place_chol, sources=sources, nocc=nocc, width=width, **sizes),
        (struct(half * LANES, wide), struct(2 * nchol, LANES, dtype=f32)),
        chol_vectors,
        paired,
        crossed,
        relayed,
        phase_codes,
    )
    term = struct(half * LANES, padded, dtype=f32)
    mine = [theta] + early
    theirs = [paired] + [swap(t, 1) for t in early]
    grads, energies = None, []
    for start in range(0, nchol - 1, 3):
        group = mine[start:start + 3] + theirs[start:start + 3]
        walkers = len(group)
        *terms, energy = call(
            functools.partial(first_walkers, first=start, walkers=walkers, nocc=nocc, **sizes),
            (term,) * 4 + (struct(walkers, LANES, dtype=f32),),
            *group,
            chol,
            weight,
            scratch=[pltpu.VMEM((walkers * LANES, wide), bf16), pltpu.VMEM((half * LANES, walkers * LANES), bf16)],
        )
        grads = terms if grads is None else [a + b for a, b in zip(grads, terms)]
        energies += [(energy[:walkers // 2], energy[walkers // 2:])]
    if len(energies) > 1:
        energy = jnp.concatenate([e[i] for i in (0, 1) for e in energies])
    if nchol == 4:
        held = last
        last = call(join, block, *held)

    walkers = 2
    same, other, tmat, theta_s, cotan_s = call(
        functools.partial(last_walkers, nocc=nocc, **sizes),
        (
            struct(half * nocc, padded),
            struct(half * nocc, padded),
            struct(walkers * LANES, half * LANES, dtype=f32),
            struct(walkers * LANES, wide),
            struct(half * LANES, walkers * LANES),
        ),
        last,
        swap(last, 1),
        chol,
        weight,
        grads[2],
        grads[3],
    )
    same, other = swap(same, 2), swap(other, 3)
    tall = max(half, nchol)
    own, core, energy = call(
        functools.partial(chip_walkers, nocc=nocc, rows=rows, **sizes),
        (struct(half, rows, padded, dtype=f32), struct(tall, rows, padded, dtype=f32), struct(nchol, LANES, dtype=f32)),
        tmat,
        theta_s,
        cotan_s,
        grads[0],
        grads[1],
        energy,
    )
    core = swap(core, 1)
    part, *parts = call(
        functools.partial(pick_energies, nocc=nocc), (struct(1, LANES, dtype=f32),) * nchol, energy, core
    )
    parts = [turn(p, [(b, a) for a, b in path]) for p, path in zip(parts, paths)]
    chol_grad, energies = call(
        finish,
        (struct(nocc, gdev, width, dtype=f32), struct(1, 1, dtype=f32)),
        own,
        same,
        other,
        core,
        part,
        *parts,
        out=HBM,
        scratch=[
            pltpu.VMEM((nocc, gdev, width), f32),
            pltpu.VMEM((1, 1), f32),
            pltpu.SemaphoreType.DMA((1 - (-rows // 32),)),
        ],
    )
    return jnp.swapaxes(chol_grad, 0, 1), energies


def solution(mesh):
    placed = (
        P("chol", None, "walk"),
        P(("dom", "walk"), "chol", None, None),
        P(("dom", "walk"), None),
        P(("dom", "walk"), "chol", None),
    )
    return jax.shard_map(
        functools.partial(body, nchol=mesh.shape["chol"], nwalk=mesh.shape["walk"]),
        mesh=mesh,
        in_specs=placed,
        out_specs=(P(("dom", "chol"), None, "walk"), P(("dom", "walk"), "chol")),
        check_vma=False,
    )
```

time: 38.6 us -> 36.9 us (0.956)
  local copies, waits for them, and re-layouts: 1.67 us -> 0.09 us
  waiting for transfers between devices: 15 us -> 14 us
  Pallas kernels: 4.9 us -> 5.69 us
    unnamed x9 -> x5, local copies, waits for them, and re-layouts: 1.67 us -> 0.09 us
    pallas_call x10, Pallas kernels: 4.9 us -> 5.69 us  [call(): pl.pallas_call(kernel, out_shape=outs, in_specs=[pl.BlockSpec(memory_spac...]
    ppermute x7, waiting for transfers between devices: 6.46 us -> 5.76 us  [turn(): return lax.ppermute(x, 'chol', pairs)]
where the time goes in v3:
time: 36.9 us; the launch traced here: 36.5 us
  starting transfers between devices  15.9 us (43%)
  waiting for transfers between devices  14 us (38%)
  Pallas kernels  5.69 us (15%)
  between operations  0.8 us (2%)
    ppermute x7, starting transfers between devices, turn(): return lax.ppermute(x, 'chol', pairs)  11.5 us
    ppermute x9, waiting for transfers between devices, swap(): return lax.ppermute(x, 'walk', [(i, i ^ flip) for i in range(nwalk)])  8.28 us
    ppermute x7, waiting for transfers between devices, turn(): return lax.ppermute(x, 'chol', pairs)  5.76 us
    pallas_call x10, Pallas kernels, call(): pl.pallas_call(kernel, out_shape=outs, in_specs=[pl.BlockSpec(memory_spac...  5.69 us
    ppermute x9, starting transfers between devices, swap(): return lax.ppermute(x, 'walk', [(i, i ^ flip) for i in range(nwalk)])  4.34 us
  transfers between devices with their start and end apart: 16, of which 5 were waited for; matrix products, arithmetic and copies ran while one was open for 0% of the time, Pallas kernels for 6%

profile of v3, /device:TPU:0, one launch (start us, length us, event | category | flops | bytes accessed | tf_op | source)
XLA Modules:
  0.0 36.5 jit_solution(10365489175683395138)
XLA Ops:
  0.6 0.0 copy-start.1
  0.6 1.3 %shard_map.59.theta_ref.refs_0_ = bf16[200,512]{1,0:T(8,128)(2,1)S(1)} custom-call(s32[1,100]{1,0:T(1,128)} %bitcast.4, bf16[100,1000]{1,0:T(8,128)(2,1)} %bitcast.3), custom_call_target="tpu_custom_call" | custom-call | tf_op jit(solution)/shard_map/pallas_call | solution.py:216
  2.0 0.0 copy-start
  2.0 4.1 %collective-permute-start.1 = (bf16[200,512]{1,0:T(8,128)(2,1)S(1)}, bf16[200,512]{1,0:T(8,128)(2,1)S(1)}, u32[]{:S(2)}, u32[]{:S(2)}) collective-permute-start(bf16[200,512]{1,0:T(8,128)(2,1)S(1)} %shard_map.59.theta_ref.refs_0_), channel_id=1, source_target_pairs={{0,8},{8,12},{12,4},{4,0},{1,9},{9,13},{13,5},{5,1},{2,10},{10,14}... | collective-permute-start | bytes 614408 | tf_op jit(solution)/shard_map/ppermute | solution.py:239
  6.1 0.0 copy-done.1
  6.1 0.1 copy.8.chol_ref.own_ref
  6.2 1.6 %collective-permute-start.5 = (bf16[8,100,250]{2,1,0:T(8,128)(2,1)S(1)}, bf16[8,100,250]{2,1,0:T(8,128)(2,1)S(1)}, u32[]{:S(2)}, u32[]{:S(2)}) collective-permute-start(bf16[8,100,250]{2,1,0:T(8,128)(2,1)S(1)} %copy.8.chol_ref.own_ref), channel_id=1, source_target_pairs={{0,2},{1,3},{2,0},{3,1},{4,6},{5,7},{6,4},{7,5},{8,10},{9,11},{10,... | collective-permute-start | bytes 1200008 | tf_op jit(solution)/shard_map/ppermute | solution.py:236
  7.7 0.0 copy-done
  7.7 0.1 shard_map.61
  7.8 0.0 collective-permute-start.4
  7.9 0.1 collective-permute-start.7
  7.9 0.7 %collective-permute-start = (bf16[200,512]{1,0:T(8,128)(2,1)S(1)}, bf16[200,512]{1,0:T(8,128)(2,1)S(1)}, u32[]{:S(2)}, u32[]{:S(2)}) collective-permute-start(bf16[200,512]{1,0:T(8,128)(2,1)S(1)} %shard_map.59.theta_ref.refs_0_), channel_id=1, source_target_pairs={{4,8},{8,4},{5,9},{9,5},{6,10},{10,6},{7,11},{11,7},{20,24},{24,20... | collective-permute-start | bytes 614408 | tf_op jit(solution)/shard_map/ppermute | solution.py:239
  8.6 3.0 %collective-permute-done.1.refs_1_ = bf16[200,512]{1,0:T(8,128)(2,1)S(1)} collective-permute-done((bf16[200,512]{1,0:T(8,128)(2,1)S(1)}, bf16[200,512]{1,0:T(8,128)(2,1)S(1)}, u32[]{:S(2)}, u32[]{:S(2)}) %collective-permute-start.1) | collective-permute-done | bytes 204832 | tf_op jit(solution)/shard_map/ppermute | solution.py:239
  11.6 1.3 %collective-permute-start.2 = (bf16[200,512]{1,0:T(8,128)(2,1)S(1)}, bf16[200,512]{1,0:T(8,128)(2,1)S(1)}, u32[]{:S(2)}, u32[]{:S(2)}) collective-permute-start(bf16[200,512]{1,0:T(8,128)(2,1)S(1)} %collective-permute-done.1.refs_1_), channel_id=1, source_target_pairs={{4,0},{8,12},{5,1},{9,13},{6,2},{10,14},{7,3},{11,15},{20,16},{24,... | collective-permute-start | bytes 614408 | tf_op jit(solution)/shard_map/ppermute | solution.py:239
  12.9 4.7 %collective-permute-done.5.crossed_ref.same_ref = bf16[8,100,250]{2,1,0:T(8,128)(2,1)S(1)} collective-permute-done((bf16[8,100,250]{2,1,0:T(8,128)(2,1)S(1)}, bf16[8,100,250]{2,1,0:T(8,128)(2,1)S(1)}, u32[]{:S(2)}, u32[]{:S(2)}) %collective-permute-start.5) | collective-permute-done | bytes 400032 | tf_op jit(solution)/shard_map/ppermute | solution.py:236
  17.6 0.1 collective-permute-start.6
  17.6 0.0 collective-permute-done.7.refs_2_
  17.6 0.5 %collective-permute-start.9 = (bf16[200,512]{1,0:T(8,128)(2,1)S(1)}, bf16[200,512]{1,0:T(8,128)(2,1)S(1)}, u32[]{:S(2)}, u32[]{:S(2)}) collective-permute-start(bf16[200,512]{1,0:T(8,128)(2,1)S(1)} %collective-permute-done.7.refs_2_), channel_id=1, source_target_pairs={{0,1},{1,0},{2,3},{3,2},{4,5},{5,4},{6,7},{7,6},{8,9},{9,8},{10,11... | collective-permute-start | bytes 614408 | tf_op jit(solution)/shard_map/ppermute | solution.py:236
  18.1 0.0 collective-permute-done.a_ref
  18.1 0.1 collective-permute-start.8
  18.2 2.8 %collective-permute-done.2.b_ref = bf16[200,512]{1,0:T(8,128)(2,1)S(1)} collective-permute-done((bf16[200,512]{1,0:T(8,128)(2,1)S(1)}, bf16[200,512]{1,0:T(8,128)(2,1)S(1)}, u32[]{:S(2)}, u32[]{:S(2)}) %collective-permute-start.2) | collective-permute-done | bytes 204832 | tf_op jit(solution)/shard_map/ppermute | solution.py:239
  21.0 0.1 collective-permute-start.3
  21.1 0.0 collective-permute-done.4.pair_ref.refs_3_
  21.1 0.0 collective-permute-done.6.other_ref
  21.1 0.2 shard_map.63
  21.4 0.0 collective-permute-done.9.refs_5_
  21.4 0.0 collective-permute-done.8.refs_4_
  21.4 1.9 %shard_map.64 = (f32[512,256]{1,0:T(8,128)S(1)}, f32[512,256]{1,0:T(8,128)S(1)}, f32[512,256]{1,0:T(8,128)S(1)}, f32[512,256]{1,0:T(8,128)S(1)}, f32[6,128]{1,0:T(8,128)S(1)}) custom-call(bf16[200,512]{1,0:T(8,128)(2,1)S(1)} %shard_map.59.theta_ref.refs_0_, bf16[200,512]{1,0:T(8,128)(2,1)S(1)} %collective-permute-done.1.refs_1_, ...), custom_call_target="tpu_custom_call" | custom-call | tf_op jit(solution)/shard_map/pallas_call | solution.py:216
  23.3 0.0 collective-permute-done.3.theirs
  23.3 0.7 %shard_map.65 = (bf16[400,256]{1,0:T(8,128)(2,1)S(1)}, bf16[400,256]{1,0:T(8,128)(2,1)S(1)}, f32[256,512]{1,0:T(8,128)S(1)}, bf16[256,1024]{1,0:T(8,128)(2,1)S(1)}, bf16[512,256]{1,0:T(8,128)(2,1)S(1)}) custom-call(bf16[200,512]{1,0:T(8,128)(2,1)S(1)} %shard_map.60.mine, bf16[200,512]{1,0:T(8,128)(2,1)S(1)} %collective-permute-done.3.theirs, ...), custom_call_target="tpu_custom_call" | custom-call | tf_op jit(solution)/shard_map/pallas_call | solution.py:216
  24.0 0.3 shard_map.66
  24.4 0.5 %collective-permute-start.12 = (f32[4,104,256]{2,1,0:T(8,128)S(1)}, f32[4,104,256]{2,1,0:T(8,128)S(1)}, u32[]{:S(2)}, u32[]{:S(2)}) collective-permute-start(f32[4,104,256]{2,1,0:T(8,128)S(1)} %get-tuple-element.36), channel_id=1, source_target_pairs={{0,1},{1,0},{2,3},{3,2},{4,5},{5,4},{6,7},{7,6},{8,9},{9,8},{10,11... | collective-permute-start | bytes 1277960 | tf_op jit(solution)/shard_map/ppermute | solution.py:236
  24.9 1.5 %collective-permute-start.10 = (bf16[400,256]{1,0:T(8,128)(2,1)S(1)}, bf16[400,256]{1,0:T(8,128)(2,1)S(1)}, u32[]{:S(2)}, u32[]{:S(2)}) collective-permute-start(bf16[400,256]{1,0:T(8,128)(2,1)S(1)} %get-tuple-element.34), channel_id=1, source_target_pairs={{0,2},{1,3},{2,0},{3,1},{4,6},{5,7},{6,4},{7,5},{8,10},{9,11},{10,... | collective-permute-start | bytes 614408 | tf_op jit(solution)/shard_map/ppermute | solution.py:236
  26.4 0.0 collective-permute-start.11
  26.4 0.0 collective-permute-done.12.core_ref.refs_3_
  26.4 1.5 %collective-permute-start.13 = (f32[1,128]{1,0:T(1,128)S(1)}, f32[1,128]{1,0:T(1,128)S(1)}, u32[]{:S(2)}, u32[]{:S(2)}) collective-permute-start(f32[1,128]{1,0:T(1,128)S(1)} %get-tuple-element.39), channel_id=1, source_target_pairs={{8,0},{12,8},{4,12},{0,4},{9,1},{13,9},{5,13},{1,5},{10,2},{14,10}... | collective-permute-start | bytes 1544 | tf_op jit(solution)/shard_map/ppermute | solution.py:239
  27.9 1.5 %collective-permute-start.14 = (f32[1,128]{1,0:T(1,128)S(1)}, f32[1,128]{1,0:T(1,128)S(1)}, u32[]{:S(2)}, u32[]{:S(2)}) collective-permute-start(f32[1,128]{1,0:T(1,128)S(1)} %get-tuple-element.40), channel_id=1, source_target_pairs={{0,8},{8,12},{12,4},{4,0},{1,9},{9,13},{13,5},{5,1},{2,10},{10,14}... | collective-permute-start | bytes 1544 | tf_op jit(solution)/shard_map/ppermute | solution.py:239
  29.4 2.5 %collective-permute-start.15 = (f32[1,128]{1,0:T(1,128)S(1)}, f32[1,128]{1,0:T(1,128)S(1)}, u32[]{:S(2)}, u32[]{:S(2)}) collective-permute-start(f32[1,128]{1,0:T(1,128)S(1)} %get-tuple-element.41), channel_id=1, source_target_pairs={{12,0},{8,4},{4,8},{0,12},{13,1},{9,5},{5,9},{1,13},{14,2},{10,6},... | collective-permute-start | bytes 1544 | tf_op jit(solution)/shard_map/ppermute | solution.py:239
  31.9 1.0 %collective-permute-done.10.refs_1_ = bf16[400,256]{1,0:T(8,128)(2,1)S(1)} collective-permute-done((bf16[400,256]{1,0:T(8,128)(2,1)S(1)}, bf16[400,256]{1,0:T(8,128)(2,1)S(1)}, u32[]{:S(2)}, u32[]{:S(2)}) %collective-permute-start.10) | collective-permute-done | bytes 204832 | tf_op jit(solution)/shard_map/ppermute | solution.py:236
  32.8 2.6 %collective-permute-done.11.refs_2_ = bf16[400,256]{1,0:T(8,128)(2,1)S(1)} collective-permute-done((bf16[400,256]{1,0:T(8,128)(2,1)S(1)}, bf16[400,256]{1,0:T(8,128)(2,1)S(1)}, u32[]{:S(2)}, u32[]{:S(2)}) %collective-permute-start.11) | collective-permute-done | bytes 204832 | tf_op jit(solution)/shard_map/ppermute | solution.py:236
  35.5 0.0 collective-permute-done.13.refs_5_
  35.5 0.0 collective-permute-done.14.refs_6_
  35.5 0.0 collective-permute-done.15.refs_7_
  35.5 1.0 %shard_map.68 = (f32[100,8,250]{2,1,0:T(8,128)}, f32[1,1]{1,0:T(1,128)}) custom-call(f32[4,104,256]{2,1,0:T(8,128)S(1)} %get-tuple-element.33.refs_0_, bf16[400,256]{1,0:T(8,128)(2,1)S(1)} %collective-permute-done.10.refs_1_, bf16[400,256]{1,0:T(8,128)(2,1)S(1)} %collective-permute-done.11.refs_2_, ...), custom_call_target="tpu_custom_call" | custom-call | tf_op jit(solution)/shard_map/pallas_call | solution.py:216
  (3 shorter events, 0.1 us)
Async XLA Ops:
  0.6 5.5 %copy-start.1 = (bf16[8,100,250]{2,0,1:T(8,128)(2,1)S(1)}, bf16[8,100,250]{2,0,1:T(8,128)(2,1)}, u32[]{:S(2)}) copy-start(bf16[8,100,250]{2,0,1:T(8,128)(2,1)} %param.4) | copy-start | bytes 1200004
  2.0 5.7 %copy-start = (s32[1,4]{1,0:T(1,128)S(1)}, s32[1,4]{1,0:T(1,128)}, u32[]{:S(2)}) copy-start(s32[1,4]{1,0:T(1,128)} %code_ref.3) | copy-start | bytes 52
  2.0 9.6 %collective-permute-start.1 = (bf16[200,512]{1,0:T(8,128)(2,1)S(1)}, bf16[200,512]{1,0:T(8,128)(2,1)S(1)}, u32[]{:S(2)}, u32[]{:S(2)}) collective-permute-start(bf16[200,512]{1,0:T(8,128)(2,1)S(1)} %shard_map.59.theta_ref.refs_0_), channel_id=1, source_target_pairs={{0,8},{8,12},{12,4},{4,0},{1,9},{9,13},{13,5},{5,1},{2,10},{10,14}... | collective-permute-start | bytes 614408 | tf_op jit(solution)/shard_map/ppermute | solution.py:239
  6.2 11.3 %collective-permute-start.5 = (bf16[8,100,250]{2,1,0:T(8,128)(2,1)S(1)}, bf16[8,100,250]{2,1,0:T(8,128)(2,1)S(1)}, u32[]{:S(2)}, u32[]{:S(2)}) collective-permute-start(bf16[8,100,250]{2,1,0:T(8,128)(2,1)S(1)} %copy.8.chol_ref.own_ref), channel_id=1, source_target_pairs={{0,2},{1,3},{2,0},{3,1},{4,6},{5,7},{6,4},{7,5},{8,10},{9,11},{10,... | collective-permute-start | bytes 1200008 | tf_op jit(solution)/shard_map/ppermute | solution.py:236
  7.8 13.3 %collective-permute-start.4 = (bf16[2,200,512]{2,1,0:T(8,128)(2,1)S(1)}, bf16[2,200,512]{2,1,0:T(8,128)(2,1)S(1)}, u32[]{:S(2)}, u32[]{:S(2)}) collective-permute-start(bf16[2,200,512]{2,1,0:T(8,128)(2,1)S(1)} %shard_map.61), channel_id=1, source_target_pairs={{0,1},{1,0},{2,3},{3,2},{4,5},{5,4},{6,7},{7,6},{8,9},{9,8},{10,11... | collective-permute-start | bytes 1228808 | tf_op jit(solution)/shard_map/ppermute | solution.py:236
  7.9 9.8 %collective-permute-start.7 = (bf16[200,512]{1,0:T(8,128)(2,1)S(1)}, bf16[200,512]{1,0:T(8,128)(2,1)S(1)}, u32[]{:S(2)}, u32[]{:S(2)}) collective-permute-start(bf16[200,512]{1,0:T(8,128)(2,1)S(1)} %shard_map.59.theta_ref.refs_0_), channel_id=1, source_target_pairs={{8,0},{12,8},{4,12},{0,4},{9,1},{13,9},{5,13},{1,5},{10,2},{14,10}... | collective-permute-start | bytes 614408 | tf_op jit(solution)/shard_map/ppermute | solution.py:239
  7.9 10.2 %collective-permute-start = (bf16[200,512]{1,0:T(8,128)(2,1)S(1)}, bf16[200,512]{1,0:T(8,128)(2,1)S(1)}, u32[]{:S(2)}, u32[]{:S(2)}) collective-permute-start(bf16[200,512]{1,0:T(8,128)(2,1)S(1)} %shard_map.59.theta_ref.refs_0_), channel_id=1, source_target_pairs={{4,8},{8,4},{5,9},{9,5},{6,10},{10,6},{7,11},{11,7},{20,24},{24,20... | collective-permute-start | bytes 614408 | tf_op jit(solution)/shard_map/ppermute | solution.py:239
  11.6 9.4 %collective-permute-start.2 = (bf16[200,512]{1,0:T(8,128)(2,1)S(1)}, bf16[200,512]{1,0:T(8,128)(2,1)S(1)}, u32[]{:S(2)}, u32[]{:S(2)}) collective-permute-start(bf16[200,512]{1,0:T(8,128)(2,1)S(1)} %collective-permute-done.1.refs_1_), channel_id=1, source_target_pairs={{4,0},{8,12},{5,1},{9,13},{6,2},{10,14},{7,3},{11,15},{20,16},{24,... | collective-permute-start | bytes 614408 | tf_op jit(solution)/shard_map/ppermute | solution.py:239
  17.6 3.6 %collective-permute-start.6 = (bf16[200,512]{1,0:T(8,128)(2,1)S(1)}, bf16[200,512]{1,0:T(8,128)(2,1)S(1)}, u32[]{:S(2)}, u32[]{:S(2)}) collective-permute-start(bf16[200,512]{1,0:T(8,128)(2,1)S(1)} %shard_map.62), channel_id=1, source_target_pairs={{0,1},{1,0},{2,3},{3,2},{4,5},{5,4},{6,7},{7,6},{8,9},{9,8},{10,11... | collective-permute-start | bytes 614408 | tf_op jit(solution)/shard_map/ppermute | solution.py:236
  17.6 3.7 %collective-permute-start.9 = (bf16[200,512]{1,0:T(8,128)(2,1)S(1)}, bf16[200,512]{1,0:T(8,128)(2,1)S(1)}, u32[]{:S(2)}, u32[]{:S(2)}) collective-permute-start(bf16[200,512]{1,0:T(8,128)(2,1)S(1)} %collective-permute-done.7.refs_2_), channel_id=1, source_target_pairs={{0,1},{1,0},{2,3},{3,2},{4,5},{5,4},{6,7},{7,6},{8,9},{9,8},{10,11... | collective-permute-start | bytes 614408 | tf_op jit(solution)/shard_map/ppermute | solution.py:236
  18.1 3.2 %collective-permute-start.8 = (bf16[200,512]{1,0:T(8,128)(2,1)S(1)}, bf16[200,512]{1,0:T(8,128)(2,1)S(1)}, u32[]{:S(2)}, u32[]{:S(2)}) collective-permute-start(bf16[200,512]{1,0:T(8,128)(2,1)S(1)} %collective-permute-done.1.refs_1_), channel_id=1, source_target_pairs={{0,1},{1,0},{2,3},{3,2},{4,5},{5,4},{6,7},{7,6},{8,9},{9,8},{10,11... | collective-permute-start | bytes 614408 | tf_op jit(solution)/shard_map/ppermute | solution.py:236
  21.0 2.2 %collective-permute-start.3 = (bf16[200,512]{1,0:T(8,128)(2,1)S(1)}, bf16[200,512]{1,0:T(8,128)(2,1)S(1)}, u32[]{:S(2)}, u32[]{:S(2)}) collective-permute-start(bf16[200,512]{1,0:T(8,128)(2,1)S(1)} %shard_map.60.mine), channel_id=1, source_target_pairs={{0,1},{1,0},{2,3},{3,2},{4,5},{5,4},{6,7},{7,6},{8,9},{9,8},{10,11... | collective-permute-start | bytes 614408 | tf_op jit(solution)/shard_map/ppermute | solution.py:236
  24.4 2.0 %collective-permute-start.12 = (f32[4,104,256]{2,1,0:T(8,128)S(1)}, f32[4,104,256]{2,1,0:T(8,128)S(1)}, u32[]{:S(2)}, u32[]{:S(2)}) collective-permute-start(f32[4,104,256]{2,1,0:T(8,128)S(1)} %get-tuple-element.36), channel_id=1, source_target_pairs={{0,1},{1,0},{2,3},{3,2},{4,5},{5,4},{6,7},{7,6},{8,9},{9,8},{10,11... | collective-permute-start | bytes 1277960 | tf_op jit(solution)/shard_map/ppermute | solution.py:236
  24.9 7.9 %collective-permute-start.10 = (bf16[400,256]{1,0:T(8,128)(2,1)S(1)}, bf16[400,256]{1,0:T(8,128)(2,1)S(1)}, u32[]{:S(2)}, u32[]{:S(2)}) collective-permute-start(bf16[400,256]{1,0:T(8,128)(2,1)S(1)} %get-tuple-element.34), channel_id=1, source_target_pairs={{0,2},{1,3},{2,0},{3,1},{4,6},{5,7},{6,4},{7,5},{8,10},{9,11},{10,... | collective-permute-start | bytes 614408 | tf_op jit(solution)/shard_map/ppermute | solution.py:236
  26.4 9.1 %collective-permute-start.11 = (bf16[400,256]{1,0:T(8,128)(2,1)S(1)}, bf16[400,256]{1,0:T(8,128)(2,1)S(1)}, u32[]{:S(2)}, u32[]{:S(2)}) collective-permute-start(bf16[400,256]{1,0:T(8,128)(2,1)S(1)} %get-tuple-element.35), channel_id=1, source_target_pairs={{0,3},{1,2},{2,1},{3,0},{4,7},{5,6},{6,5},{7,4},{8,11},{9,10},{10,... | collective-permute-start | bytes 614408 | tf_op jit(solution)/shard_map/ppermute | solution.py:236
  26.4 9.1 %collective-permute-start.13 = (f32[1,128]{1,0:T(1,128)S(1)}, f32[1,128]{1,0:T(1,128)S(1)}, u32[]{:S(2)}, u32[]{:S(2)}) collective-permute-start(f32[1,128]{1,0:T(1,128)S(1)} %get-tuple-element.39), channel_id=1, source_target_pairs={{8,0},{12,8},{4,12},{0,4},{9,1},{13,9},{5,13},{1,5},{10,2},{14,10}... | collective-permute-start | bytes 1544 | tf_op jit(solution)/shard_map/ppermute | solution.py:239
  27.9 7.5 %collective-permute-start.14 = (f32[1,128]{1,0:T(1,128)S(1)}, f32[1,128]{1,0:T(1,128)S(1)}, u32[]{:S(2)}, u32[]{:S(2)}) collective-permute-start(f32[1,128]{1,0:T(1,128)S(1)} %get-tuple-element.40), channel_id=1, source_target_pairs={{0,8},{8,12},{12,4},{4,0},{1,9},{9,13},{13,5},{5,1},{2,10},{10,14}... | collective-permute-start | bytes 1544 | tf_op jit(solution)/shard_map/ppermute | solution.py:239
  29.4 6.1 %collective-permute-start.15 = (f32[1,128]{1,0:T(1,128)S(1)}, f32[1,128]{1,0:T(1,128)S(1)}, u32[]{:S(2)}, u32[]{:S(2)}) collective-permute-start(f32[1,128]{1,0:T(1,128)S(1)} %get-tuple-element.41), channel_id=1, source_target_pairs={{12,0},{8,4},{4,8},{0,12},{13,1},{9,5},{5,9},{1,13},{14,2},{10,6},... | collective-permute-start | bytes 1544 | tf_op jit(solution)/shard_map/ppermute | solution.py:239

commit v4 on v3

--- a/solution.py
+++ b/solution.py
@@ -8,6 +8,8 @@
 from jax.sharding import PartitionSpec as P
 
 LANES = 128
+SPARE = 92
+OPT = {'c1': 'pair', 'a': 8, 'b2': 8, 'force': 0, 'c3': 0, 'hold': 0}
 GRANT = 16 * 1024 * 1024
 PREP = 56 * 1024 * 1024
 HBM = pltpu.MemorySpace.HBM
@@ -35,19 +37,28 @@
         out_ref[row:row + nocc, lane:lane + width] = theta[:, width * k:width * (k + 1)].astype(bf16)
 
 
-def prep_chol(chol_ref, theta_ref, code_ref, pair_ref):
+def prep_chol(chol_ref, code_ref, *refs):
+    *theta_ref, pair_ref = refs
     gdev, nocc, width = chol_ref.shape
     half = gdev // 2
-    padded = pair_ref.shape[2] // (half // 2)
-    pair_ref[0] = theta_ref[...]
-    pair_ref[1] = jnp.zeros(pair_ref.shape[1:], bf16)
-    fold_half(chol_ref, pair_ref.at[1], 1 - lax.rem(lax.axis_index("walk"), 2), padded)
+    cross_ref = pair_ref
+    if theta_ref:
+        pair_ref[0] = theta_ref[0][...]
+        cross_ref = pair_ref.at[1]
+    padded = cross_ref.shape[1] // (half // 2)
+    cross_ref[...] = jnp.zeros(cross_ref.shape, bf16)
+    fold_half(chol_ref, cross_ref, 1 - lax.rem(lax.axis_index("walk"), 2), padded)
     nchol = code_ref.shape[1]
     shape = (ceil_to(nchol, 8), nchol)
     diagonal = lax.broadcasted_iota(jnp.int32, shape, 0) == lax.broadcasted_iota(jnp.int32, shape, 1)
     codes = jnp.sum(jnp.where(diagonal, code_ref[...], 0).astype(f32), axis=1, keepdims=True)
-    lane = pair_ref.shape[2] - padded + width
-    pair_ref[1, :shape[0], lane:lane + 1] = codes.astype(bf16)
+    lane = cross_ref.shape[1] - padded + width
+    cross_ref[:shape[0], lane:lane + 1] = codes.astype(bf16)
+
+
+def pack(a_ref, b_ref, out_ref):
+    out_ref[0] = a_ref[...]
+    out_ref[1] = b_ref[...]
 
 
 def fold_half(chol_ref, out_ref, which, padded):
@@ -63,31 +74,39 @@
     fold_half(crossed_ref, out_ref, 1 - lax.rem(lax.axis_index("walk"), 2), padded)
 
 
-def join(a_ref, b_ref, out_ref):
-    out_ref[...] = a_ref[...] + b_ref[...]
+def lift(in_ref, *refs):
+    out_ref = refs[-1]
+    rows = in_ref.shape[0]
+    out_ref[:rows] = in_ref[...]
+    out_ref[rows:] = jnp.zeros((out_ref.shape[0] - rows, out_ref.shape[1]), out_ref.dtype)
+
+
+def source_of(me, path):
+    return sum(jnp.where(me == i, s, 0) for i, s in enumerate(path))
 
 
 def place_chol(
     own_ref, pair_ref, same_ref, other_ref, code_ref, out_ref, weight_ref, *, sources, half, nocc, width, padded
 ):
     out_ref[...] = jnp.zeros_like(out_ref)
+    cross_ref = pair_ref.at[1] if len(pair_ref.shape) == 3 else pair_ref
     h = lax.rem(lax.axis_index("walk"), 2)
     for g in range(half):
         row, lane = g // (half // 2) * nocc, g % (half // 2) * padded
         rows = slice(g * LANES, g * LANES + nocc)
         for s, ref in ((0, own_ref), (2, same_ref)):
             out_ref[rows, column(s, padded)] = jnp.pad(ref[h * half + g], ((0, 0), (0, padded - width)))
-        for s, ref in ((1, pair_ref.at[1]), (3, other_ref)):
+        for s, ref in ((1, cross_ref), (3, other_ref)):
             out_ref[rows, column(s, padded)] = ref[row:row + nocc, lane:lane + padded]
     nchol = code_ref.shape[1]
     me = lax.axis_index("chol")
-    lane = pair_ref.shape[2] - padded + width
-    theirs = pair_ref[1, :ceil_to(nchol, 16), lane:lane + 1].astype(f32)
+    lane = cross_ref.shape[1] - padded + width
+    theirs = cross_ref[:ceil_to(nchol, 16), lane:lane + 1].astype(f32)
     mine = code_ref[...].astype(f32)
     codes = jnp.zeros(weight_ref.shape, f32)
     at = lax.broadcasted_iota(jnp.int32, codes.shape, 0)
     for n, path in enumerate(sources):
-        source = sum(jnp.where(me == i, s, 0) for i, s in enumerate(path))
+        source = source_of(me, path)
         for group, (values, axis) in enumerate(((mine, 1), (theirs, 0))):
             here = lax.broadcasted_iota(jnp.int32, values.shape, axis) == source
             code = jnp.sum(jnp.where(here, values, 0.0), axis=axis, keepdims=True)
@@ -101,16 +120,17 @@
 
 def place_theta(thetas, theta_s, nocc):
     theta_s[...] = jnp.zeros_like(theta_s)
-    for w, ref in enumerate(thetas):
-        theta = ref[0] if len(ref.shape) == 3 else ref[...]
+    for w, (ref, n) in enumerate(thetas):
+        theta = ref[n] if len(ref.shape) == 3 else ref[...]
         wide = theta.shape[1]
         for i in range(2):
             theta_s[w * LANES:w * LANES + nocc, i * wide:(i + 1) * wide] = theta[i * nocc:(i + 1) * nocc]
 
 
-def first_walkers(*refs, first, walkers, half, nocc, padded):
+def first_walkers(*refs, first, counts, walkers, half, nocc, padded):
+    counts = list(counts)
     *thetas, chol_s, weight_ref, own_ref, core_ref, same_ref, other_ref, energy_ref, theta_s, cotan_s = refs
-    place_theta(thetas, theta_s, nocc)
+    place_theta([(ref, n) for ref in thetas for n in range(counts.pop(0))], theta_s, nocc)
     tmat = lax.dot_general(theta_s[...], chol_s[...], (((1,), (1,)), ((), ())), preferred_element_type=f32)
     n = walkers // 2
     for w in range(walkers):
@@ -130,7 +150,7 @@
     mine, theirs, chol_s, weight_ref, same_part, other_part, same_ref, other_ref, tmat_ref, theta_s, cotan_s,
     *, half, nocc, padded
 ):
-    place_theta([mine, theirs], theta_s, nocc)
+    place_theta([(mine, 0), (theirs, 0)], theta_s, nocc)
     tmat = lax.dot_general(theta_s[...], chol_s[...], (((1,), (1,)), ((), ())), preferred_element_type=f32)
     tmat_ref[...] = tmat
     for w in range(2):
@@ -147,47 +167,47 @@
 def store_grad(grad, ref, half, nocc):
     for g in range(half):
         if len(ref.shape) == 2:
-            ref[g * nocc:(g + 1) * nocc] = grad[g * LANES:g * LANES + nocc].astype(ref.dtype)
+            ref[g * nocc:(g + 1) * nocc] = grad[g * LANES:g * LANES + nocc, :ref.shape[1]].astype(ref.dtype)
         else:
             ref[g] = grad[g * LANES:g * LANES + ref.shape[1]].astype(ref.dtype)
 
 
-def chip_walkers(
-    tmat_ref, theta_s, cotan_s, own_part, core_part, first_ref, own_ref, core_ref, energy_ref,
-    *, nocc, half, rows, padded
-):
-    for ref, part, s in ((core_ref, core_part, 1), (own_ref, own_part, 0)):
+def chip_walkers(theta_s, cotan_s, own_part, core_part, own_ref, low_ref, high_ref, *, half, nocc, padded):
+    for part, s in ((core_part, 1), (own_part, 0)):
         grad = part[...] + jnp.dot(cotan_s[...], theta_s[:, column(s, padded)], preferred_element_type=f32)
-        for g in range(half):
-            ref[g] = grad[g * LANES:g * LANES + rows]
+        if s == 0:
+            store_grad(grad, own_ref, half, nocc)
+        else:
+            store_grad(grad, low_ref, half // 2, nocc)
+            store_grad(grad[half // 2 * LANES:], high_ref, half // 2, nocc)
+
+
+def last_energies(tmat_ref, first_ref, energy_ref, *, sources, half):
+    energy_ref[...] = jnp.zeros_like(energy_ref)
     early = first_ref.shape[0] // 2
-    for w in range(2 * early):
-        energy = first_ref[w:w + 1, :]
-        if w < early:
-            energy_ref[w:w + 1, :] = energy
-        else:
-            core_ref[w - early, nocc:nocc + 1, :LANES] = energy
+    me = lax.axis_index("chol")
+    rows = [pl.ds(me ^ source_of(me, path), 1) for path in sources]
     for w in range(2):
         total = jnp.zeros((LANES, LANES), f32)
         for g in range(half):
             block = tmat_ref[w * LANES:(w + 1) * LANES, g * LANES:(g + 1) * LANES]
             total += block * block.T
-        energy = -0.5 * jnp.sum(total, axis=0, keepdims=True)
-        if w == 0:
-            energy_ref[early:early + 1, :] = energy
-        else:
-            core_ref[early, nocc:nocc + 1, :LANES] = energy
-
-
-def pick_energies(energy_ref, core_ref, *out_refs, nocc):
-    for w, ref in enumerate(out_refs):
-        ref[...] = energy_ref[w:w + 1, :] + core_ref[w, nocc:nocc + 1, :LANES]
+        for n in range(early):
+            energy_ref[w, rows[n], :] = first_ref[w * early + n:w * early + n + 1]
+        energy_ref[w, rows[early], :] = -0.5 * jnp.sum(total, axis=0, keepdims=True)
+
+
+def halve(mine_ref, arrived_ref, keep_ref, send_ref):
+    ours, theirs = (ref.at[i] if len(ref.shape) == 3 else ref for i, ref in enumerate((mine_ref, arrived_ref)))
+    for n in range(keep_ref.shape[0]):
+        for ref, row in ((keep_ref, 2 * n), (send_ref, 2 * n + 1)):
+            ref[n:n + 1, :] = ours[row:row + 1, :] + theirs[row:row + 1, :]
 
 
 def finish(*refs):
     *refs, out_hbm, energy_hbm, out_ref, energy_ref, sems = refs
-    own_ref, same_ref, other_ref, core_ref, *energy_refs = refs
-    half, rows = own_ref.shape[:2]
+    own_ref, same_ref, other_ref, low_ref, high_ref, *energy_refs = refs
+    half = own_ref.shape[0]
     nocc, gdev, width = out_ref.shape
     h = lax.rem(lax.axis_index("walk"), 2)
     energy = sum(ref[...] for ref in energy_refs)
@@ -197,15 +217,17 @@
     for n, start in enumerate(range(0, nocc, 32), start=1):
         stop = min(start + 32, nocc)
 
-        def arrived(ref):
-            return jnp.stack([ref[g * nocc + start:g * nocc + stop, :].astype(f32) for g in range(half)])
-
-        mine = own_ref[:, start:stop, :] + arrived(same_ref)
-        theirs = core_ref[:half, start:stop, :] + arrived(other_ref)
+        def arrived(*refs):
+            n = half // len(refs)
+            blocks = [ref[g * nocc + start:g * nocc + stop, :width] for ref in refs for g in range(n)]
+            return jnp.stack([block.astype(f32) for block in blocks])
+
+        mine = own_ref[:, start:stop, :width] + arrived(same_ref)
+        theirs = arrived(low_ref, high_ref) + arrived(other_ref)
         low = jnp.where(h == 0, mine, theirs)
         high = jnp.where(h == 0, theirs, mine)
         both = jnp.swapaxes(jnp.concatenate([low, high], axis=0), 0, 1)
-        out_ref[start:stop] = both[:, :, :width]
+        out_ref[start:stop] = both
         copies.append(pltpu.make_async_copy(out_ref.at[start:stop], out_hbm.at[start:stop], sems.at[n]))
         copies[-1].start()
     for copy in copies:
@@ -227,7 +249,7 @@
     gdev, nocc, width = chol_vectors.shape
     norb = green_blocks.shape[3]
     half = gdev // 2
-    rows = ceil_to(nocc + 1, 8)
+    rows = ceil_to(nocc, 8)
     padded = ceil_to(width, LANES)
     wide = padded * nwalk
     sizes = dict(half=half, padded=padded)
@@ -251,7 +273,10 @@
         ins=HBM,
         grant=PREP,
     )
-    pair = call(prep_chol, struct(2, *block.shape), chol_vectors, theta, phase_codes)
+    if OPT["c1"] == "pair":
+        pair = call(prep_chol, struct(2, *block.shape), chol_vectors, phase_codes, theta)
+    else:
+        pair = call(prep_chol, block, chol_vectors, phase_codes)
 
     if nchol == 4:
         there = [(0, 2), (2, 3), (3, 1), (1, 0)]
@@ -259,7 +284,7 @@
         paths = [there, back, [(i, 3 - i) for i in range(4)]]
         first = turn(theta, there)
         early = [first, turn(theta, back)]
-        last = turn(theta, [(1, 2), (2, 1)]), turn(first, [(1, 0), (2, 3)])
+        last = turn(first, there)
     else:
         paths = [[(i, (i + d) % nchol) for i in range(nchol)] for d in range(1, nchol)]
         *early, last = [turn(theta, path) for path in paths]
@@ -279,13 +304,29 @@
     )
     term = struct(half * LANES, padded, dtype=f32)
     mine = [theta] + early
-    theirs = [paired] + [swap(t, 1) for t in early]
+    def lifted(x, extra, *dummy):
+        if not extra:
+            return x
+        return call(lift, struct(2 * nocc + extra, wide // 2), x, *dummy)
+
+    if OPT["c1"] == "pair":
+        a_ops = [paired, swap(lifted(early[0], OPT["a"]), 1)]
+        b_dummy = []
+    else:
+        a_ops = [swap(call(pack, struct(2, *block.shape), theta, early[0]), 1)]
+        b_dummy = [paired] if OPT["force"] else []
+    theirs = a_ops + [swap(lifted(early[1], OPT["b2"], *b_dummy), 1)] + [swap(t, 1) for t in early[2:]]
     grads, energies = None, []
     for start in range(0, nchol - 1, 3):
-        group = mine[start:start + 3] + theirs[start:start + 3]
-        walkers = len(group)
+        if start == 0 and len(a_ops) == 1:
+            group, counts = mine[:3] + theirs[:2], (1, 1, 1, 2, 1)
+        else:
+            shift = len(a_ops) - 2
+            group = mine[start:start + 3] + theirs[start + shift:start + 3 + shift]
+            counts = (1,) * len(group)
+        walkers = sum(counts)
         *terms, energy = call(
-            functools.partial(first_walkers, first=start, walkers=walkers, nocc=nocc, **sizes),
+            functools.partial(first_walkers, first=start, counts=counts, walkers=walkers, nocc=nocc, **sizes),
             (term,) * 4 + (struct(walkers, LANES, dtype=f32),),
             *group,
             chol,
@@ -296,9 +337,7 @@
         energies += [(energy[:walkers // 2], energy[walkers // 2:])]
     if len(energies) > 1:
         energy = jnp.concatenate([e[i] for i in (0, 1) for e in energies])
-    if nchol == 4:
-        held = last
-        last = call(join, block, *held)
+    theirs_last = swap(lifted(last, OPT["c3"]) if not OPT["hold"] else lax.optimization_barrier((last, energy))[0], 1)
 
     walkers = 2
     same, other, tmat, theta_s, cotan_s = call(
@@ -311,38 +350,42 @@
             struct(half * LANES, walkers * LANES),
         ),
         last,
-        swap(last, 1),
+        theirs_last,
         chol,
         weight,
         grads[2],
         grads[3],
     )
     same, other = swap(same, 2), swap(other, 3)
-    tall = max(half, nchol)
-    own, core, energy = call(
-        functools.partial(chip_walkers, nocc=nocc, rows=rows, **sizes),
-        (struct(half, rows, padded, dtype=f32), struct(tall, rows, padded, dtype=f32), struct(nchol, LANES, dtype=f32)),
+    energy = call(
+        functools.partial(last_energies, sources=sources, half=half),
+        struct(2, nchol + SPARE, LANES, dtype=f32),
         tmat,
+        energy,
+    )
+    own, *core = call(
+        functools.partial(chip_walkers, nocc=nocc, **sizes),
+        (struct(half, rows, padded, dtype=f32),) + (struct(half // 2 * nocc, width),) * 2,
         theta_s,
         cotan_s,
         grads[0],
         grads[1],
-        energy,
-    )
-    core = swap(core, 1)
-    part, *parts = call(
-        functools.partial(pick_energies, nocc=nocc), (struct(1, LANES, dtype=f32),) * nchol, energy, core
-    )
-    parts = [turn(p, [(b, a) for a, b in path]) for p, path in zip(parts, paths)]
+    )
+    core = [swap(c, 1) for c in core]
+    arrived, n, flip = swap(energy, 1), nchol // 2, 1
+    while n:
+        energy, send = call(halve, (struct(n, LANES, dtype=f32),) * 2, energy, arrived)
+        arrived = turn(send, [(i, i ^ flip) for i in range(nchol)])
+        n, flip = n // 2, flip * 2
     chol_grad, energies = call(
         finish,
         (struct(nocc, gdev, width, dtype=f32), struct(1, 1, dtype=f32)),
         own,
         same,
         other,
-        core,
-        part,
-        *parts,
+        *core,
+        energy,
+        arrived,
         out=HBM,
         scratch=[
             pltpu.VMEM((nocc, gdev, width), f32),

time: 36.9 us -> 36.3 us (0.984)
    ppermute x9 -> x11, waiting for transfers between devices: 8.28 us -> 0.15 us  [swap(): return lax.ppermute(x, 'walk', [(i, i ^ flip) for i in range(nwalk)])]
    ppermute x7 -> x5, waiting for transfers between devices: 5.76 us -> 13.6 us  [turn(): return lax.ppermute(x, 'chol', pairs)]
    ppermute x7 -> x5, starting transfers between devices: 11.5 us -> 10.5 us  [turn(): return lax.ppermute(x, 'chol', pairs)]
    ppermute x9 -> x11, starting transfers between devices: 4.34 us -> 5.12 us  [swap(): return lax.ppermute(x, 'walk', [(i, i ^ flip) for i in range(nwalk)])]
    pallas_call x10 -> x13, Pallas kernels: 5.69 us -> 5.9 us  [call(): pl.pallas_call(kernel, out_shape=outs, in_specs=[pl.BlockSpec(memory_spac...]
  transfers between devices with their start and end apart: 16 -> 16, of which waited for: 5 -> 6; matrix products, arithmetic and copies ran while one was open for 0% -> 0% of each run, Pallas kernels for 6% -> 8%
where the time goes in v4:
time: 36.3 us; the launch traced here: 36.1 us
  starting transfers between devices  15.6 us (43%)
  waiting for transfers between devices  13.7 us (38%)
  Pallas kernels  5.9 us (16%)
  between operations  0.78 us (2%)
    ppermute x5, waiting for transfers between devices, turn(): return lax.ppermute(x, 'chol', pairs)  13.6 us
    ppermute x5, starting transfers between devices, turn(): return lax.ppermute(x, 'chol', pairs)  10.5 us
    pallas_call x13, Pallas kernels, call(): pl.pallas_call(kernel, out_shape=outs, in_specs=[pl.BlockSpec(memory_spac...  5.9 us
    ppermute x11, starting transfers between devices, swap(): return lax.ppermute(x, 'walk', [(i, i ^ flip) for i in range(nwalk)])  5.12 us
  transfers between devices with their start and end apart: 16, of which 6 were waited for; matrix products, arithmetic and copies ran while one was open for 0% of the time, Pallas kernels for 8%

profile of v4, /device:TPU:0, one launch (start us, length us, event | category | flops | bytes accessed | tf_op | source)
XLA Modules:
  0.0 36.1 jit_solution(11669073423385658473)
XLA Ops:
  0.6 0.0 copy-start.1
  0.6 1.3 %shard_map.59.refs_0_ = bf16[200,512]{1,0:T(8,128)(2,1)S(1)} custom-call(s32[1,100]{1,0:T(1,128)} %bitcast.4, bf16[100,1000]{1,0:T(8,128)(2,1)} %bitcast.3), custom_call_target="tpu_custom_call" | custom-call | tf_op jit(solution)/shard_map/pallas_call | solution.py:238
  2.0 0.0 copy-start
  2.0 4.1 %collective-permute-start = (bf16[200,512]{1,0:T(8,128)(2,1)S(1)}, bf16[200,512]{1,0:T(8,128)(2,1)S(1)}, u32[]{:S(2)}, u32[]{:S(2)}) collective-permute-start(bf16[200,512]{1,0:T(8,128)(2,1)S(1)} %shard_map.59.refs_0_), channel_id=1, source_target_pairs={{0,8},{8,12},{12,4},{4,0},{1,9},{9,13},{13,5},{5,1},{2,10},{10,14}... | collective-permute-start | bytes 614408 | tf_op jit(solution)/shard_map/ppermute | solution.py:261
  6.1 0.0 copy-done.1
  6.1 0.1 copy.8.chol_ref.own_ref
  6.2 1.6 %collective-permute-start.4 = (bf16[8,100,250]{2,1,0:T(8,128)(2,1)S(1)}, bf16[8,100,250]{2,1,0:T(8,128)(2,1)S(1)}, u32[]{:S(2)}, u32[]{:S(2)}) collective-permute-start(bf16[8,100,250]{2,1,0:T(8,128)(2,1)S(1)} %copy.8.chol_ref.own_ref), channel_id=1, source_target_pairs={{0,2},{1,3},{2,0},{3,1},{4,6},{5,7},{6,4},{7,5},{8,10},{9,11},{10,... | collective-permute-start | bytes 1200008 | tf_op jit(solution)/shard_map/ppermute | solution.py:258
  7.7 0.0 collective-permute-start.6
  7.7 0.0 copy-done
  7.7 0.1 shard_map.60
  7.8 0.0 collective-permute-start.3
  7.9 3.7 %collective-permute-done.in_ref.refs_1_ = bf16[200,512]{1,0:T(8,128)(2,1)S(1)} collective-permute-done((bf16[200,512]{1,0:T(8,128)(2,1)S(1)}, bf16[200,512]{1,0:T(8,128)(2,1)S(1)}, u32[]{:S(2)}, u32[]{:S(2)}) %collective-permute-start) | collective-permute-done | bytes 204832 | tf_op jit(solution)/shard_map/ppermute | solution.py:261
  11.6 3.4 %collective-permute-start.1 = (bf16[200,512]{1,0:T(8,128)(2,1)S(1)}, bf16[200,512]{1,0:T(8,128)(2,1)S(1)}, u32[]{:S(2)}, u32[]{:S(2)}) collective-permute-start(bf16[200,512]{1,0:T(8,128)(2,1)S(1)} %collective-permute-done.in_ref.refs_1_), channel_id=1, source_target_pairs={{0,8},{8,12},{12,4},{4,0},{1,9},{9,13},{13,5},{5,1},{2,10},{10,14}... | collective-permute-start | bytes 614408 | tf_op jit(solution)/shard_map/ppermute | solution.py:261
  15.0 0.1 collective-permute-start.7
  15.1 2.7 %collective-permute-done.6.in_ref.refs_2_ = bf16[200,512]{1,0:T(8,128)(2,1)S(1)} collective-permute-done((bf16[200,512]{1,0:T(8,128)(2,1)S(1)}, bf16[200,512]{1,0:T(8,128)(2,1)S(1)}, u32[]{:S(2)}, u32[]{:S(2)}) %collective-permute-start.6) | collective-permute-done | bytes 204832 | tf_op jit(solution)/shard_map/ppermute | solution.py:261
  17.8 0.1 collective-permute-start.8
  17.9 0.0 collective-permute-done.4.crossed_ref.same_ref
  18.0 0.6 %collective-permute-start.5 = (bf16[200,512]{1,0:T(8,128)(2,1)S(1)}, bf16[200,512]{1,0:T(8,128)(2,1)S(1)}, u32[]{:S(2)}, u32[]{:S(2)}) collective-permute-start(bf16[200,512]{1,0:T(8,128)(2,1)S(1)} %shard_map.61), channel_id=1, source_target_pairs={{0,1},{1,0},{2,3},{3,2},{4,5},{5,4},{6,7},{7,6},{8,9},{9,8},{10,11... | collective-permute-start | bytes 614408 | tf_op jit(solution)/shard_map/ppermute | solution.py:258
  18.5 2.1 %collective-permute-done.1.mine = bf16[200,512]{1,0:T(8,128)(2,1)S(1)} collective-permute-done((bf16[200,512]{1,0:T(8,128)(2,1)S(1)}, bf16[200,512]{1,0:T(8,128)(2,1)S(1)}, u32[]{:S(2)}, u32[]{:S(2)}) %collective-permute-start.1) | collective-permute-done | bytes 204832 | tf_op jit(solution)/shard_map/ppermute | solution.py:261
  20.6 0.0 collective-permute-start.2
  20.6 0.0 collective-permute-done.3.pair_ref.refs_3_
  20.6 0.0 collective-permute-done.5.other_ref
  20.6 0.2 shard_map.62
  20.9 0.0 collective-permute-done.7.refs_4_
  20.9 0.0 collective-permute-done.8.refs_5_
  20.9 1.9 %shard_map.65 = (f32[512,256]{1,0:T(8,128)S(1)}, f32[512,256]{1,0:T(8,128)S(1)}, f32[512,256]{1,0:T(8,128)S(1)}, f32[512,256]{1,0:T(8,128)S(1)}, f32[6,128]{1,0:T(8,128)S(1)}) custom-call(bf16[200,512]{1,0:T(8,128)(2,1)S(1)} %shard_map.59.refs_0_, bf16[200,512]{1,0:T(8,128)(2,1)S(1)} %collective-permute-done.in_ref.refs_1_, ...), custom_call_target="tpu_custom_call" | custom-call | tf_op jit(solution)/shard_map/pallas_call | solution.py:238
  22.8 0.0 collective-permute-done.2.theirs
  22.8 0.7 %shard_map.66 = (bf16[400,256]{1,0:T(8,128)(2,1)S(1)}, bf16[400,256]{1,0:T(8,128)(2,1)S(1)}, f32[256,512]{1,0:T(8,128)S(1)}, bf16[256,1024]{1,0:T(8,128)(2,1)S(1)}, bf16[512,256]{1,0:T(8,128)(2,1)S(1)}) custom-call(bf16[200,512]{1,0:T(8,128)(2,1)S(1)} %collective-permute-done.1.mine, bf16[200,512]{1,0:T(8,128)(2,1)S(1)} %collective-permute-done.2.theirs, ...), custom_call_target="tpu_custom_call" | custom-call | tf_op jit(solution)/shard_map/pallas_call | solution.py:238
  23.5 1.5 %collective-permute-start.9 = (bf16[400,256]{1,0:T(8,128)(2,1)S(1)}, bf16[400,256]{1,0:T(8,128)(2,1)S(1)}, u32[]{:S(2)}, u32[]{:S(2)}) collective-permute-start(bf16[400,256]{1,0:T(8,128)(2,1)S(1)} %get-tuple-element.32), channel_id=1, source_target_pairs={{0,2},{1,3},{2,0},{3,1},{4,6},{5,7},{6,4},{7,5},{8,10},{9,11},{10,... | collective-permute-start | bytes 614408 | tf_op jit(solution)/shard_map/ppermute | solution.py:258
  25.1 0.4 %collective-permute-start.10 = (bf16[400,256]{1,0:T(8,128)(2,1)S(1)}, bf16[400,256]{1,0:T(8,128)(2,1)S(1)}, u32[]{:S(2)}, u32[]{:S(2)}) collective-permute-start(bf16[400,256]{1,0:T(8,128)(2,1)S(1)} %get-tuple-element.33), channel_id=1, source_target_pairs={{0,3},{1,2},{2,1},{3,0},{4,7},{5,6},{6,5},{7,4},{8,11},{9,10},{10,... | collective-permute-start | bytes 614408 | tf_op jit(solution)/shard_map/ppermute | solution.py:258
  25.4 0.2 shard_map.68.mine_ref
  25.6 0.4 %collective-permute-start.13 = (f32[2,96,128]{2,1,0:T(8,128)S(1)}, f32[2,96,128]{2,1,0:T(8,128)S(1)}, u32[]{:S(2)}, u32[]{:S(2)}) collective-permute-start(f32[2,96,128]{2,1,0:T(8,128)S(1)} %shard_map.68.mine_ref), channel_id=1, source_target_pairs={{0,1},{1,0},{2,3},{3,2},{4,5},{5,4},{6,7},{7,6},{8,9},{9,8},{10,11... | collective-permute-start | bytes 294920 | tf_op jit(solution)/shard_map/ppermute | solution.py:258
  26.0 0.3 shard_map.67
  26.3 0.3 collective-permute-start.11
  26.6 0.3 collective-permute-start.12
  26.9 0.1 collective-permute-done.13.arrived_ref
  27.0 1.0 %collective-permute-start.14 = (f32[2,128]{1,0:T(2,128)S(1)}, f32[2,128]{1,0:T(2,128)S(1)}, u32[]{:S(2)}, u32[]{:S(2)}) collective-permute-start(f32[2,128]{1,0:T(2,128)S(1)} %get-tuple-element.39), channel_id=1, source_target_pairs={{0,4},{4,0},{8,12},{12,8},{1,5},{5,1},{9,13},{13,9},{2,6},{6,2},{1... | collective-permute-start | bytes 3080 | tf_op jit(solution)/shard_map/ppermute | solution.py:261
  28.0 2.6 %collective-permute-done.14.arrived_ref = f32[2,128]{1,0:T(2,128)S(1)} collective-permute-done((f32[2,128]{1,0:T(2,128)S(1)}, f32[2,128]{1,0:T(2,128)S(1)}, u32[]{:S(2)}, u32[]{:S(2)}) %collective-permute-start.14) | collective-permute-done | bytes 1056 | tf_op jit(solution)/shard_map/ppermute | solution.py:261
  30.6 2.0 %collective-permute-start.15 = (f32[1,128]{1,0:T(1,128)S(1)}, f32[1,128]{1,0:T(1,128)S(1)}, u32[]{:S(2)}, u32[]{:S(2)}) collective-permute-start(f32[1,128]{1,0:T(1,128)S(1)} %get-tuple-element.41), channel_id=1, source_target_pairs={{0,8},{4,12},{8,0},{12,4},{1,9},{5,13},{9,1},{13,5},{2,10},{6,14},... | collective-permute-start | bytes 1544 | tf_op jit(solution)/shard_map/ppermute | solution.py:261
  32.6 2.4 %collective-permute-done.15.refs_6_ = f32[1,128]{1,0:T(1,128)S(1)} collective-permute-done((f32[1,128]{1,0:T(1,128)S(1)}, f32[1,128]{1,0:T(1,128)S(1)}, u32[]{:S(2)}, u32[]{:S(2)}) %collective-permute-start.15) | collective-permute-done | bytes 544 | tf_op jit(solution)/shard_map/ppermute | solution.py:261
  35.0 0.0 collective-permute-done.11.refs_3_
  35.0 0.0 collective-permute-done.12.refs_4_
  35.0 0.0 collective-permute-done.9.refs_1_
  35.0 0.0 collective-permute-done.10.refs_2_
  35.0 1.0 %shard_map.71 = (f32[100,8,250]{2,1,0:T(8,128)}, f32[1,1]{1,0:T(1,128)}) custom-call(f32[4,104,256]{2,1,0:T(8,128)S(1)} %get-tuple-element.31.refs_0_, bf16[400,256]{1,0:T(8,128)(2,1)S(1)} %collective-permute-done.9.refs_1_, bf16[400,256]{1,0:T(8,128)(2,1)S(1)} %collective-permute-done.10.refs_2_, bf16[200,250]{1,0:T(8,128)(2,1)S(1)} %collective-permute-done.11.refs_3_, ...), custom_call_target="tpu_custom_call" | custom-call | tf_op jit(solution)/shard_map/pallas_call | solution.py:238
  (5 shorter events, 0.1 us)
Async XLA Ops:
  0.6 5.5 %copy-start.1 = (bf16[8,100,250]{2,0,1:T(8,128)(2,1)S(1)}, bf16[8,100,250]{2,0,1:T(8,128)(2,1)}, u32[]{:S(2)}) copy-start(bf16[8,100,250]{2,0,1:T(8,128)(2,1)} %param.4) | copy-start | bytes 1200004
  2.0 5.7 %copy-start = (s32[1,4]{1,0:T(1,128)S(1)}, s32[1,4]{1,0:T(1,128)}, u32[]{:S(2)}) copy-start(s32[1,4]{1,0:T(1,128)} %code_ref.3) | copy-start | bytes 52
  2.0 9.6 %collective-permute-start = (bf16[200,512]{1,0:T(8,128)(2,1)S(1)}, bf16[200,512]{1,0:T(8,128)(2,1)S(1)}, u32[]{:S(2)}, u32[]{:S(2)}) collective-permute-start(bf16[200,512]{1,0:T(8,128)(2,1)S(1)} %shard_map.59.refs_0_), channel_id=1, source_target_pairs={{0,8},{8,12},{12,4},{4,0},{1,9},{9,13},{13,5},{5,1},{2,10},{10,14}... | collective-permute-start | bytes 614408 | tf_op jit(solution)/shard_map/ppermute | solution.py:261
  6.2 11.8 %collective-permute-start.4 = (bf16[8,100,250]{2,1,0:T(8,128)(2,1)S(1)}, bf16[8,100,250]{2,1,0:T(8,128)(2,1)S(1)}, u32[]{:S(2)}, u32[]{:S(2)}) collective-permute-start(bf16[8,100,250]{2,1,0:T(8,128)(2,1)S(1)} %copy.8.chol_ref.own_ref), channel_id=1, source_target_pairs={{0,2},{1,3},{2,0},{3,1},{4,6},{5,7},{6,4},{7,5},{8,10},{9,11},{10,... | collective-permute-start | bytes 1200008 | tf_op jit(solution)/shard_map/ppermute | solution.py:258
  7.7 10.1 %collective-permute-start.6 = (bf16[200,512]{1,0:T(8,128)(2,1)S(1)}, bf16[200,512]{1,0:T(8,128)(2,1)S(1)}, u32[]{:S(2)}, u32[]{:S(2)}) collective-permute-start(bf16[200,512]{1,0:T(8,128)(2,1)S(1)} %shard_map.59.refs_0_), channel_id=1, source_target_pairs={{8,0},{12,8},{4,12},{0,4},{9,1},{13,9},{5,13},{1,5},{10,2},{14,10}... | collective-permute-start | bytes 614408 | tf_op jit(solution)/shard_map/ppermute | solution.py:261
  7.8 12.8 %collective-permute-start.3 = (bf16[2,200,512]{2,1,0:T(8,128)(2,1)S(1)}, bf16[2,200,512]{2,1,0:T(8,128)(2,1)S(1)}, u32[]{:S(2)}, u32[]{:S(2)}) collective-permute-start(bf16[2,200,512]{2,1,0:T(8,128)(2,1)S(1)} %shard_map.60), channel_id=1, source_target_pairs={{0,1},{1,0},{2,3},{3,2},{4,5},{5,4},{6,7},{7,6},{8,9},{9,8},{10,11... | collective-permute-start | bytes 1228808 | tf_op jit(solution)/shard_map/ppermute | solution.py:258
  11.6 9.0 %collective-permute-start.1 = (bf16[200,512]{1,0:T(8,128)(2,1)S(1)}, bf16[200,512]{1,0:T(8,128)(2,1)S(1)}, u32[]{:S(2)}, u32[]{:S(2)}) collective-permute-start(bf16[200,512]{1,0:T(8,128)(2,1)S(1)} %collective-permute-done.in_ref.refs_1_), channel_id=1, source_target_pairs={{0,8},{8,12},{12,4},{4,0},{1,9},{9,13},{13,5},{5,1},{2,10},{10,14}... | collective-permute-start | bytes 614408 | tf_op jit(solution)/shard_map/ppermute | solution.py:261
  15.0 5.9 %collective-permute-start.7 = (bf16[208,512]{1,0:T(8,128)(2,1)S(1)}, bf16[208,512]{1,0:T(8,128)(2,1)S(1)}, u32[]{:S(2)}, u32[]{:S(2)}) collective-permute-start(bf16[208,512]{1,0:T(8,128)(2,1)S(1)} %shard_map.63), channel_id=1, source_target_pairs={{0,1},{1,0},{2,3},{3,2},{4,5},{5,4},{6,7},{7,6},{8,9},{9,8},{10,11... | collective-permute-start | bytes 638984 | tf_op jit(solution)/shard_map/ppermute | solution.py:258
  17.8 3.0 %collective-permute-start.8 = (bf16[208,512]{1,0:T(8,128)(2,1)S(1)}, bf16[208,512]{1,0:T(8,128)(2,1)S(1)}, u32[]{:S(2)}, u32[]{:S(2)}) collective-permute-start(bf16[208,512]{1,0:T(8,128)(2,1)S(1)} %shard_map.64), channel_id=1, source_target_pairs={{0,1},{1,0},{2,3},{3,2},{4,5},{5,4},{6,7},{7,6},{8,9},{9,8},{10,11... | collective-permute-start | bytes 638984 | tf_op jit(solution)/shard_map/ppermute | solution.py:258
  18.0 2.7 %collective-permute-start.5 = (bf16[200,512]{1,0:T(8,128)(2,1)S(1)}, bf16[200,512]{1,0:T(8,128)(2,1)S(1)}, u32[]{:S(2)}, u32[]{:S(2)}) collective-permute-start(bf16[200,512]{1,0:T(8,128)(2,1)S(1)} %shard_map.61), channel_id=1, source_target_pairs={{0,1},{1,0},{2,3},{3,2},{4,5},{5,4},{6,7},{7,6},{8,9},{9,8},{10,11... | collective-permute-start | bytes 614408 | tf_op jit(solution)/shard_map/ppermute | solution.py:258
  20.6 2.1 %collective-permute-start.2 = (bf16[200,512]{1,0:T(8,128)(2,1)S(1)}, bf16[200,512]{1,0:T(8,128)(2,1)S(1)}, u32[]{:S(2)}, u32[]{:S(2)}) collective-permute-start(bf16[200,512]{1,0:T(8,128)(2,1)S(1)} %collective-permute-done.1.mine), channel_id=1, source_target_pairs={{0,1},{1,0},{2,3},{3,2},{4,5},{5,4},{6,7},{7,6},{8,9},{9,8},{10,11... | collective-permute-start | bytes 614408 | tf_op jit(solution)/shard_map/ppermute | solution.py:258
  23.5 11.5 %collective-permute-start.9 = (bf16[400,256]{1,0:T(8,128)(2,1)S(1)}, bf16[400,256]{1,0:T(8,128)(2,1)S(1)}, u32[]{:S(2)}, u32[]{:S(2)}) collective-permute-start(bf16[400,256]{1,0:T(8,128)(2,1)S(1)} %get-tuple-element.32), channel_id=1, source_target_pairs={{0,2},{1,3},{2,0},{3,1},{4,6},{5,7},{6,4},{7,5},{8,10},{9,11},{10,... | collective-permute-start | bytes 614408 | tf_op jit(solution)/shard_map/ppermute | solution.py:258
  25.1 10.0 %collective-permute-start.10 = (bf16[400,256]{1,0:T(8,128)(2,1)S(1)}, bf16[400,256]{1,0:T(8,128)(2,1)S(1)}, u32[]{:S(2)}, u32[]{:S(2)}) collective-permute-start(bf16[400,256]{1,0:T(8,128)(2,1)S(1)} %get-tuple-element.33), channel_id=1, source_target_pairs={{0,3},{1,2},{2,1},{3,0},{4,7},{5,6},{6,5},{7,4},{8,11},{9,10},{10,... | collective-permute-start | bytes 614408 | tf_op jit(solution)/shard_map/ppermute | solution.py:258
  25.6 1.4 %collective-permute-start.13 = (f32[2,96,128]{2,1,0:T(8,128)S(1)}, f32[2,96,128]{2,1,0:T(8,128)S(1)}, u32[]{:S(2)}, u32[]{:S(2)}) collective-permute-start(f32[2,96,128]{2,1,0:T(8,128)S(1)} %shard_map.68.mine_ref), channel_id=1, source_target_pairs={{0,1},{1,0},{2,3},{3,2},{4,5},{5,4},{6,7},{7,6},{8,9},{9,8},{10,11... | collective-permute-start | bytes 294920 | tf_op jit(solution)/shard_map/ppermute | solution.py:258
  26.3 8.7 %collective-permute-start.11 = (bf16[200,250]{1,0:T(8,128)(2,1)S(1)}, bf16[200,250]{1,0:T(8,128)(2,1)S(1)}, u32[]{:S(2)}, u32[]{:S(2)}) collective-permute-start(bf16[200,250]{1,0:T(8,128)(2,1)S(1)} %get-tuple-element.34), channel_id=1, source_target_pairs={{0,1},{1,0},{2,3},{3,2},{4,5},{5,4},{6,7},{7,6},{8,9},{9,8},{10,11... | collective-permute-start | bytes 300008 | tf_op jit(solution)/shard_map/ppermute | solution.py:258
  26.6 8.4 %collective-permute-start.12 = (bf16[200,250]{1,0:T(8,128)(2,1)S(1)}, bf16[200,250]{1,0:T(8,128)(2,1)S(1)}, u32[]{:S(2)}, u32[]{:S(2)}) collective-permute-start(bf16[200,250]{1,0:T(8,128)(2,1)S(1)} %get-tuple-element.35), channel_id=1, source_target_pairs={{0,1},{1,0},{2,3},{3,2},{4,5},{5,4},{6,7},{7,6},{8,9},{9,8},{10,11... | collective-permute-start | bytes 300008 | tf_op jit(solution)/shard_map/ppermute | solution.py:258
  27.0 3.6 %collective-permute-start.14 = (f32[2,128]{1,0:T(2,128)S(1)}, f32[2,128]{1,0:T(2,128)S(1)}, u32[]{:S(2)}, u32[]{:S(2)}) collective-permute-start(f32[2,128]{1,0:T(2,128)S(1)} %get-tuple-element.39), channel_id=1, source_target_pairs={{0,4},{4,0},{8,12},{12,8},{1,5},{5,1},{9,13},{13,9},{2,6},{6,2},{1... | collective-permute-start | bytes 3080 | tf_op jit(solution)/shard_map/ppermute | solution.py:261
  30.6 4.4 %collective-permute-start.15 = (f32[1,128]{1,0:T(1,128)S(1)}, f32[1,128]{1,0:T(1,128)S(1)}, u32[]{:S(2)}, u32[]{:S(2)}) collective-permute-start(f32[1,128]{1,0:T(1,128)S(1)} %get-tuple-element.41), channel_id=1, source_target_pairs={{0,8},{4,12},{8,0},{12,4},{1,9},{5,13},{9,1},{13,5},{2,10},{6,14},... | collective-permute-start | bytes 1544 | tf_op jit(solution)/shard_map/ppermute | solution.py:261

commit v5 on v4

v5 whole, which is shorter than its diff:
```python
import functools

import jax
import jax.numpy as jnp
from jax import lax
from jax.experimental import pallas as pl
from jax.experimental.pallas import tpu as pltpu
from jax.sharding import PartitionSpec as P

LANES = 128
STEP = 32
HELD = 1
SPARE = 104
OPT = {'aw': 1, 'bw': 1, 'ar': 2, 'br': 4, 'rel': 0, 'hold': 1, 'c1r': 0}
GRANT = 16 * 1024 * 1024
PREP = 56 * 1024 * 1024
HBM = pltpu.MemorySpace.HBM
VMEM = pltpu.MemorySpace.VMEM
bf16, f32 = jnp.bfloat16, jnp.float32


def ceil_to(value, step):
    return -(-value // step) * step


def prep_theta(occ_hbm, green_hbm, chol_hbm, out_ref, chol_ref, occ_ref, green_ref, sems, *, width, padded):
    pairs = (green_hbm, green_ref), (occ_hbm, occ_ref), (chol_hbm, chol_ref)
    copies = [pltpu.make_async_copy(source, target, sems.at[i]) for i, (source, target) in enumerate(pairs)]
    for copy in copies:
        copy.start()
    out_ref[...] = jnp.zeros_like(out_ref)
    nocc, norb = green_ref.shape
    fold = norb // width // 2
    copies[1].wait()
    pick = (lax.broadcasted_iota(jnp.int32, (nocc, nocc), 0) == occ_ref[...]).astype(bf16)
    copies[0].wait()
    theta = lax.dot_general(pick, green_ref[...], (((0,), (0,)), ((), ())), preferred_element_type=f32)
    for k in range(norb // width):
        row, lane = k // fold * nocc, k % fold * padded
        out_ref[row:row + nocc, lane:lane + width] = theta[:, width * k:width * (k + 1)].astype(bf16)
    copies[2].wait()


def prep_chol(chol_ref, code_ref, cross_ref):
    gdev, nocc, width = chol_ref.shape
    padded = cross_ref.shape[1] // (gdev // 4)
    cross_ref[...] = jnp.zeros(cross_ref.shape, bf16)
    fold_half(chol_ref, cross_ref, 1 - lax.rem(lax.axis_index("walk"), 2), padded)
    nchol = code_ref.shape[1]
    shape = (ceil_to(nchol, 8), nchol)
    diagonal = lax.broadcasted_iota(jnp.int32, shape, 0) == lax.broadcasted_iota(jnp.int32, shape, 1)
    codes = jnp.sum(jnp.where(diagonal, code_ref[...], 0).astype(f32), axis=1, keepdims=True)
    lane = cross_ref.shape[1] - padded + width
    cross_ref[:shape[0], lane:lane + 1] = codes.astype(bf16)


def mail(*refs, width):
    *ins, out_ref = refs
    out_ref[...] = jnp.zeros_like(out_ref)
    for n, ref in enumerate(ins):
        rows, padded = ref.shape[0], ref.shape[1] // 2
        target = out_ref.at[n] if len(out_ref.shape) == 3 else out_ref
        span = target.shape[1] // 2
        for k in range(2):
            target[:rows, k * span:k * span + width] = ref[:, k * padded:k * padded + width]


def fold_half(chol_ref, out_ref, which, padded):
    gdev, nocc, width = chol_ref.shape
    half = gdev // 2
    for g in range(half):
        row, lane = g // (half // 2) * nocc, g % (half // 2) * padded
        out_ref[row:row + nocc, lane:lane + width] = chol_ref[which * half + g]


def relay(crossed_ref, out_ref):
    half = crossed_ref.shape[0] // 2
    h = lax.rem(lax.axis_index("walk"), 2)
    for g in range(half):
        out_ref[g] = crossed_ref[(1 - h) * half + g]


def source_of(me, path):
    return sum(jnp.where(me == i, s, 0) for i, s in enumerate(path))


def place_chol(
    own_ref, cross_ref, same_ref, other_ref, code_ref, out_ref, weight_ref, *, sources, half, nocc, width, padded
):
    out_ref[...] = jnp.zeros_like(out_ref)
    h = lax.rem(lax.axis_index("walk"), 2)
    for g in range(half):
        row, lane = g // (half // 2) * nocc, g % (half // 2) * padded
        rows = slice(g * LANES, g * LANES + nocc)
        for s, block in ((0, own_ref[h * half + g]), (2, same_ref[h * half + g]), (3, other_ref[g])):
            out_ref[rows, column(s, padded)] = jnp.pad(block, ((0, 0), (0, padded - width)))
        out_ref[rows, column(1, padded)] = cross_ref[row:row + nocc, lane:lane + padded]
    nchol = code_ref.shape[1]
    me = lax.axis_index("chol")
    lane = cross_ref.shape[1] - padded + width
    theirs = cross_ref[:ceil_to(nchol, 16), lane:lane + 1].astype(f32)
    mine = code_ref[...].astype(f32)
    codes = jnp.zeros(weight_ref.shape, f32)
    at = lax.broadcasted_iota(jnp.int32, codes.shape, 0)
    for n, path in enumerate(sources):
        source = source_of(me, path)
        for group, (values, axis) in enumerate(((mine, 1), (theirs, 0))):
            here = lax.broadcasted_iota(jnp.int32, values.shape, axis) == source
            code = jnp.sum(jnp.where(here, values, 0.0), axis=axis, keepdims=True)
            codes = jnp.where(at == group * nchol + n, code, codes)
    weight_ref[...] = -jnp.cos(jnp.pi * codes / 4.0)


def column(s, padded):
    return pl.ds(pl.multiple_of((lax.axis_index("walk") ^ s) * padded, padded), padded)


def place_theta(thetas, theta_s, nocc, width, padded):
    theta_s[...] = jnp.zeros_like(theta_s)
    for w, (ref, n) in enumerate(thetas):
        theta = ref[n] if len(ref.shape) == 3 else ref[...]
        span = theta.shape[1] // 2
        rows = slice(w * LANES, w * LANES + nocc)
        for i in range(2):
            part = theta[i * nocc:(i + 1) * nocc]
            if span == padded:
                theta_s[rows, 2 * i * padded:2 * (i + 1) * padded] = part
            else:
                for k in range(2):
                    lane = (2 * i + k) * padded
                    theta_s[rows, lane:lane + width] = part[:, k * span:k * span + width]


def first_walkers(*refs, first, counts, walkers, half, nocc, width, padded):
    counts = list(counts)
    *thetas, chol_s, weight_ref, same_ref, other_ref, tmat_ref, theta_s, cotan_s = refs
    place_theta([(ref, n) for ref in thetas for n in range(counts.pop(0))], theta_s, nocc, width, padded)
    tmat = lax.dot_general(theta_s[...], chol_s[...], (((1,), (1,)), ((), ())), preferred_element_type=f32)
    tmat_ref[...] = tmat
    n = walkers // 2
    for w in range(walkers):
        row = w // n * (weight_ref.shape[0] // 2) + first + w % n
        weight = weight_ref[row:row + 1, :]
        for g in range(half):
            block = tmat[w * LANES:(w + 1) * LANES, g * LANES:(g + 1) * LANES]
            cotan_s[g * LANES:(g + 1) * LANES, w * LANES:(w + 1) * LANES] = (weight * block).astype(bf16)
    for s, ref in ((2, same_ref), (3, other_ref)):
        ref[...] = jnp.dot(cotan_s[...], theta_s[:, column(s, padded)], preferred_element_type=f32)


def first_energies(tmat_ref, energy_ref, *, half):
    for w in range(energy_ref.shape[0]):
        total = jnp.zeros((LANES, LANES), f32)
        for g in range(half):
            block = tmat_ref[w * LANES:(w + 1) * LANES, g * LANES:(g + 1) * LANES]
            total += block * block.T
        energy_ref[w:w + 1, :] = -0.5 * jnp.sum(total, axis=0, keepdims=True)


def last_walkers(
    mine, theirs, chol_s, weight_ref, same_part, other_part, first_ref, same_ref, other_ref, energy_ref, theta_s, cotan_s,
    *, sources, half, nocc, width, padded
):
    place_theta([(mine, 0), (theirs, 0)], theta_s, nocc, width, padded)
    tmat = lax.dot_general(theta_s[...], chol_s[...], (((1,), (1,)), ((), ())), preferred_element_type=f32)
    for w in range(2):
        row = (w + 1) * (weight_ref.shape[0] // 2) - 1
        weight = weight_ref[row:row + 1, :]
        for g in range(half):
            block = tmat[w * LANES:(w + 1) * LANES, g * LANES:(g + 1) * LANES]
            cotan_s[g * LANES:(g + 1) * LANES, w * LANES:(w + 1) * LANES] = (weight * block).astype(bf16)
    for ref, part, s in ((same_ref, same_part, 2), (other_ref, other_part, 3)):
        grad = part[...] + jnp.dot(cotan_s[...], theta_s[:, column(s, padded)], preferred_element_type=f32)
        store_grad(grad, ref, half, nocc)
    energy_ref[...] = jnp.zeros_like(energy_ref)
    early = first_ref.shape[0] // 2
    me = lax.axis_index("chol")
    rows = [pl.ds(me ^ source_of(me, path), 1) for path in sources]
    for w in range(2):
        total = jnp.zeros((LANES, LANES), f32)
        for g in range(half):
            block = tmat[w * LANES:(w + 1) * LANES, g * LANES:(g + 1) * LANES]
            total += block * block.T
        for n in range(early):
            energy_ref[w, rows[n], :] = first_ref[w * early + n:w * early + n + 1]
        energy_ref[w, rows[early], :] = -0.5 * jnp.sum(total, axis=0, keepdims=True)


def store_grad(grad, ref, half, nocc):
    for g in range(half):
        if len(ref.shape) == 2:
            ref[g * nocc:(g + 1) * nocc] = grad[g * LANES:g * LANES + nocc, :ref.shape[1]].astype(ref.dtype)
        else:
            ref[g] = grad[g * LANES:g * LANES + ref.shape[1]].astype(ref.dtype)


def chip_walkers(*refs, half, nocc, padded):
    *factors, own_ref, low_ref, high_ref = refs
    for s in (1, 0):
        grad = 0.0
        for cotan_s, theta_s in zip(factors[::2], factors[1::2]):
            grad += jnp.dot(cotan_s[...], theta_s[:, column(s, padded)], preferred_element_type=f32)
        if s == 0:
            store_grad(grad, own_ref, half, nocc)
        else:
            store_grad(grad, low_ref, half // 2, nocc)
            store_grad(grad[half // 2 * LANES:], high_ref, half // 2, nocc)


def halve(mine_ref, arrived_ref, keep_ref, send_ref):
    ours, theirs = (ref.at[i] if len(ref.shape) == 3 else ref for i, ref in enumerate((mine_ref, arrived_ref)))
    for n in range(keep_ref.shape[0]):
        for ref, row in ((keep_ref, 2 * n), (send_ref, 2 * n + 1)):
            ref[n:n + 1, :] = ours[row:row + 1, :] + theirs[row:row + 1, :]


def finish(*refs):
    *refs, out_hbm, energy_hbm, out_ref, energy_ref, sems = refs
    own_ref, same_ref, other_ref, low_ref, high_ref, *energy_refs = refs
    half = own_ref.shape[0]
    nocc, gdev, width = out_ref.shape
    h = lax.rem(lax.axis_index("walk"), 2)
    energy = sum(ref[...] for ref in energy_refs)
    energy_ref[...] = jnp.sum(energy, axis=1, keepdims=True)
    copies = [pltpu.make_async_copy(energy_ref, energy_hbm, sems.at[0])]
    copies[0].start()

    def arrived(*refs):
        n = half // len(refs)
        blocks = [ref[g * nocc + start:g * nocc + stop, :width] for ref in refs for g in range(n)]
        return jnp.stack([block.astype(f32) for block in blocks])

    for n, start in enumerate(range(0, nocc, STEP), start=1):
        stop = min(start + STEP, nocc)
        mine = own_ref[:, start:stop, :width] + arrived(same_ref)
        theirs = arrived(low_ref, high_ref) + arrived(other_ref)

        @pl.when(h == 0)
        def _():
            out_ref[start:stop] = jnp.swapaxes(jnp.concatenate([mine, theirs], axis=0), 0, 1)

        @pl.when(h == 1)
        def _():
            out_ref[start:stop] = jnp.swapaxes(jnp.concatenate([theirs, mine], axis=0), 0, 1)

        copies.append(pltpu.make_async_copy(out_ref.at[start:stop], out_hbm.at[start:stop], sems.at[n]))
        copies[-1].start()
    for copy in copies:
        copy.wait()


def call(kernel, outs, *operands, scratch=(), ins=VMEM, out=VMEM, grant=GRANT):
    return pl.pallas_call(
        kernel,
        out_shape=outs,
        in_specs=[pl.BlockSpec(memory_space=ins)] * len(operands),
        out_specs=jax.tree.map(lambda _: pl.BlockSpec(memory_space=out), outs),
        scratch_shapes=scratch,
        compiler_params=pltpu.CompilerParams(vmem_limit_bytes=grant),
    )(*operands)


def body(chol_vectors, green_blocks, phase_codes, occupations, *, nchol, nwalk):
    gdev, nocc, width = chol_vectors.shape
    norb = green_blocks.shape[3]
    half = gdev // 2
    rows = ceil_to(nocc, 8)
    padded = ceil_to(width, LANES)
    wide = padded * nwalk
    sizes = dict(half=half, padded=padded)

    def swap(x, flip):
        return lax.ppermute(x, "walk", [(i, i ^ flip) for i in range(nwalk)])

    def turn(x, pairs):
        return lax.ppermute(x, "chol", pairs)

    def struct(*shape, dtype=bf16):
        return jax.ShapeDtypeStruct(shape, dtype)

    block = struct(2 * nocc, wide // 2)
    theta, chol_vectors = call(
        functools.partial(prep_theta, width=width, padded=padded),
        (pltpu.VMEM(block.shape, bf16), pltpu.VMEM((nocc, gdev, width), bf16)),
        occupations.reshape(1, nocc),
        green_blocks.reshape(nocc, norb),
        jnp.swapaxes(chol_vectors, 0, 1),
        scratch=[pltpu.VMEM((1, nocc), jnp.int32), pltpu.VMEM((nocc, norb), bf16), pltpu.SemaphoreType.DMA((3,))],
        ins=HBM,
        grant=PREP,
    )
    chol_vectors = jnp.swapaxes(chol_vectors, 0, 1)
    cross = call(prep_chol, struct(2 * nocc + OPT["c1r"], wide // 2), chol_vectors, phase_codes)

    if nchol == 4:
        there = [(0, 2), (2, 3), (3, 1), (1, 0)]
        back = [(b, a) for a, b in there]
        paths = [there, back, [(i, 3 - i) for i in range(4)]]
        first = turn(theta, there)
        early = [first, turn(theta, back)]
        last = turn(first, there)
    else:
        paths = [[(i, (i + d) % nchol) for i in range(nchol)] for d in range(1, nchol)]
        *early, last = [turn(theta, path) for path in paths]
    sources = [list(range(nchol))] + [[a for a, _ in sorted(path, key=lambda p: p[1])] for path in paths]

    paired = swap(cross, 1)
    crossed = swap(chol_vectors, 2)
    relayed = swap(call(relay, struct(half, nocc + OPT["rel"], width), crossed), 1)
    chol, weight = call(
        functools.partial(place_chol, sources=sources, nocc=nocc, width=width, **sizes),
        (struct(half * LANES, wide), struct(2 * nchol, LANES, dtype=f32)),
        chol_vectors,
        paired,
        crossed,
        relayed,
        phase_codes,
    )
    term = struct(half * LANES, padded, dtype=f32)
    mine = [theta] + early
    def message(extra, span, *blocks):
        shape = (2 * nocc + extra, 2 * span)
        return call(
            functools.partial(mail, width=width), struct(*shape) if len(blocks) == 1 else struct(2, *shape), *blocks
        )

    a_ops = [swap(message(OPT["ar"], width if OPT["aw"] else padded, theta, early[0]), 1)]
    b_op = message(OPT["br"], width if OPT["bw"] else padded, early[1])
    theirs = a_ops + [swap(b_op, 1)] + [swap(t, 1) for t in early[2:]]
    grads, energies, factors = None, [], []
    for start in range(0, nchol - 1, 3):
        if start == 0 and len(a_ops) == 1:
            group, counts = mine[:3] + theirs[:2], (1, 1, 1, 2, 1)
        else:
            shift = len(a_ops) - 2
            group = mine[start:start + 3] + theirs[start + shift:start + 3 + shift]
            counts = (1,) * len(group)
        walkers = sum(counts)
        *terms, tmat, theta_s, cotan_s = call(
            functools.partial(
                first_walkers, first=start, counts=counts, walkers=walkers, nocc=nocc, width=width, **sizes
            ),
            (
                term,
                term,
                struct(walkers * LANES, half * LANES, dtype=f32),
                struct(walkers * LANES, wide),
                struct(half * LANES, walkers * LANES),
            ),
            *group,
            chol,
            weight,
        )
        energy = call(functools.partial(first_energies, half=half), struct(walkers, LANES, dtype=f32), tmat)
        grads = terms if grads is None else [a + b for a, b in zip(grads, terms)]
        energies += [(energy[:walkers // 2], energy[walkers // 2:])]
        factors += [cotan_s, theta_s]
    if len(energies) > 1:
        energy = jnp.concatenate([e[i] for i in (0, 1) for e in energies])
    theirs_last = swap(lax.optimization_barrier((last, grads[0]))[0], 1)

    walkers = 2
    same, other, energy, theta_s, cotan_s = call(
        functools.partial(last_walkers, sources=sources, nocc=nocc, width=width, **sizes),
        (
            struct(half * nocc, padded),
            struct(half * nocc, padded),
            struct(2, nchol + SPARE, LANES, dtype=f32),
            struct(walkers * LANES, wide),
            struct(half * LANES, walkers * LANES),
        ),
        last,
        theirs_last,
        chol,
        weight,
        grads[0],
        grads[1],
        energy,
    )
    same, other = swap(same, 2), swap(other, 3)
    arrived, n, flip = swap(energy, 1), nchol // 2, 1
    while n:
        energy, send = call(halve, (struct(n, LANES, dtype=f32),) * 2, energy, arrived)
        arrived = turn(send, [(i, i ^ flip) for i in range(nchol)])
        if flip == HELD:
            theta_s, _ = lax.optimization_barrier((theta_s, arrived))
        n, flip = n // 2, flip * 2
    own, *core = call(
        functools.partial(chip_walkers, nocc=nocc, **sizes),
        (struct(half, rows, padded, dtype=f32),) + (struct(half // 2 * nocc, width),) * 2,
        *factors,
        cotan_s,
        theta_s,
    )
    core = [swap(c, 1) for c in core]
    chol_grad, energies = call(
        finish,
        (struct(nocc, gdev, width, dtype=f32), struct(1, 1, dtype=f32)),
        own,
        same,
        other,
        *core,
        energy,
        arrived,
        out=HBM,
        scratch=[
            pltpu.VMEM((nocc, gdev, width), f32),
            pltpu.VMEM((1, 1), f32),
            pltpu.SemaphoreType.DMA((1 - (-nocc // STEP),)),
        ],
    )
    return jnp.swapaxes(chol_grad, 0, 1), energies


def solution(mesh):
    placed = (
        P("chol", None, "walk"),
        P(("dom", "walk"), "chol", None, None),
        P(("dom", "walk"), None),
        P(("dom", "walk"), "chol", None),
    )
    return jax.shard_map(
        functools.partial(body, nchol=mesh.shape["chol"], nwalk=mesh.shape["walk"]),
        mesh=mesh,
        in_specs=placed,
        out_specs=(P(("dom", "chol"), None, "walk"), P(("dom", "walk"), "chol")),
        check_vma=False,
    )
```

time: 36.3 us -> 35.8 us (0.986)
  waiting for transfers between devices: 13.7 us -> 11.7 us
  starting transfers between devices: 15.6 us -> 16.7 us
  Pallas kernels: 5.9 us -> 6.33 us
    ppermute x5, waiting for transfers between devices: 13.6 us -> 8.58 us  [turn(): return lax.ppermute(x, 'chol', pairs)]
    ppermute x11, waiting for transfers between devices: 0.15 us -> 3.12 us  [swap(): return lax.ppermute(x, 'walk', [(i, i ^ flip) for i in range(nwalk)])]
    ppermute x5, starting transfers between devices: 10.5 us -> 11.9 us  [turn(): return lax.ppermute(x, 'chol', pairs)]
    pallas_call x13, Pallas kernels: 5.9 us -> 6.33 us  [call(): pl.pallas_call(kernel, out_shape=outs, in_specs=[pl.BlockSpec(memory_spac...]
  transfers between devices with their start and end apart: 16 -> 16, of which waited for: 6 -> 9; matrix products, arithmetic and copies ran while one was open for 0% -> 0% of each run, Pallas kernels for 8% -> 9%
where the time goes in v5:
time: 35.8 us; the launch traced here: 35.6 us
  starting transfers between devices  16.7 us (47%)
  waiting for transfers between devices  11.7 us (33%)
  Pallas kernels  6.33 us (18%)
  between operations  0.77 us (2%)
    ppermute x5, starting transfers between devices, turn(): return lax.ppermute(x, 'chol', pairs)  11.9 us
    ppermute x5, waiting for transfers between devices, turn(): return lax.ppermute(x, 'chol', pairs)  8.58 us
    pallas_call x13, Pallas kernels, call(): pl.pallas_call(kernel, out_shape=outs, in_specs=[pl.BlockSpec(memory_spac...  6.33 us
    ppermute x11, starting transfers between devices, swap(): return lax.ppermute(x, 'walk', [(i, i ^ flip) for i in range(nwalk)])  4.83 us
    ppermute x11, waiting for transfers between devices, swap(): return lax.ppermute(x, 'walk', [(i, i ^ flip) for i in range(nwalk)])  3.12 us
  transfers between devices with their start and end apart: 16, of which 9 were waited for; matrix products, arithmetic and copies ran while one was open for 0% of the time, Pallas kernels for 9%

profile of v5, /device:TPU:0, one launch (start us, length us, event | category | flops | bytes accessed | tf_op | source)
XLA Modules:
  0.0 35.6 jit_solution(11613463935559391492)
XLA Ops:
  0.6 0.0 copy-start
  0.6 1.3 %shard_map.59 = (bf16[200,512]{1,0:T(8,128)(2,1)S(1)}, bf16[100,8,250]{2,1,0:T(8,128)(2,1)S(1)}) custom-call(s32[1,100]{1,0:T(1,128)} %bitcast.12, bf16[100,1000]{1,0:T(8,128)(2,1)} %bitcast.11, bf16[100,8,250]{2,1,0:T(8,128)(2,1)} %bitcast.10), custom_call_target="tpu_custom_call" | custom-call | tf_op jit(solution)/shard_map/pallas_call | solution.py:253
  2.0 4.1 %collective-permute-start = (bf16[200,512]{1,0:T(8,128)(2,1)S(1)}, bf16[200,512]{1,0:T(8,128)(2,1)S(1)}, u32[]{:S(2)}, u32[]{:S(2)}) collective-permute-start(bf16[200,512]{1,0:T(8,128)(2,1)S(1)} %get-tuple-element.27.refs_0_), channel_id=1, source_target_pairs={{0,8},{8,12},{12,4},{4,0},{1,9},{9,13},{13,5},{5,1},{2,10},{10,14}... | collective-permute-start | bytes 614408 | tf_op jit(solution)/shard_map/ppermute | solution.py:276
  6.0 0.1 copy.8
  6.1 1.6 %collective-permute-start.5 = (bf16[8,100,250]{2,1,0:T(8,128)(2,1)S(1)}, bf16[8,100,250]{2,1,0:T(8,128)(2,1)S(1)}, u32[]{:S(2)}, u32[]{:S(2)}) collective-permute-start(bf16[8,100,250]{2,1,0:T(8,128)(2,1)S(1)} %bitcast.7), channel_id=1, source_target_pairs={{0,2},{1,3},{2,0},{3,1},{4,6},{5,7},{6,4},{7,5},{8,10},{9,11},{10,... | collective-permute-start | bytes 1200008 | tf_op jit(solution)/shard_map/ppermute | solution.py:273
  7.7 0.0 collective-permute-start.1
  7.7 3.9 %collective-permute-done.refs_1_ = bf16[200,512]{1,0:T(8,128)(2,1)S(1)} collective-permute-done((bf16[200,512]{1,0:T(8,128)(2,1)S(1)}, bf16[200,512]{1,0:T(8,128)(2,1)S(1)}, u32[]{:S(2)}, u32[]{:S(2)}) %collective-permute-start) | collective-permute-done | bytes 204832 | tf_op jit(solution)/shard_map/ppermute | solution.py:276
  11.6 0.1 shard_map.60
  11.7 0.1 collective-permute-start.2
  11.8 0.0 copy-done
  11.8 0.1 shard_map.62
  11.9 0.5 %collective-permute-start.4 = (bf16[200,512]{1,0:T(8,128)(2,1)S(1)}, bf16[200,512]{1,0:T(8,128)(2,1)S(1)}, u32[]{:S(2)}, u32[]{:S(2)}) collective-permute-start(bf16[200,512]{1,0:T(8,128)(2,1)S(1)} %shard_map.62), channel_id=1, source_target_pairs={{0,1},{1,0},{2,3},{3,2},{4,5},{5,4},{6,7},{7,6},{8,9},{9,8},{10,11... | collective-permute-start | bytes 614408 | tf_op jit(solution)/shard_map/ppermute | solution.py:273
  12.4 3.4 %collective-permute-start.7 = (bf16[200,512]{1,0:T(8,128)(2,1)S(1)}, bf16[200,512]{1,0:T(8,128)(2,1)S(1)}, u32[]{:S(2)}, u32[]{:S(2)}) collective-permute-start(bf16[200,512]{1,0:T(8,128)(2,1)S(1)} %collective-permute-done.refs_1_), channel_id=1, source_target_pairs={{0,8},{8,12},{12,4},{4,0},{1,9},{9,13},{13,5},{5,1},{2,10},{10,14}... | collective-permute-start | bytes 614408 | tf_op jit(solution)/shard_map/ppermute | solution.py:276
  15.8 0.9 %collective-permute-done.1.refs_0_.refs_2_ = bf16[200,512]{1,0:T(8,128)(2,1)S(1)} collective-permute-done((bf16[200,512]{1,0:T(8,128)(2,1)S(1)}, bf16[200,512]{1,0:T(8,128)(2,1)S(1)}, u32[]{:S(2)}, u32[]{:S(2)}) %collective-permute-start.1) | collective-permute-done | bytes 204832 | tf_op jit(solution)/shard_map/ppermute | solution.py:276
  16.7 0.1 shard_map.61
  16.8 0.1 collective-permute-start.3
  16.9 0.6 %collective-permute-done.5.crossed_ref.same_ref = bf16[8,100,250]{2,1,0:T(8,128)(2,1)S(1)} collective-permute-done((bf16[8,100,250]{2,1,0:T(8,128)(2,1)S(1)}, bf16[8,100,250]{2,1,0:T(8,128)(2,1)S(1)}, u32[]{:S(2)}, u32[]{:S(2)}) %collective-permute-start.5) | collective-permute-done | bytes 400032 | tf_op jit(solution)/shard_map/ppermute | solution.py:273
  17.5 0.1 collective-permute-start.6
  17.6 0.0 collective-permute-done.4.cross_ref
  17.6 1.4 %collective-permute-done.6.other_ref = bf16[4,100,250]{2,1,0:T(8,128)(2,1)S(1)} collective-permute-done((bf16[4,100,250]{2,1,0:T(8,128)(2,1)S(1)}, bf16[4,100,250]{2,1,0:T(8,128)(2,1)S(1)}, u32[]{:S(2)}, u32[]{:S(2)}) %collective-permute-start.6) | collective-permute-done | bytes 200032 | tf_op jit(solution)/shard_map/ppermute | solution.py:273
  19.0 0.2 shard_map.64
  19.2 0.0 collective-permute-done.3.refs_4_
  19.3 0.0 collective-permute-done.2.refs_3_
  19.3 1.5 %shard_map.65 = (f32[512,256]{1,0:T(8,128)S(1)}, f32[512,256]{1,0:T(8,128)S(1)}, f32[768,512]{1,0:T(8,128)S(1)}, bf16[768,1024]{1,0:T(8,128)(2,1)S(1)}, bf16[512,768]{1,0:T(8,128)(2,1)S(1)}) custom-call(bf16[200,512]{1,0:T(8,128)(2,1)S(1)} %get-tuple-element.27.refs_0_, bf16[200,512]{1,0:T(8,128)(2,1)S(1)} %collective-permute-done.refs_1_, ...), custom_call_target="tpu_custom_call" | custom-call | tf_op jit(solution)/shard_map/pallas_call | solution.py:253
  20.7 0.2 collective-permute-done.7.mine
  21.0 0.1 collective-permute-start.8
  21.0 0.5 %shard_map.66.first_ref = f32[6,128]{1,0:T(8,128)S(1)} custom-call(f32[768,512]{1,0:T(8,128)S(1)} %get-tuple-element.36.tmat_ref), custom_call_target="tpu_custom_call" | custom-call | tf_op jit(solution)/shard_map/pallas_call | solution.py:253
  21.5 0.9 %collective-permute-done.8.theirs = bf16[200,512]{1,0:T(8,128)(2,1)S(1)} collective-permute-done((bf16[200,512]{1,0:T(8,128)(2,1)S(1)}, bf16[200,512]{1,0:T(8,128)(2,1)S(1)}, u32[]{:S(2)}, u32[]{:S(2)}) %collective-permute-start.8) | collective-permute-done | bytes 204832 | tf_op jit(solution)/shard_map/ppermute | solution.py:273
  22.4 0.7 %shard_map.67 = (bf16[400,256]{1,0:T(8,128)(2,1)S(1)}, bf16[400,256]{1,0:T(8,128)(2,1)S(1)}, f32[2,108,128]{2,1,0:T(8,128)S(1)}, bf16[256,1024]{1,0:T(8,128)(2,1)S(1)}, bf16[512,256]{1,0:T(8,128)(2,1)S(1)}) custom-call(bf16[200,512]{1,0:T(8,128)(2,1)S(1)} %collective-permute-done.7.mine, bf16[200,512]{1,0:T(8,128)(2,1)S(1)} %collective-permute-done.8.theirs, ...), custom_call_target="tpu_custom_call" | custom-call | tf_op jit(solution)/shard_map/pallas_call | solution.py:253
  23.2 0.2 collective-permute-start.9
  23.4 1.5 %collective-permute-start.11 = (bf16[400,256]{1,0:T(8,128)(2,1)S(1)}, bf16[400,256]{1,0:T(8,128)(2,1)S(1)}, u32[]{:S(2)}, u32[]{:S(2)}) collective-permute-start(bf16[400,256]{1,0:T(8,128)(2,1)S(1)} %get-tuple-element.43), channel_id=1, source_target_pairs={{0,2},{1,3},{2,0},{3,1},{4,6},{5,7},{6,4},{7,5},{8,10},{9,11},{10,... | collective-permute-start | bytes 614408 | tf_op jit(solution)/shard_map/ppermute | solution.py:273
  24.9 0.2 collective-permute-start.12
  25.1 0.0 collective-permute-done.9.arrived_ref
  25.1 1.7 %collective-permute-start.10 = (f32[2,128]{1,0:T(2,128)S(1)}, f32[2,128]{1,0:T(2,128)S(1)}, u32[]{:S(2)}, u32[]{:S(2)}) collective-permute-start(f32[2,128]{1,0:T(2,128)S(1)} %get-tuple-element.40), channel_id=1, source_target_pairs={{0,4},{4,0},{8,12},{12,8},{1,5},{5,1},{9,13},{13,9},{2,6},{6,2},{1... | collective-permute-start | bytes 3080 | tf_op jit(solution)/shard_map/ppermute | solution.py:276
  26.8 1.9 %collective-permute-done.10.arrived_ref = f32[2,128]{1,0:T(2,128)S(1)} collective-permute-done((f32[2,128]{1,0:T(2,128)S(1)}, f32[2,128]{1,0:T(2,128)S(1)}, u32[]{:S(2)}, u32[]{:S(2)}) %collective-permute-start.10) | collective-permute-done | bytes 1056 | tf_op jit(solution)/shard_map/ppermute | solution.py:276
  28.7 0.7 %shard_map.69 = (f32[4,104,256]{2,1,0:T(8,128)S(1)}, bf16[200,250]{1,0:T(8,128)(2,1)S(1)}, bf16[200,250]{1,0:T(8,128)(2,1)S(1)}) custom-call(bf16[512,768]{1,0:T(8,128)(2,1)S(1)} %get-tuple-element.31.refs_0_, bf16[768,1024]{1,0:T(8,128)(2,1)S(1)} %get-tuple-element.32.refs_1_, bf16[512,256]{1,0:T(8,128)(2,1)S(1)} %get-tuple-element.37.refs_2_, ...), custom_call_target="tpu_custom_call" | custom-call | tf_op jit(solution)/shard_map/pallas_call | solution.py:253
  29.4 0.1 collective-permute-start.13
  29.5 0.5 %collective-permute-start.14 = (bf16[200,250]{1,0:T(8,128)(2,1)S(1)}, bf16[200,250]{1,0:T(8,128)(2,1)S(1)}, u32[]{:S(2)}, u32[]{:S(2)}) collective-permute-start(bf16[200,250]{1,0:T(8,128)(2,1)S(1)} %get-tuple-element.46), channel_id=1, source_target_pairs={{0,1},{1,0},{2,3},{3,2},{4,5},{5,4},{6,7},{7,6},{8,9},{9,8},{10,11... | collective-permute-start | bytes 300008 | tf_op jit(solution)/shard_map/ppermute | solution.py:273
  30.0 2.7 %collective-permute-start.15 = (f32[1,128]{1,0:T(1,128)S(1)}, f32[1,128]{1,0:T(1,128)S(1)}, u32[]{:S(2)}, u32[]{:S(2)}) collective-permute-start(f32[1,128]{1,0:T(1,128)S(1)} %get-tuple-element.49), channel_id=1, source_target_pairs={{0,8},{4,12},{8,0},{12,4},{1,9},{5,13},{9,1},{13,5},{2,10},{6,14},... | collective-permute-start | bytes 1544 | tf_op jit(solution)/shard_map/ppermute | solution.py:276
  32.7 1.7 %collective-permute-done.15.refs_6_ = f32[1,128]{1,0:T(1,128)S(1)} collective-permute-done((f32[1,128]{1,0:T(1,128)S(1)}, f32[1,128]{1,0:T(1,128)S(1)}, u32[]{:S(2)}, u32[]{:S(2)}) %collective-permute-start.15) | collective-permute-done | bytes 544 | tf_op jit(solution)/shard_map/ppermute | solution.py:276
  34.4 0.0 collective-permute-done.11.refs_1_
  34.4 0.1 collective-permute-done.12.refs_2_
  34.6 0.0 collective-permute-done.13.refs_3_
  34.6 0.0 collective-permute-done.14.refs_4_
  34.6 1.1 %shard_map.71 = (f32[100,8,250]{2,1,0:T(8,128)}, f32[1,1]{1,0:T(1,128)}) custom-call(f32[4,104,256]{2,1,0:T(8,128)S(1)} %get-tuple-element.42.refs_0_, bf16[400,256]{1,0:T(8,128)(2,1)S(1)} %collective-permute-done.11.refs_1_, bf16[400,256]{1,0:T(8,128)(2,1)S(1)} %collective-permute-done.12.refs_2_, bf16[200,250]{1,0:T(8,128)(2,1)S(1)} %collective-permute-done.13.refs_3_, ...), custom_call_target="tpu_custom_call" | custom-call | tf_op jit(solution)/shard_map/pallas_call | solution.py:253
  (3 shorter events, 0.0 us)
Async XLA Ops:
  0.6 11.1 %copy-start = (s32[1,4]{1,0:T(1,128)S(1)}, s32[1,4]{1,0:T(1,128)}, u32[]{:S(2)}) copy-start(s32[1,4]{1,0:T(1,128)} %code_ref.3) | copy-start | bytes 52
  2.0 9.6 %collective-permute-start = (bf16[200,512]{1,0:T(8,128)(2,1)S(1)}, bf16[200,512]{1,0:T(8,128)(2,1)S(1)}, u32[]{:S(2)}, u32[]{:S(2)}) collective-permute-start(bf16[200,512]{1,0:T(8,128)(2,1)S(1)} %get-tuple-element.27.refs_0_), channel_id=1, source_target_pairs={{0,8},{8,12},{12,4},{4,0},{1,9},{9,13},{13,5},{5,1},{2,10},{10,14}... | collective-permute-start | bytes 614408 | tf_op jit(solution)/shard_map/ppermute | solution.py:276
  6.1 11.3 %collective-permute-start.5 = (bf16[8,100,250]{2,1,0:T(8,128)(2,1)S(1)}, bf16[8,100,250]{2,1,0:T(8,128)(2,1)S(1)}, u32[]{:S(2)}, u32[]{:S(2)}) collective-permute-start(bf16[8,100,250]{2,1,0:T(8,128)(2,1)S(1)} %bitcast.7), channel_id=1, source_target_pairs={{0,2},{1,3},{2,0},{3,1},{4,6},{5,7},{6,4},{7,5},{8,10},{9,11},{10,... | collective-permute-start | bytes 1200008 | tf_op jit(solution)/shard_map/ppermute | solution.py:273
  7.7 9.0 %collective-permute-start.1 = (bf16[200,512]{1,0:T(8,128)(2,1)S(1)}, bf16[200,512]{1,0:T(8,128)(2,1)S(1)}, u32[]{:S(2)}, u32[]{:S(2)}) collective-permute-start(bf16[200,512]{1,0:T(8,128)(2,1)S(1)} %get-tuple-element.27.refs_0_), channel_id=1, source_target_pairs={{8,0},{12,8},{4,12},{0,4},{9,1},{13,9},{5,13},{1,5},{10,2},{14,10}... | collective-permute-start | bytes 614408 | tf_op jit(solution)/shard_map/ppermute | solution.py:276
  11.7 7.6 %collective-permute-start.2 = (bf16[2,202,500]{2,1,0:T(8,128)(2,1)S(1)}, bf16[2,202,500]{2,1,0:T(8,128)(2,1)S(1)}, u32[]{:S(2)}, u32[]{:S(2)}) collective-permute-start(bf16[2,202,500]{2,1,0:T(8,128)(2,1)S(1)} %shard_map.60), channel_id=1, source_target_pairs={{0,1},{1,0},{2,3},{3,2},{4,5},{5,4},{6,7},{7,6},{8,9},{9,8},{10,11... | collective-permute-start | bytes 1212008 | tf_op jit(solution)/shard_map/ppermute | solution.py:273
  11.9 5.7 %collective-permute-start.4 = (bf16[200,512]{1,0:T(8,128)(2,1)S(1)}, bf16[200,512]{1,0:T(8,128)(2,1)S(1)}, u32[]{:S(2)}, u32[]{:S(2)}) collective-permute-start(bf16[200,512]{1,0:T(8,128)(2,1)S(1)} %shard_map.62), channel_id=1, source_target_pairs={{0,1},{1,0},{2,3},{3,2},{4,5},{5,4},{6,7},{7,6},{8,9},{9,8},{10,11... | collective-permute-start | bytes 614408 | tf_op jit(solution)/shard_map/ppermute | solution.py:273
  12.4 8.6 %collective-permute-start.7 = (bf16[200,512]{1,0:T(8,128)(2,1)S(1)}, bf16[200,512]{1,0:T(8,128)(2,1)S(1)}, u32[]{:S(2)}, u32[]{:S(2)}) collective-permute-start(bf16[200,512]{1,0:T(8,128)(2,1)S(1)} %collective-permute-done.refs_1_), channel_id=1, source_target_pairs={{0,8},{8,12},{12,4},{4,0},{1,9},{9,13},{13,5},{5,1},{2,10},{10,14}... | collective-permute-start | bytes 614408 | tf_op jit(solution)/shard_map/ppermute | solution.py:276
  16.8 2.5 %collective-permute-start.3 = (bf16[204,500]{1,0:T(8,128)(2,1)S(1)}, bf16[204,500]{1,0:T(8,128)(2,1)S(1)}, u32[]{:S(2)}, u32[]{:S(2)}) collective-permute-start(bf16[204,500]{1,0:T(8,128)(2,1)S(1)} %shard_map.61), channel_id=1, source_target_pairs={{0,1},{1,0},{2,3},{3,2},{4,5},{5,4},{6,7},{7,6},{8,9},{9,8},{10,11... | collective-permute-start | bytes 612008 | tf_op jit(solution)/shard_map/ppermute | solution.py:273
  17.5 1.5 %collective-permute-start.6 = (bf16[4,100,250]{2,1,0:T(8,128)(2,1)S(1)}, bf16[4,100,250]{2,1,0:T(8,128)(2,1)S(1)}, u32[]{:S(2)}, u32[]{:S(2)}) collective-permute-start(bf16[4,100,250]{2,1,0:T(8,128)(2,1)S(1)} %shard_map.63), channel_id=1, source_target_pairs={{0,1},{1,0},{2,3},{3,2},{4,5},{5,4},{6,7},{7,6},{8,9},{9,8},{10,11... | collective-permute-start | bytes 600008 | tf_op jit(solution)/shard_map/ppermute | solution.py:273
  21.0 1.5 %collective-permute-start.8 = (bf16[200,512]{1,0:T(8,128)(2,1)S(1)}, bf16[200,512]{1,0:T(8,128)(2,1)S(1)}, u32[]{:S(2)}, u32[]{:S(2)}) collective-permute-start(bf16[200,512]{1,0:T(8,128)(2,1)S(1)} %collective-permute-done.7.mine), channel_id=1, source_target_pairs={{0,1},{1,0},{2,3},{3,2},{4,5},{5,4},{6,7},{7,6},{8,9},{9,8},{10,11... | collective-permute-start | bytes 614408 | tf_op jit(solution)/shard_map/ppermute | solution.py:273
  23.2 1.9 %collective-permute-start.9 = (f32[2,108,128]{2,1,0:T(8,128)S(1)}, f32[2,108,128]{2,1,0:T(8,128)S(1)}, u32[]{:S(2)}, u32[]{:S(2)}) collective-permute-start(f32[2,108,128]{2,1,0:T(8,128)S(1)} %get-tuple-element.39.mine_ref), channel_id=1, source_target_pairs={{0,1},{1,0},{2,3},{3,2},{4,5},{5,4},{6,7},{7,6},{8,9},{9,8},{10,11... | collective-permute-start | bytes 331784 | tf_op jit(solution)/shard_map/ppermute | solution.py:273
  23.4 11.1 %collective-permute-start.11 = (bf16[400,256]{1,0:T(8,128)(2,1)S(1)}, bf16[400,256]{1,0:T(8,128)(2,1)S(1)}, u32[]{:S(2)}, u32[]{:S(2)}) collective-permute-start(bf16[400,256]{1,0:T(8,128)(2,1)S(1)} %get-tuple-element.43), channel_id=1, source_target_pairs={{0,2},{1,3},{2,0},{3,1},{4,6},{5,7},{6,4},{7,5},{8,10},{9,11},{10,... | collective-permute-start | bytes 614408 | tf_op jit(solution)/shard_map/ppermute | solution.py:273
  24.9 9.7 %collective-permute-start.12 = (bf16[400,256]{1,0:T(8,128)(2,1)S(1)}, bf16[400,256]{1,0:T(8,128)(2,1)S(1)}, u32[]{:S(2)}, u32[]{:S(2)}) collective-permute-start(bf16[400,256]{1,0:T(8,128)(2,1)S(1)} %get-tuple-element.44), channel_id=1, source_target_pairs={{0,3},{1,2},{2,1},{3,0},{4,7},{5,6},{6,5},{7,4},{8,11},{9,10},{10,... | collective-permute-start | bytes 614408 | tf_op jit(solution)/shard_map/ppermute | solution.py:273
  25.1 3.6 %collective-permute-start.10 = (f32[2,128]{1,0:T(2,128)S(1)}, f32[2,128]{1,0:T(2,128)S(1)}, u32[]{:S(2)}, u32[]{:S(2)}) collective-permute-start(f32[2,128]{1,0:T(2,128)S(1)} %get-tuple-element.40), channel_id=1, source_target_pairs={{0,4},{4,0},{8,12},{12,8},{1,5},{5,1},{9,13},{13,9},{2,6},{6,2},{1... | collective-permute-start | bytes 3080 | tf_op jit(solution)/shard_map/ppermute | solution.py:276
  29.4 5.2 %collective-permute-start.13 = (bf16[200,250]{1,0:T(8,128)(2,1)S(1)}, bf16[200,250]{1,0:T(8,128)(2,1)S(1)}, u32[]{:S(2)}, u32[]{:S(2)}) collective-permute-start(bf16[200,250]{1,0:T(8,128)(2,1)S(1)} %get-tuple-element.45), channel_id=1, source_target_pairs={{0,1},{1,0},{2,3},{3,2},{4,5},{5,4},{6,7},{7,6},{8,9},{9,8},{10,11... | collective-permute-start | bytes 300008 | tf_op jit(solution)/shard_map/ppermute | solution.py:273
  29.5 5.1 %collective-permute-start.14 = (bf16[200,250]{1,0:T(8,128)(2,1)S(1)}, bf16[200,250]{1,0:T(8,128)(2,1)S(1)}, u32[]{:S(2)}, u32[]{:S(2)}) collective-permute-start(bf16[200,250]{1,0:T(8,128)(2,1)S(1)} %get-tuple-element.46), channel_id=1, source_target_pairs={{0,1},{1,0},{2,3},{3,2},{4,5},{5,4},{6,7},{7,6},{8,9},{9,8},{10,11... | collective-permute-start | bytes 300008 | tf_op jit(solution)/shard_map/ppermute | solution.py:273
  30.0 4.4 %collective-permute-start.15 = (f32[1,128]{1,0:T(1,128)S(1)}, f32[1,128]{1,0:T(1,128)S(1)}, u32[]{:S(2)}, u32[]{:S(2)}) collective-permute-start(f32[1,128]{1,0:T(1,128)S(1)} %get-tuple-element.49), channel_id=1, source_target_pairs={{0,8},{4,12},{8,0},{12,4},{1,9},{5,13},{9,1},{13,5},{2,10},{6,14},... | collective-permute-start | bytes 1544 | tf_op jit(solution)/shard_map/ppermute | solution.py:276

commit v6 on v5

--- a/solution.py
+++ b/solution.py
@@ -32,9 +32,11 @@
     nocc, norb = green_ref.shape
     fold = norb // width // 2
     copies[1].wait()
-    pick = (lax.broadcasted_iota(jnp.int32, (nocc, nocc), 0) == occ_ref[...]).astype(bf16)
+    row, lane = (lax.broadcasted_iota(jnp.int32, (nocc, nocc), axis) for axis in (0, 1))
+    source = jnp.sum(jnp.where(row == lane, occ_ref[...], 0).astype(f32), axis=1, keepdims=True)
+    pick = (source == lane.astype(f32)).astype(bf16)
     copies[0].wait()
-    theta = lax.dot_general(pick, green_ref[...], (((0,), (0,)), ((), ())), preferred_element_type=f32)
+    theta = jnp.dot(pick, green_ref[...], preferred_element_type=f32)
     for k in range(norb // width):
         row, lane = k // fold * nocc, k % fold * padded
         out_ref[row:row + nocc, lane:lane + width] = theta[:, width * k:width * (k + 1)].astype(bf16)
@@ -43,15 +45,13 @@
 
 def prep_chol(chol_ref, code_ref, cross_ref):
     gdev, nocc, width = chol_ref.shape
-    padded = cross_ref.shape[1] // (gdev // 4)
-    cross_ref[...] = jnp.zeros(cross_ref.shape, bf16)
-    fold_half(chol_ref, cross_ref, 1 - lax.rem(lax.axis_index("walk"), 2), padded)
-    nchol = code_ref.shape[1]
-    shape = (ceil_to(nchol, 8), nchol)
-    diagonal = lax.broadcasted_iota(jnp.int32, shape, 0) == lax.broadcasted_iota(jnp.int32, shape, 1)
-    codes = jnp.sum(jnp.where(diagonal, code_ref[...], 0).astype(f32), axis=1, keepdims=True)
-    lane = cross_ref.shape[1] - padded + width
-    cross_ref[:shape[0], lane:lane + 1] = codes.astype(bf16)
+    half = gdev // 2
+    h = lax.rem(lax.axis_index("walk"), 2)
+    for g in range(half):
+        row, lane = g // (half // 2) * nocc, g % (half // 2) * width
+        cross_ref[row:row + nocc, lane:lane + width] = chol_ref[(1 - h) * half + g]
+    cross_ref[2 * nocc:, :] = jnp.zeros((1, cross_ref.shape[1]), bf16)
+    cross_ref[2 * nocc:, :code_ref.shape[1]] = code_ref[...].astype(f32).astype(bf16)
 
 
 def mail(*refs, width):
@@ -65,14 +65,6 @@
             target[:rows, k * span:k * span + width] = ref[:, k * padded:k * padded + width]
 
 
-def fold_half(chol_ref, out_ref, which, padded):
-    gdev, nocc, width = chol_ref.shape
-    half = gdev // 2
-    for g in range(half):
-        row, lane = g // (half // 2) * nocc, g % (half // 2) * padded
-        out_ref[row:row + nocc, lane:lane + width] = chol_ref[which * half + g]
-
-
 def relay(crossed_ref, out_ref):
     half = crossed_ref.shape[0] // 2
     h = lax.rem(lax.axis_index("walk"), 2)
@@ -90,23 +82,22 @@
     out_ref[...] = jnp.zeros_like(out_ref)
     h = lax.rem(lax.axis_index("walk"), 2)
     for g in range(half):
-        row, lane = g // (half // 2) * nocc, g % (half // 2) * padded
+        row, lane = g // (half // 2) * nocc, g % (half // 2) * width
         rows = slice(g * LANES, g * LANES + nocc)
-        for s, block in ((0, own_ref[h * half + g]), (2, same_ref[h * half + g]), (3, other_ref[g])):
+        crossed = cross_ref[row:row + nocc, lane:lane + width]
+        for s, block in enumerate((own_ref[h * half + g], crossed, same_ref[h * half + g], other_ref[g])):
             out_ref[rows, column(s, padded)] = jnp.pad(block, ((0, 0), (0, padded - width)))
-        out_ref[rows, column(1, padded)] = cross_ref[row:row + nocc, lane:lane + padded]
     nchol = code_ref.shape[1]
     me = lax.axis_index("chol")
-    lane = cross_ref.shape[1] - padded + width
-    theirs = cross_ref[:ceil_to(nchol, 16), lane:lane + 1].astype(f32)
     mine = code_ref[...].astype(f32)
+    theirs = cross_ref[2 * nocc:, :nchol].astype(f32)
     codes = jnp.zeros(weight_ref.shape, f32)
     at = lax.broadcasted_iota(jnp.int32, codes.shape, 0)
     for n, path in enumerate(sources):
         source = source_of(me, path)
-        for group, (values, axis) in enumerate(((mine, 1), (theirs, 0))):
-            here = lax.broadcasted_iota(jnp.int32, values.shape, axis) == source
-            code = jnp.sum(jnp.where(here, values, 0.0), axis=axis, keepdims=True)
+        for group, values in enumerate((mine, theirs)):
+            here = lax.broadcasted_iota(jnp.int32, values.shape, 1) == source
+            code = jnp.sum(jnp.where(here, values, 0.0), axis=1, keepdims=True)
             codes = jnp.where(at == group * nchol + n, code, codes)
     weight_ref[...] = -jnp.cos(jnp.pi * codes / 4.0)
 
@@ -290,7 +281,7 @@
         grant=PREP,
     )
     chol_vectors = jnp.swapaxes(chol_vectors, 0, 1)
-    cross = call(prep_chol, struct(2 * nocc + OPT["c1r"], wide // 2), chol_vectors, phase_codes)
+    cross = call(prep_chol, struct(2 * nocc + 1, half // 2 * width), chol_vectors, phase_codes)
 
     if nchol == 4:
         there = [(0, 2), (2, 3), (3, 1), (1, 0)]

time: 35.8 us -> 35.7 us (level)
    ppermute x11, waiting for transfers between devices: 3.12 us -> 2.25 us  [swap(): return lax.ppermute(x, 'walk', [(i, i ^ flip) for i in range(nwalk)])]
    ppermute x5, waiting for transfers between devices: 8.58 us -> 9.38 us  [turn(): return lax.ppermute(x, 'chol', pairs)]
  transfers between devices with their start and end apart: 16 -> 16, of which waited for: 9 -> 8; matrix products, arithmetic and copies ran while one was open for 0% -> 0% of each run, Pallas kernels for 9% -> 9%
where the time goes in v6:
time: 35.7 us; the launch traced here: 35.5 us
  starting transfers between devices  16.7 us (47%)
  waiting for transfers between devices  11.6 us (32%)
  Pallas kernels  6.39 us (18%)
  between operations  0.76 us (2%)
    ppermute x5, starting transfers between devices, turn(): return lax.ppermute(x, 'chol', pairs)  11.6 us
    ppermute x5, waiting for transfers between devices, turn(): return lax.ppermute(x, 'chol', pairs)  9.38 us
    pallas_call x13, Pallas kernels, call(): pl.pallas_call(kernel, out_shape=outs, in_specs=[pl.BlockSpec(memory_spac...  6.39 us
    ppermute x11, starting transfers between devices, swap(): return lax.ppermute(x, 'walk', [(i, i ^ flip) for i in range(nwalk)])  5.04 us
    ppermute x11, waiting for transfers between devices, swap(): return lax.ppermute(x, 'walk', [(i, i ^ flip) for i in range(nwalk)])  2.25 us
  transfers between devices with their start and end apart: 16, of which 8 were waited for; matrix products, arithmetic and copies ran while one was open for 0% of the time, Pallas kernels for 9%

profile of v6, /device:TPU:0, one launch (start us, length us, event | category | flops | bytes accessed | tf_op | source)
XLA Modules:
  0.0 35.5 jit_solution(5632828260592335340)
XLA Ops:
  0.6 0.0 copy-start
  0.6 1.3 %shard_map.59 = (bf16[200,512]{1,0:T(8,128)(2,1)S(1)}, bf16[100,8,250]{2,1,0:T(8,128)(2,1)S(1)}) custom-call(s32[1,100]{1,0:T(1,128)} %bitcast.12, bf16[100,1000]{1,0:T(8,128)(2,1)} %bitcast.11, bf16[100,8,250]{2,1,0:T(8,128)(2,1)} %bitcast.10), custom_call_target="tpu_custom_call" | custom-call | tf_op jit(solution)/shard_map/pallas_call | solution.py:244
  1.9 4.1 %collective-permute-start = (bf16[200,512]{1,0:T(8,128)(2,1)S(1)}, bf16[200,512]{1,0:T(8,128)(2,1)S(1)}, u32[]{:S(2)}, u32[]{:S(2)}) collective-permute-start(bf16[200,512]{1,0:T(8,128)(2,1)S(1)} %get-tuple-element.27.refs_0_), channel_id=1, source_target_pairs={{0,8},{8,12},{12,4},{4,0},{1,9},{9,13},{13,5},{5,1},{2,10},{10,14}... | collective-permute-start | bytes 614408 | tf_op jit(solution)/shard_map/ppermute | solution.py:267
  6.0 0.1 copy.8
  6.1 1.6 %collective-permute-start.5 = (bf16[8,100,250]{2,1,0:T(8,128)(2,1)S(1)}, bf16[8,100,250]{2,1,0:T(8,128)(2,1)S(1)}, u32[]{:S(2)}, u32[]{:S(2)}) collective-permute-start(bf16[8,100,250]{2,1,0:T(8,128)(2,1)S(1)} %bitcast.7), channel_id=1, source_target_pairs={{0,2},{1,3},{2,0},{3,1},{4,6},{5,7},{6,4},{7,5},{8,10},{9,11},{10,... | collective-permute-start | bytes 1200008 | tf_op jit(solution)/shard_map/ppermute | solution.py:264
  7.6 0.0 collective-permute-start.1
  7.6 3.9 %collective-permute-done.refs_1_ = bf16[200,512]{1,0:T(8,128)(2,1)S(1)} collective-permute-done((bf16[200,512]{1,0:T(8,128)(2,1)S(1)}, bf16[200,512]{1,0:T(8,128)(2,1)S(1)}, u32[]{:S(2)}, u32[]{:S(2)}) %collective-permute-start) | collective-permute-done | bytes 204832 | tf_op jit(solution)/shard_map/ppermute | solution.py:267
  11.5 0.1 shard_map.60
  11.6 0.1 collective-permute-start.2
  11.7 3.4 %collective-permute-start.7 = (bf16[200,512]{1,0:T(8,128)(2,1)S(1)}, bf16[200,512]{1,0:T(8,128)(2,1)S(1)}, u32[]{:S(2)}, u32[]{:S(2)}) collective-permute-start(bf16[200,512]{1,0:T(8,128)(2,1)S(1)} %collective-permute-done.refs_1_), channel_id=1, source_target_pairs={{0,8},{8,12},{12,4},{4,0},{1,9},{9,13},{13,5},{5,1},{2,10},{10,14}... | collective-permute-start | bytes 614408 | tf_op jit(solution)/shard_map/ppermute | solution.py:267
  15.2 1.5 %collective-permute-done.1.refs_0_.refs_2_ = bf16[200,512]{1,0:T(8,128)(2,1)S(1)} collective-permute-done((bf16[200,512]{1,0:T(8,128)(2,1)S(1)}, bf16[200,512]{1,0:T(8,128)(2,1)S(1)}, u32[]{:S(2)}, u32[]{:S(2)}) %collective-permute-start.1) | collective-permute-done | bytes 204832 | tf_op jit(solution)/shard_map/ppermute | solution.py:267
  16.6 0.1 shard_map.61
  16.7 0.1 collective-permute-start.3
  16.8 0.0 copy-done
  16.8 0.1 shard_map.62
  16.9 0.5 %collective-permute-start.4 = (bf16[201,500]{1,0:T(8,128)(2,1)S(1)}, bf16[201,500]{1,0:T(8,128)(2,1)S(1)}, u32[]{:S(2)}, u32[]{:S(2)}) collective-permute-start(bf16[201,500]{1,0:T(8,128)(2,1)S(1)} %shard_map.62), channel_id=1, source_target_pairs={{0,1},{1,0},{2,3},{3,2},{4,5},{5,4},{6,7},{7,6},{8,9},{9,8},{10,11... | collective-permute-start | bytes 603008 | tf_op jit(solution)/shard_map/ppermute | solution.py:264
  17.5 0.0 collective-permute-done.5.crossed_ref.same_ref
  17.5 0.1 collective-permute-start.6
  17.6 1.0 %collective-permute-done.4.cross_ref = bf16[201,500]{1,0:T(8,128)(2,1)S(1)} collective-permute-done((bf16[201,500]{1,0:T(8,128)(2,1)S(1)}, bf16[201,500]{1,0:T(8,128)(2,1)S(1)}, u32[]{:S(2)}, u32[]{:S(2)}) %collective-permute-start.4) | collective-permute-done | bytes 201032 | tf_op jit(solution)/shard_map/ppermute | solution.py:264
  18.6 0.5 %collective-permute-done.6.other_ref = bf16[4,100,250]{2,1,0:T(8,128)(2,1)S(1)} collective-permute-done((bf16[4,100,250]{2,1,0:T(8,128)(2,1)S(1)}, bf16[4,100,250]{2,1,0:T(8,128)(2,1)S(1)}, u32[]{:S(2)}, u32[]{:S(2)}) %collective-permute-start.6) | collective-permute-done | bytes 200032 | tf_op jit(solution)/shard_map/ppermute | solution.py:264
  19.0 0.3 shard_map.64
  19.3 0.0 collective-permute-done.3.refs_4_
  19.3 0.0 collective-permute-done.2.refs_3_
  19.4 1.5 %shard_map.65 = (f32[512,256]{1,0:T(8,128)S(1)}, f32[512,256]{1,0:T(8,128)S(1)}, f32[768,512]{1,0:T(8,128)S(1)}, bf16[768,1024]{1,0:T(8,128)(2,1)S(1)}, bf16[512,768]{1,0:T(8,128)(2,1)S(1)}) custom-call(bf16[200,512]{1,0:T(8,128)(2,1)S(1)} %get-tuple-element.27.refs_0_, bf16[200,512]{1,0:T(8,128)(2,1)S(1)} %collective-permute-done.refs_1_, ...), custom_call_target="tpu_custom_call" | custom-call | tf_op jit(solution)/shard_map/pallas_call | solution.py:244
  20.8 0.1 collective-permute-done.7.mine
  20.9 0.2 collective-permute-start.8
  21.1 0.5 %shard_map.66.first_ref = f32[6,128]{1,0:T(8,128)S(1)} custom-call(f32[768,512]{1,0:T(8,128)S(1)} %get-tuple-element.36.tmat_ref), custom_call_target="tpu_custom_call" | custom-call | tf_op jit(solution)/shard_map/pallas_call | solution.py:244
  21.6 0.8 %collective-permute-done.8.theirs = bf16[200,512]{1,0:T(8,128)(2,1)S(1)} collective-permute-done((bf16[200,512]{1,0:T(8,128)(2,1)S(1)}, bf16[200,512]{1,0:T(8,128)(2,1)S(1)}, u32[]{:S(2)}, u32[]{:S(2)}) %collective-permute-start.8) | collective-permute-done | bytes 204832 | tf_op jit(solution)/shard_map/ppermute | solution.py:264
  22.4 0.7 %shard_map.67 = (bf16[400,256]{1,0:T(8,128)(2,1)S(1)}, bf16[400,256]{1,0:T(8,128)(2,1)S(1)}, f32[2,108,128]{2,1,0:T(8,128)S(1)}, bf16[256,1024]{1,0:T(8,128)(2,1)S(1)}, bf16[512,256]{1,0:T(8,128)(2,1)S(1)}) custom-call(bf16[200,512]{1,0:T(8,128)(2,1)S(1)} %collective-permute-done.7.mine, bf16[200,512]{1,0:T(8,128)(2,1)S(1)} %collective-permute-done.8.theirs, ...), custom_call_target="tpu_custom_call" | custom-call | tf_op jit(solution)/shard_map/pallas_call | solution.py:244
  23.1 0.3 collective-permute-start.9
  23.4 1.5 %collective-permute-start.11 = (bf16[400,256]{1,0:T(8,128)(2,1)S(1)}, bf16[400,256]{1,0:T(8,128)(2,1)S(1)}, u32[]{:S(2)}, u32[]{:S(2)}) collective-permute-start(bf16[400,256]{1,0:T(8,128)(2,1)S(1)} %get-tuple-element.43), channel_id=1, source_target_pairs={{0,2},{1,3},{2,0},{3,1},{4,6},{5,7},{6,4},{7,5},{8,10},{9,11},{10,... | collective-permute-start | bytes 614408 | tf_op jit(solution)/shard_map/ppermute | solution.py:264
  24.9 0.2 collective-permute-start.12
  25.1 0.0 collective-permute-done.9.arrived_ref
  25.1 1.5 %collective-permute-start.10 = (f32[2,128]{1,0:T(2,128)S(1)}, f32[2,128]{1,0:T(2,128)S(1)}, u32[]{:S(2)}, u32[]{:S(2)}) collective-permute-start(f32[2,128]{1,0:T(2,128)S(1)} %get-tuple-element.40), channel_id=1, source_target_pairs={{0,4},{4,0},{8,12},{12,8},{1,5},{5,1},{9,13},{13,9},{2,6},{6,2},{1... | collective-permute-start | bytes 3080 | tf_op jit(solution)/shard_map/ppermute | solution.py:267
  26.6 2.1 %collective-permute-done.10.arrived_ref = f32[2,128]{1,0:T(2,128)S(1)} collective-permute-done((f32[2,128]{1,0:T(2,128)S(1)}, f32[2,128]{1,0:T(2,128)S(1)}, u32[]{:S(2)}, u32[]{:S(2)}) %collective-permute-start.10) | collective-permute-done | bytes 1056 | tf_op jit(solution)/shard_map/ppermute | solution.py:267
  28.6 0.7 %shard_map.69 = (f32[4,104,256]{2,1,0:T(8,128)S(1)}, bf16[200,250]{1,0:T(8,128)(2,1)S(1)}, bf16[200,250]{1,0:T(8,128)(2,1)S(1)}) custom-call(bf16[512,768]{1,0:T(8,128)(2,1)S(1)} %get-tuple-element.31.refs_0_, bf16[768,1024]{1,0:T(8,128)(2,1)S(1)} %get-tuple-element.32.refs_1_, bf16[512,256]{1,0:T(8,128)(2,1)S(1)} %get-tuple-element.37.refs_2_, ...), custom_call_target="tpu_custom_call" | custom-call | tf_op jit(solution)/shard_map/pallas_call | solution.py:244
  29.4 0.1 collective-permute-start.13
  29.5 0.5 %collective-permute-start.14 = (bf16[200,250]{1,0:T(8,128)(2,1)S(1)}, bf16[200,250]{1,0:T(8,128)(2,1)S(1)}, u32[]{:S(2)}, u32[]{:S(2)}) collective-permute-start(bf16[200,250]{1,0:T(8,128)(2,1)S(1)} %get-tuple-element.46), channel_id=1, source_target_pairs={{0,1},{1,0},{2,3},{3,2},{4,5},{5,4},{6,7},{7,6},{8,9},{9,8},{10,11... | collective-permute-start | bytes 300008 | tf_op jit(solution)/shard_map/ppermute | solution.py:264
  30.0 2.6 %collective-permute-start.15 = (f32[1,128]{1,0:T(1,128)S(1)}, f32[1,128]{1,0:T(1,128)S(1)}, u32[]{:S(2)}, u32[]{:S(2)}) collective-permute-start(f32[1,128]{1,0:T(1,128)S(1)} %get-tuple-element.49), channel_id=1, source_target_pairs={{0,8},{4,12},{8,0},{12,4},{1,9},{5,13},{9,1},{13,5},{2,10},{6,14},... | collective-permute-start | bytes 1544 | tf_op jit(solution)/shard_map/ppermute | solution.py:267
  32.5 1.9 %collective-permute-done.15.refs_6_ = f32[1,128]{1,0:T(1,128)S(1)} collective-permute-done((f32[1,128]{1,0:T(1,128)S(1)}, f32[1,128]{1,0:T(1,128)S(1)}, u32[]{:S(2)}, u32[]{:S(2)}) %collective-permute-start.15) | collective-permute-done | bytes 544 | tf_op jit(solution)/shard_map/ppermute | solution.py:267
  34.4 0.0 collective-permute-done.11.refs_1_
  34.4 0.0 collective-permute-done.12.refs_2_
  34.5 0.0 collective-permute-done.13.refs_3_
  34.5 0.0 collective-permute-done.14.refs_4_
  34.5 1.1 %shard_map.71 = (f32[100,8,250]{2,1,0:T(8,128)}, f32[1,1]{1,0:T(1,128)}) custom-call(f32[4,104,256]{2,1,0:T(8,128)S(1)} %get-tuple-element.42.refs_0_, bf16[400,256]{1,0:T(8,128)(2,1)S(1)} %collective-permute-done.11.refs_1_, bf16[400,256]{1,0:T(8,128)(2,1)S(1)} %collective-permute-done.12.refs_2_, bf16[200,250]{1,0:T(8,128)(2,1)S(1)} %collective-permute-done.13.refs_3_, ...), custom_call_target="tpu_custom_call" | custom-call | tf_op jit(solution)/shard_map/pallas_call | solution.py:244
  (3 shorter events, 0.0 us)
Async XLA Ops:
  0.6 16.2 %copy-start = (s32[1,4]{1,0:T(1,128)S(1)}, s32[1,4]{1,0:T(1,128)}, u32[]{:S(2)}) copy-start(s32[1,4]{1,0:T(1,128)} %code_ref.3) | copy-start | bytes 52
  1.9 9.6 %collective-permute-start = (bf16[200,512]{1,0:T(8,128)(2,1)S(1)}, bf16[200,512]{1,0:T(8,128)(2,1)S(1)}, u32[]{:S(2)}, u32[]{:S(2)}) collective-permute-start(bf16[200,512]{1,0:T(8,128)(2,1)S(1)} %get-tuple-element.27.refs_0_), channel_id=1, source_target_pairs={{0,8},{8,12},{12,4},{4,0},{1,9},{9,13},{13,5},{5,1},{2,10},{10,14}... | collective-permute-start | bytes 614408 | tf_op jit(solution)/shard_map/ppermute | solution.py:267
  6.1 11.4 %collective-permute-start.5 = (bf16[8,100,250]{2,1,0:T(8,128)(2,1)S(1)}, bf16[8,100,250]{2,1,0:T(8,128)(2,1)S(1)}, u32[]{:S(2)}, u32[]{:S(2)}) collective-permute-start(bf16[8,100,250]{2,1,0:T(8,128)(2,1)S(1)} %bitcast.7), channel_id=1, source_target_pairs={{0,2},{1,3},{2,0},{3,1},{4,6},{5,7},{6,4},{7,5},{8,10},{9,11},{10,... | collective-permute-start | bytes 1200008 | tf_op jit(solution)/shard_map/ppermute | solution.py:264
  7.6 9.0 %collective-permute-start.1 = (bf16[200,512]{1,0:T(8,128)(2,1)S(1)}, bf16[200,512]{1,0:T(8,128)(2,1)S(1)}, u32[]{:S(2)}, u32[]{:S(2)}) collective-permute-start(bf16[200,512]{1,0:T(8,128)(2,1)S(1)} %get-tuple-element.27.refs_0_), channel_id=1, source_target_pairs={{8,0},{12,8},{4,12},{0,4},{9,1},{13,9},{5,13},{1,5},{10,2},{14,10}... | collective-permute-start | bytes 614408 | tf_op jit(solution)/shard_map/ppermute | solution.py:267
  11.6 7.7 %collective-permute-start.2 = (bf16[2,202,500]{2,1,0:T(8,128)(2,1)S(1)}, bf16[2,202,500]{2,1,0:T(8,128)(2,1)S(1)}, u32[]{:S(2)}, u32[]{:S(2)}) collective-permute-start(bf16[2,202,500]{2,1,0:T(8,128)(2,1)S(1)} %shard_map.60), channel_id=1, source_target_pairs={{0,1},{1,0},{2,3},{3,2},{4,5},{5,4},{6,7},{7,6},{8,9},{9,8},{10,11... | collective-permute-start | bytes 1212008 | tf_op jit(solution)/shard_map/ppermute | solution.py:264
  11.7 9.2 %collective-permute-start.7 = (bf16[200,512]{1,0:T(8,128)(2,1)S(1)}, bf16[200,512]{1,0:T(8,128)(2,1)S(1)}, u32[]{:S(2)}, u32[]{:S(2)}) collective-permute-start(bf16[200,512]{1,0:T(8,128)(2,1)S(1)} %collective-permute-done.refs_1_), channel_id=1, source_target_pairs={{0,8},{8,12},{12,4},{4,0},{1,9},{9,13},{13,5},{5,1},{2,10},{10,14}... | collective-permute-start | bytes 614408 | tf_op jit(solution)/shard_map/ppermute | solution.py:267
  16.7 2.6 %collective-permute-start.3 = (bf16[204,500]{1,0:T(8,128)(2,1)S(1)}, bf16[204,500]{1,0:T(8,128)(2,1)S(1)}, u32[]{:S(2)}, u32[]{:S(2)}) collective-permute-start(bf16[204,500]{1,0:T(8,128)(2,1)S(1)} %shard_map.61), channel_id=1, source_target_pairs={{0,1},{1,0},{2,3},{3,2},{4,5},{5,4},{6,7},{7,6},{8,9},{9,8},{10,11... | collective-permute-start | bytes 612008 | tf_op jit(solution)/shard_map/ppermute | solution.py:264
  16.9 1.6 %collective-permute-start.4 = (bf16[201,500]{1,0:T(8,128)(2,1)S(1)}, bf16[201,500]{1,0:T(8,128)(2,1)S(1)}, u32[]{:S(2)}, u32[]{:S(2)}) collective-permute-start(bf16[201,500]{1,0:T(8,128)(2,1)S(1)} %shard_map.62), channel_id=1, source_target_pairs={{0,1},{1,0},{2,3},{3,2},{4,5},{5,4},{6,7},{7,6},{8,9},{9,8},{10,11... | collective-permute-start | bytes 603008 | tf_op jit(solution)/shard_map/ppermute | solution.py:264
  17.5 1.5 %collective-permute-start.6 = (bf16[4,100,250]{2,1,0:T(8,128)(2,1)S(1)}, bf16[4,100,250]{2,1,0:T(8,128)(2,1)S(1)}, u32[]{:S(2)}, u32[]{:S(2)}) collective-permute-start(bf16[4,100,250]{2,1,0:T(8,128)(2,1)S(1)} %shard_map.63), channel_id=1, source_target_pairs={{0,1},{1,0},{2,3},{3,2},{4,5},{5,4},{6,7},{7,6},{8,9},{9,8},{10,11... | collective-permute-start | bytes 600008 | tf_op jit(solution)/shard_map/ppermute | solution.py:264
  20.9 1.5 %collective-permute-start.8 = (bf16[200,512]{1,0:T(8,128)(2,1)S(1)}, bf16[200,512]{1,0:T(8,128)(2,1)S(1)}, u32[]{:S(2)}, u32[]{:S(2)}) collective-permute-start(bf16[200,512]{1,0:T(8,128)(2,1)S(1)} %collective-permute-done.7.mine), channel_id=1, source_target_pairs={{0,1},{1,0},{2,3},{3,2},{4,5},{5,4},{6,7},{7,6},{8,9},{9,8},{10,11... | collective-permute-start | bytes 614408 | tf_op jit(solution)/shard_map/ppermute | solution.py:264
  23.1 1.9 %collective-permute-start.9 = (f32[2,108,128]{2,1,0:T(8,128)S(1)}, f32[2,108,128]{2,1,0:T(8,128)S(1)}, u32[]{:S(2)}, u32[]{:S(2)}) collective-permute-start(f32[2,108,128]{2,1,0:T(8,128)S(1)} %get-tuple-element.39.mine_ref), channel_id=1, source_target_pairs={{0,1},{1,0},{2,3},{3,2},{4,5},{5,4},{6,7},{7,6},{8,9},{9,8},{10,11... | collective-permute-start | bytes 331784 | tf_op jit(solution)/shard_map/ppermute | solution.py:264
  23.4 11.0 %collective-permute-start.11 = (bf16[400,256]{1,0:T(8,128)(2,1)S(1)}, bf16[400,256]{1,0:T(8,128)(2,1)S(1)}, u32[]{:S(2)}, u32[]{:S(2)}) collective-permute-start(bf16[400,256]{1,0:T(8,128)(2,1)S(1)} %get-tuple-element.43), channel_id=1, source_target_pairs={{0,2},{1,3},{2,0},{3,1},{4,6},{5,7},{6,4},{7,5},{8,10},{9,11},{10,... | collective-permute-start | bytes 614408 | tf_op jit(solution)/shard_map/ppermute | solution.py:264
  24.9 9.6 %collective-permute-start.12 = (bf16[400,256]{1,0:T(8,128)(2,1)S(1)}, bf16[400,256]{1,0:T(8,128)(2,1)S(1)}, u32[]{:S(2)}, u32[]{:S(2)}) collective-permute-start(bf16[400,256]{1,0:T(8,128)(2,1)S(1)} %get-tuple-element.44), channel_id=1, source_target_pairs={{0,3},{1,2},{2,1},{3,0},{4,7},{5,6},{6,5},{7,4},{8,11},{9,10},{10,... | collective-permute-start | bytes 614408 | tf_op jit(solution)/shard_map/ppermute | solution.py:264
  25.1 3.6 %collective-permute-start.10 = (f32[2,128]{1,0:T(2,128)S(1)}, f32[2,128]{1,0:T(2,128)S(1)}, u32[]{:S(2)}, u32[]{:S(2)}) collective-permute-start(f32[2,128]{1,0:T(2,128)S(1)} %get-tuple-element.40), channel_id=1, source_target_pairs={{0,4},{4,0},{8,12},{12,8},{1,5},{5,1},{9,13},{13,9},{2,6},{6,2},{1... | collective-permute-start | bytes 3080 | tf_op jit(solution)/shard_map/ppermute | solution.py:267
  29.4 5.1 %collective-permute-start.13 = (bf16[200,250]{1,0:T(8,128)(2,1)S(1)}, bf16[200,250]{1,0:T(8,128)(2,1)S(1)}, u32[]{:S(2)}, u32[]{:S(2)}) collective-permute-start(bf16[200,250]{1,0:T(8,128)(2,1)S(1)} %get-tuple-element.45), channel_id=1, source_target_pairs={{0,1},{1,0},{2,3},{3,2},{4,5},{5,4},{6,7},{7,6},{8,9},{9,8},{10,11... | collective-permute-start | bytes 300008 | tf_op jit(solution)/shard_map/ppermute | solution.py:264
  29.5 5.0 %collective-permute-start.14 = (bf16[200,250]{1,0:T(8,128)(2,1)S(1)}, bf16[200,250]{1,0:T(8,128)(2,1)S(1)}, u32[]{:S(2)}, u32[]{:S(2)}) collective-permute-start(bf16[200,250]{1,0:T(8,128)(2,1)S(1)} %get-tuple-element.46), channel_id=1, source_target_pairs={{0,1},{1,0},{2,3},{3,2},{4,5},{5,4},{6,7},{7,6},{8,9},{9,8},{10,11... | collective-permute-start | bytes 300008 | tf_op jit(solution)/shard_map/ppermute | solution.py:264
  30.0 4.4 %collective-permute-start.15 = (f32[1,128]{1,0:T(1,128)S(1)}, f32[1,128]{1,0:T(1,128)S(1)}, u32[]{:S(2)}, u32[]{:S(2)}) collective-permute-start(f32[1,128]{1,0:T(1,128)S(1)} %get-tuple-element.49), channel_id=1, source_target_pairs={{0,8},{4,12},{8,0},{12,4},{1,9},{5,13},{9,1},{13,5},{2,10},{6,14},... | collective-permute-start | bytes 1544 | tf_op jit(solution)/shard_map/ppermute | solution.py:267

commit v7 on v6

--- a/solution.py
+++ b/solution.py
@@ -9,9 +9,6 @@
 
 LANES = 128
 STEP = 32
-HELD = 1
-SPARE = 104
-OPT = {'aw': 1, 'bw': 1, 'ar': 2, 'br': 4, 'rel': 0, 'hold': 1, 'c1r': 0}
 GRANT = 16 * 1024 * 1024
 PREP = 56 * 1024 * 1024
 HBM = pltpu.MemorySpace.HBM
@@ -163,7 +160,6 @@
     for ref, part, s in ((same_ref, same_part, 2), (other_ref, other_part, 3)):
         grad = part[...] + jnp.dot(cotan_s[...], theta_s[:, column(s, padded)], preferred_element_type=f32)
         store_grad(grad, ref, half, nocc)
-    energy_ref[...] = jnp.zeros_like(energy_ref)
     early = first_ref.shape[0] // 2
     me = lax.axis_index("chol")
     rows = [pl.ds(me ^ source_of(me, path), 1) for path in sources]
@@ -186,16 +182,12 @@
 
 
 def chip_walkers(*refs, half, nocc, padded):
-    *factors, own_ref, low_ref, high_ref = refs
+    *factors, own_ref, core_ref = refs
     for s in (1, 0):
         grad = 0.0
         for cotan_s, theta_s in zip(factors[::2], factors[1::2]):
             grad += jnp.dot(cotan_s[...], theta_s[:, column(s, padded)], preferred_element_type=f32)
-        if s == 0:
-            store_grad(grad, own_ref, half, nocc)
-        else:
-            store_grad(grad, low_ref, half // 2, nocc)
-            store_grad(grad[half // 2 * LANES:], high_ref, half // 2, nocc)
+        store_grad(grad, core_ref if s else own_ref, half, nocc)
 
 
 def halve(mine_ref, arrived_ref, keep_ref, send_ref):
@@ -207,7 +199,7 @@
 
 def finish(*refs):
     *refs, out_hbm, energy_hbm, out_ref, energy_ref, sems = refs
-    own_ref, same_ref, other_ref, low_ref, high_ref, *energy_refs = refs
+    own_ref, same_ref, other_ref, core_ref, *energy_refs = refs
     half = own_ref.shape[0]
     nocc, gdev, width = out_ref.shape
     h = lax.rem(lax.axis_index("walk"), 2)
@@ -224,7 +216,7 @@
     for n, start in enumerate(range(0, nocc, STEP), start=1):
         stop = min(start + STEP, nocc)
         mine = own_ref[:, start:stop, :width] + arrived(same_ref)
-        theirs = arrived(low_ref, high_ref) + arrived(other_ref)
+        theirs = arrived(core_ref) + arrived(other_ref)
 
         @pl.when(h == 0)
         def _():
@@ -297,7 +289,7 @@
 
     paired = swap(cross, 1)
     crossed = swap(chol_vectors, 2)
-    relayed = swap(call(relay, struct(half, nocc + OPT["rel"], width), crossed), 1)
+    relayed = swap(call(relay, struct(half, nocc, width), crossed), 1)
     chol, weight = call(
         functools.partial(place_chol, sources=sources, nocc=nocc, width=width, **sizes),
         (struct(half * LANES, wide), struct(2 * nchol, LANES, dtype=f32)),
@@ -315,8 +307,8 @@
             functools.partial(mail, width=width), struct(*shape) if len(blocks) == 1 else struct(2, *shape), *blocks
         )
 
-    a_ops = [swap(message(OPT["ar"], width if OPT["aw"] else padded, theta, early[0]), 1)]
-    b_op = message(OPT["br"], width if OPT["bw"] else padded, early[1])
+    a_ops = [swap(message(2, width, theta, early[0]), 1)]
+    b_op = message(4, width, early[1])
     theirs = a_ops + [swap(b_op, 1)] + [swap(t, 1) for t in early[2:]]
     grads, energies, factors = None, [], []
     for start in range(0, nchol - 1, 3):
@@ -355,8 +347,8 @@
         functools.partial(last_walkers, sources=sources, nocc=nocc, width=width, **sizes),
         (
             struct(half * nocc, padded),
-            struct(half * nocc, padded),
-            struct(2, nchol + SPARE, LANES, dtype=f32),
+            struct(half * nocc, width),
+            struct(2, nchol, LANES, dtype=f32),
             struct(walkers * LANES, wide),
             struct(half * LANES, walkers * LANES),
         ),
@@ -373,17 +365,17 @@
     while n:
         energy, send = call(halve, (struct(n, LANES, dtype=f32),) * 2, energy, arrived)
         arrived = turn(send, [(i, i ^ flip) for i in range(nchol)])
-        if flip == HELD:
-            theta_s, _ = lax.optimization_barrier((theta_s, arrived))
+        if flip == 1:
+            first_in = arrived
         n, flip = n // 2, flip * 2
     own, *core = call(
         functools.partial(chip_walkers, nocc=nocc, **sizes),
-        (struct(half, rows, padded, dtype=f32),) + (struct(half // 2 * nocc, width),) * 2,
+        (struct(half, rows, padded, dtype=f32), struct(half * nocc, width)),
         *factors,
         cotan_s,
         theta_s,
     )
-    core = [swap(c, 1) for c in core]
+    core = [swap(c, 1) for c in lax.optimization_barrier((*core, first_in))[:-1]]
     chol_grad, energies = call(
         finish,
         (struct(nocc, gdev, width, dtype=f32), struct(1, 1, dtype=f32)),

time: 35.7 us -> 35.7 us (level)
  waiting for transfers between devices: 11.6 us -> 12 us
  starting transfers between devices: 16.7 us -> 16.3 us
    ppermute x11 -> x10, waiting for transfers between devices: 2.25 us -> 3.76 us  [swap(): return lax.ppermute(x, 'walk', [(i, i ^ flip) for i in range(nwalk)])]
    ppermute x5, waiting for transfers between devices: 9.38 us -> 8.19 us  [turn(): return lax.ppermute(x, 'chol', pairs)]
    ppermute x11 -> x10, starting transfers between devices: 5.04 us -> 4.8 us  [swap(): return lax.ppermute(x, 'walk', [(i, i ^ flip) for i in range(nwalk)])]
  transfers between devices with their start and end apart: 16 -> 15, of which waited for: 8 -> 9; matrix products, arithmetic and copies ran while one was open for 0% -> 0% of each run, Pallas kernels for 9% -> 9%
where the time goes in v7:
time: 35.7 us; the launch traced here: 35.5 us
  starting transfers between devices  16.3 us (46%)
  waiting for transfers between devices  12 us (34%)
  Pallas kernels  6.39 us (18%)
  between operations  0.75 us (2%)
    ppermute x5, starting transfers between devices, turn(): return lax.ppermute(x, 'chol', pairs)  11.5 us
    ppermute x5, waiting for transfers between devices, turn(): return lax.ppermute(x, 'chol', pairs)  8.19 us
    pallas_call x13, Pallas kernels, call(): pl.pallas_call(kernel, out_shape=outs, in_specs=[pl.BlockSpec(memory_spac...  6.39 us
    ppermute x10, starting transfers between devices, swap(): return lax.ppermute(x, 'walk', [(i, i ^ flip) for i in range(nwalk)])  4.8 us
    ppermute x10, waiting for transfers between devices, swap(): return lax.ppermute(x, 'walk', [(i, i ^ flip) for i in range(nwalk)])  3.76 us
  transfers between devices with their start and end apart: 15, of which 9 were waited for; matrix products, arithmetic and copies ran while one was open for 0% of the time, Pallas kernels for 9%

profile of v7, /device:TPU:0, one launch (start us, length us, event | category | flops | bytes accessed | tf_op | source)
XLA Modules:
  0.0 35.5 jit_solution(14375392531833596225)
XLA Ops:
  0.6 0.0 copy-start
  0.6 1.3 %shard_map.59 = (bf16[200,512]{1,0:T(8,128)(2,1)S(1)}, bf16[100,8,250]{2,1,0:T(8,128)(2,1)S(1)}) custom-call(s32[1,100]{1,0:T(1,128)} %bitcast.12, bf16[100,1000]{1,0:T(8,128)(2,1)} %bitcast.11, bf16[100,8,250]{2,1,0:T(8,128)(2,1)} %bitcast.10), custom_call_target="tpu_custom_call" | custom-call | tf_op jit(solution)/shard_map/pallas_call | solution.py:236
  1.9 4.1 %collective-permute-start = (bf16[200,512]{1,0:T(8,128)(2,1)S(1)}, bf16[200,512]{1,0:T(8,128)(2,1)S(1)}, u32[]{:S(2)}, u32[]{:S(2)}) collective-permute-start(bf16[200,512]{1,0:T(8,128)(2,1)S(1)} %get-tuple-element.26.refs_0_), channel_id=1, source_target_pairs={{0,8},{8,12},{12,4},{4,0},{1,9},{9,13},{13,5},{5,1},{2,10},{10,14}... | collective-permute-start | bytes 614408 | tf_op jit(solution)/shard_map/ppermute | solution.py:259
  6.0 0.1 copy.8
  6.1 1.6 %collective-permute-start.5 = (bf16[8,100,250]{2,1,0:T(8,128)(2,1)S(1)}, bf16[8,100,250]{2,1,0:T(8,128)(2,1)S(1)}, u32[]{:S(2)}, u32[]{:S(2)}) collective-permute-start(bf16[8,100,250]{2,1,0:T(8,128)(2,1)S(1)} %bitcast.7), channel_id=1, source_target_pairs={{0,2},{1,3},{2,0},{3,1},{4,6},{5,7},{6,4},{7,5},{8,10},{9,11},{10,... | collective-permute-start | bytes 1200008 | tf_op jit(solution)/shard_map/ppermute | solution.py:256
  7.6 0.0 collective-permute-start.1
  7.6 3.9 %collective-permute-done.refs_1_ = bf16[200,512]{1,0:T(8,128)(2,1)S(1)} collective-permute-done((bf16[200,512]{1,0:T(8,128)(2,1)S(1)}, bf16[200,512]{1,0:T(8,128)(2,1)S(1)}, u32[]{:S(2)}, u32[]{:S(2)}) %collective-permute-start) | collective-permute-done | bytes 204832 | tf_op jit(solution)/shard_map/ppermute | solution.py:259
  11.5 0.1 shard_map.60
  11.6 0.1 collective-permute-start.2
  11.7 3.4 %collective-permute-start.7 = (bf16[200,512]{1,0:T(8,128)(2,1)S(1)}, bf16[200,512]{1,0:T(8,128)(2,1)S(1)}, u32[]{:S(2)}, u32[]{:S(2)}) collective-permute-start(bf16[200,512]{1,0:T(8,128)(2,1)S(1)} %collective-permute-done.refs_1_), channel_id=1, source_target_pairs={{0,8},{8,12},{12,4},{4,0},{1,9},{9,13},{13,5},{5,1},{2,10},{10,14}... | collective-permute-start | bytes 614408 | tf_op jit(solution)/shard_map/ppermute | solution.py:259
  15.2 1.5 %collective-permute-done.1.refs_0_.refs_2_ = bf16[200,512]{1,0:T(8,128)(2,1)S(1)} collective-permute-done((bf16[200,512]{1,0:T(8,128)(2,1)S(1)}, bf16[200,512]{1,0:T(8,128)(2,1)S(1)}, u32[]{:S(2)}, u32[]{:S(2)}) %collective-permute-start.1) | collective-permute-done | bytes 204832 | tf_op jit(solution)/shard_map/ppermute | solution.py:259
  16.6 0.1 shard_map.61
  16.7 0.1 collective-permute-start.3
  16.8 0.0 copy-done
  16.8 0.1 shard_map.62
  16.9 0.5 %collective-permute-start.4 = (bf16[201,500]{1,0:T(8,128)(2,1)S(1)}, bf16[201,500]{1,0:T(8,128)(2,1)S(1)}, u32[]{:S(2)}, u32[]{:S(2)}) collective-permute-start(bf16[201,500]{1,0:T(8,128)(2,1)S(1)} %shard_map.62), channel_id=1, source_target_pairs={{0,1},{1,0},{2,3},{3,2},{4,5},{5,4},{6,7},{7,6},{8,9},{9,8},{10,11... | collective-permute-start | bytes 603008 | tf_op jit(solution)/shard_map/ppermute | solution.py:256
  17.5 0.0 collective-permute-done.5.crossed_ref.same_ref
  17.5 0.1 collective-permute-start.6
  17.6 1.0 %collective-permute-done.4.cross_ref = bf16[201,500]{1,0:T(8,128)(2,1)S(1)} collective-permute-done((bf16[201,500]{1,0:T(8,128)(2,1)S(1)}, bf16[201,500]{1,0:T(8,128)(2,1)S(1)}, u32[]{:S(2)}, u32[]{:S(2)}) %collective-permute-start.4) | collective-permute-done | bytes 201032 | tf_op jit(solution)/shard_map/ppermute | solution.py:256
  18.6 0.5 %collective-permute-done.6.other_ref = bf16[4,100,250]{2,1,0:T(8,128)(2,1)S(1)} collective-permute-done((bf16[4,100,250]{2,1,0:T(8,128)(2,1)S(1)}, bf16[4,100,250]{2,1,0:T(8,128)(2,1)S(1)}, u32[]{:S(2)}, u32[]{:S(2)}) %collective-permute-start.6) | collective-permute-done | bytes 200032 | tf_op jit(solution)/shard_map/ppermute | solution.py:256
  19.0 0.3 shard_map.64
  19.3 0.0 collective-permute-done.3.refs_4_
  19.3 0.0 collective-permute-done.2.refs_3_
  19.4 1.5 %shard_map.65 = (f32[512,256]{1,0:T(8,128)S(1)}, f32[512,256]{1,0:T(8,128)S(1)}, f32[768,512]{1,0:T(8,128)S(1)}, bf16[768,1024]{1,0:T(8,128)(2,1)S(1)}, bf16[512,768]{1,0:T(8,128)(2,1)S(1)}) custom-call(bf16[200,512]{1,0:T(8,128)(2,1)S(1)} %get-tuple-element.26.refs_0_, bf16[200,512]{1,0:T(8,128)(2,1)S(1)} %collective-permute-done.refs_1_, ...), custom_call_target="tpu_custom_call" | custom-call | tf_op jit(solution)/shard_map/pallas_call | solution.py:236
  20.8 0.1 collective-permute-done.7.mine
  20.9 0.2 collective-permute-start.8
  21.1 0.5 %shard_map.66.first_ref = f32[6,128]{1,0:T(8,128)S(1)} custom-call(f32[768,512]{1,0:T(8,128)S(1)} %get-tuple-element.35.tmat_ref), custom_call_target="tpu_custom_call" | custom-call | tf_op jit(solution)/shard_map/pallas_call | solution.py:236
  21.6 0.8 %collective-permute-done.8.theirs = bf16[200,512]{1,0:T(8,128)(2,1)S(1)} collective-permute-done((bf16[200,512]{1,0:T(8,128)(2,1)S(1)}, bf16[200,512]{1,0:T(8,128)(2,1)S(1)}, u32[]{:S(2)}, u32[]{:S(2)}) %collective-permute-start.8) | collective-permute-done | bytes 204832 | tf_op jit(solution)/shard_map/ppermute | solution.py:256
  22.4 0.7 %shard_map.67 = (bf16[400,256]{1,0:T(8,128)(2,1)S(1)}, bf16[400,250]{1,0:T(8,128)(2,1)S(1)}, f32[2,4,128]{2,1,0:T(4,128)S(1)}, bf16[256,1024]{1,0:T(8,128)(2,1)S(1)}, bf16[512,256]{1,0:T(8,128)(2,1)S(1)}) custom-call(bf16[200,512]{1,0:T(8,128)(2,1)S(1)} %collective-permute-done.7.mine, bf16[200,512]{1,0:T(8,128)(2,1)S(1)} %collective-permute-done.8.theirs, ...), custom_call_target="tpu_custom_call" | custom-call | tf_op jit(solution)/shard_map/pallas_call | solution.py:236
  23.1 0.3 collective-permute-start.11
  23.4 1.5 %collective-permute-start.9 = (bf16[400,256]{1,0:T(8,128)(2,1)S(1)}, bf16[400,256]{1,0:T(8,128)(2,1)S(1)}, u32[]{:S(2)}, u32[]{:S(2)}) collective-permute-start(bf16[400,256]{1,0:T(8,128)(2,1)S(1)} %get-tuple-element.39), channel_id=1, source_target_pairs={{0,2},{1,3},{2,0},{3,1},{4,6},{5,7},{6,4},{7,5},{8,10},{9,11},{10,... | collective-permute-start | bytes 614408 | tf_op jit(solution)/shard_map/ppermute | solution.py:256
  24.9 0.0 collective-permute-done.11.arrived_ref
  24.9 1.5 %collective-permute-start.12 = (f32[2,128]{1,0:T(2,128)S(1)}, f32[2,128]{1,0:T(2,128)S(1)}, u32[]{:S(2)}, u32[]{:S(2)}) collective-permute-start(f32[2,128]{1,0:T(2,128)S(1)} %get-tuple-element.43), channel_id=1, source_target_pairs={{0,4},{4,0},{8,12},{12,8},{1,5},{5,1},{9,13},{13,9},{2,6},{6,2},{1... | collective-permute-start | bytes 3080 | tf_op jit(solution)/shard_map/ppermute | solution.py:259
  26.4 0.5 %collective-permute-start.10 = (bf16[400,250]{1,0:T(8,128)(2,1)S(1)}, bf16[400,250]{1,0:T(8,128)(2,1)S(1)}, u32[]{:S(2)}, u32[]{:S(2)}) collective-permute-start(bf16[400,250]{1,0:T(8,128)(2,1)S(1)} %get-tuple-element.40), channel_id=1, source_target_pairs={{0,3},{1,2},{2,1},{3,0},{4,7},{5,6},{6,5},{7,4},{8,11},{9,10},{10,... | collective-permute-start | bytes 600008 | tf_op jit(solution)/shard_map/ppermute | solution.py:256
  26.9 0.7 %shard_map.68 = (f32[4,104,256]{2,1,0:T(8,128)S(1)}, bf16[400,250]{1,0:T(8,128)(2,1)S(1)}) custom-call(bf16[512,768]{1,0:T(8,128)(2,1)S(1)} %get-tuple-element.30.refs_0_, bf16[768,1024]{1,0:T(8,128)(2,1)S(1)} %get-tuple-element.31.refs_1_, bf16[512,256]{1,0:T(8,128)(2,1)S(1)} %get-tuple-element.36.refs_2_, bf16[256,1024]{1,0:T(8,128)(2,1)S(1)} %get-tuple-element.37.refs_3_), custom_call_target="tpu_custom_call" | custom-call | tf_op jit(solution)/shard_map/pallas_call | solution.py:236
  27.6 0.8 %collective-permute-done.12.arrived_ref = f32[2,128]{1,0:T(2,128)S(1)} collective-permute-done((f32[2,128]{1,0:T(2,128)S(1)}, f32[2,128]{1,0:T(2,128)S(1)}, u32[]{:S(2)}, u32[]{:S(2)}) %collective-permute-start.12) | collective-permute-done | bytes 1056 | tf_op jit(solution)/shard_map/ppermute | solution.py:259
  28.5 0.0 collective-permute-start.13
  28.5 2.5 %collective-permute-start.14 = (f32[1,128]{1,0:T(1,128)S(1)}, f32[1,128]{1,0:T(1,128)S(1)}, u32[]{:S(2)}, u32[]{:S(2)}) collective-permute-start(f32[1,128]{1,0:T(1,128)S(1)} %get-tuple-element.47), channel_id=1, source_target_pairs={{0,8},{4,12},{8,0},{12,4},{1,9},{5,13},{9,1},{13,5},{2,10},{6,14},... | collective-permute-start | bytes 1544 | tf_op jit(solution)/shard_map/ppermute | solution.py:259
  31.0 1.9 %collective-permute-done.14.refs_5_ = f32[1,128]{1,0:T(1,128)S(1)} collective-permute-done((f32[1,128]{1,0:T(1,128)S(1)}, f32[1,128]{1,0:T(1,128)S(1)}, u32[]{:S(2)}, u32[]{:S(2)}) %collective-permute-start.14) | collective-permute-done | bytes 544 | tf_op jit(solution)/shard_map/ppermute | solution.py:259
  32.9 1.6 %collective-permute-done.10.refs_2_ = bf16[400,250]{1,0:T(8,128)(2,1)S(1)} collective-permute-done((bf16[400,250]{1,0:T(8,128)(2,1)S(1)}, bf16[400,250]{1,0:T(8,128)(2,1)S(1)}, u32[]{:S(2)}, u32[]{:S(2)}) %collective-permute-start.10) | collective-permute-done | bytes 200032 | tf_op jit(solution)/shard_map/ppermute | solution.py:256
  34.5 0.0 collective-permute-done.9.refs_1_
  34.5 0.0 collective-permute-done.13.refs_3_
  34.5 1.1 %shard_map.71 = (f32[100,8,250]{2,1,0:T(8,128)}, f32[1,1]{1,0:T(1,128)}) custom-call(f32[4,104,256]{2,1,0:T(8,128)S(1)} %get-tuple-element.38.refs_0_, bf16[400,256]{1,0:T(8,128)(2,1)S(1)} %collective-permute-done.9.refs_1_, bf16[400,250]{1,0:T(8,128)(2,1)S(1)} %collective-permute-done.10.refs_2_, bf16[400,250]{1,0:T(8,128)(2,1)S(1)} %collective-permute-done.13.refs_3_, ...), custom_call_target="tpu_custom_call" | custom-call | tf_op jit(solution)/shard_map/pallas_call | solution.py:236
  (3 shorter events, 0.0 us)
Async XLA Ops:
  0.6 16.2 %copy-start = (s32[1,4]{1,0:T(1,128)S(1)}, s32[1,4]{1,0:T(1,128)}, u32[]{:S(2)}) copy-start(s32[1,4]{1,0:T(1,128)} %code_ref.3) | copy-start | bytes 52
  1.9 9.6 %collective-permute-start = (bf16[200,512]{1,0:T(8,128)(2,1)S(1)}, bf16[200,512]{1,0:T(8,128)(2,1)S(1)}, u32[]{:S(2)}, u32[]{:S(2)}) collective-permute-start(bf16[200,512]{1,0:T(8,128)(2,1)S(1)} %get-tuple-element.26.refs_0_), channel_id=1, source_target_pairs={{0,8},{8,12},{12,4},{4,0},{1,9},{9,13},{13,5},{5,1},{2,10},{10,14}... | collective-permute-start | bytes 614408 | tf_op jit(solution)/shard_map/ppermute | solution.py:259
  6.1 11.4 %collective-permute-start.5 = (bf16[8,100,250]{2,1,0:T(8,128)(2,1)S(1)}, bf16[8,100,250]{2,1,0:T(8,128)(2,1)S(1)}, u32[]{:S(2)}, u32[]{:S(2)}) collective-permute-start(bf16[8,100,250]{2,1,0:T(8,128)(2,1)S(1)} %bitcast.7), channel_id=1, source_target_pairs={{0,2},{1,3},{2,0},{3,1},{4,6},{5,7},{6,4},{7,5},{8,10},{9,11},{10,... | collective-permute-start | bytes 1200008 | tf_op jit(solution)/shard_map/ppermute | solution.py:256
  7.6 9.0 %collective-permute-start.1 = (bf16[200,512]{1,0:T(8,128)(2,1)S(1)}, bf16[200,512]{1,0:T(8,128)(2,1)S(1)}, u32[]{:S(2)}, u32[]{:S(2)}) collective-permute-start(bf16[200,512]{1,0:T(8,128)(2,1)S(1)} %get-tuple-element.26.refs_0_), channel_id=1, source_target_pairs={{8,0},{12,8},{4,12},{0,4},{9,1},{13,9},{5,13},{1,5},{10,2},{14,10}... | collective-permute-start | bytes 614408 | tf_op jit(solution)/shard_map/ppermute | solution.py:259
  11.6 7.7 %collective-permute-start.2 = (bf16[2,202,500]{2,1,0:T(8,128)(2,1)S(1)}, bf16[2,202,500]{2,1,0:T(8,128)(2,1)S(1)}, u32[]{:S(2)}, u32[]{:S(2)}) collective-permute-start(bf16[2,202,500]{2,1,0:T(8,128)(2,1)S(1)} %shard_map.60), channel_id=1, source_target_pairs={{0,1},{1,0},{2,3},{3,2},{4,5},{5,4},{6,7},{7,6},{8,9},{9,8},{10,11... | collective-permute-start | bytes 1212008 | tf_op jit(solution)/shard_map/ppermute | solution.py:256
  11.7 9.2 %collective-permute-start.7 = (bf16[200,512]{1,0:T(8,128)(2,1)S(1)}, bf16[200,512]{1,0:T(8,128)(2,1)S(1)}, u32[]{:S(2)}, u32[]{:S(2)}) collective-permute-start(bf16[200,512]{1,0:T(8,128)(2,1)S(1)} %collective-permute-done.refs_1_), channel_id=1, source_target_pairs={{0,8},{8,12},{12,4},{4,0},{1,9},{9,13},{13,5},{5,1},{2,10},{10,14}... | collective-permute-start | bytes 614408 | tf_op jit(solution)/shard_map/ppermute | solution.py:259
  16.7 2.6 %collective-permute-start.3 = (bf16[204,500]{1,0:T(8,128)(2,1)S(1)}, bf16[204,500]{1,0:T(8,128)(2,1)S(1)}, u32[]{:S(2)}, u32[]{:S(2)}) collective-permute-start(bf16[204,500]{1,0:T(8,128)(2,1)S(1)} %shard_map.61), channel_id=1, source_target_pairs={{0,1},{1,0},{2,3},{3,2},{4,5},{5,4},{6,7},{7,6},{8,9},{9,8},{10,11... | collective-permute-start | bytes 612008 | tf_op jit(solution)/shard_map/ppermute | solution.py:256
  16.9 1.6 %collective-permute-start.4 = (bf16[201,500]{1,0:T(8,128)(2,1)S(1)}, bf16[201,500]{1,0:T(8,128)(2,1)S(1)}, u32[]{:S(2)}, u32[]{:S(2)}) collective-permute-start(bf16[201,500]{1,0:T(8,128)(2,1)S(1)} %shard_map.62), channel_id=1, source_target_pairs={{0,1},{1,0},{2,3},{3,2},{4,5},{5,4},{6,7},{7,6},{8,9},{9,8},{10,11... | collective-permute-start | bytes 603008 | tf_op jit(solution)/shard_map/ppermute | solution.py:256
  17.5 1.5 %collective-permute-start.6 = (bf16[4,100,250]{2,1,0:T(8,128)(2,1)S(1)}, bf16[4,100,250]{2,1,0:T(8,128)(2,1)S(1)}, u32[]{:S(2)}, u32[]{:S(2)}) collective-permute-start(bf16[4,100,250]{2,1,0:T(8,128)(2,1)S(1)} %shard_map.63), channel_id=1, source_target_pairs={{0,1},{1,0},{2,3},{3,2},{4,5},{5,4},{6,7},{7,6},{8,9},{9,8},{10,11... | collective-permute-start | bytes 600008 | tf_op jit(solution)/shard_map/ppermute | solution.py:256
  20.9 1.5 %collective-permute-start.8 = (bf16[200,512]{1,0:T(8,128)(2,1)S(1)}, bf16[200,512]{1,0:T(8,128)(2,1)S(1)}, u32[]{:S(2)}, u32[]{:S(2)}) collective-permute-start(bf16[200,512]{1,0:T(8,128)(2,1)S(1)} %collective-permute-done.7.mine), channel_id=1, source_target_pairs={{0,1},{1,0},{2,3},{3,2},{4,5},{5,4},{6,7},{7,6},{8,9},{9,8},{10,11... | collective-permute-start | bytes 614408 | tf_op jit(solution)/shard_map/ppermute | solution.py:256
  23.1 1.8 %collective-permute-start.11 = (f32[2,4,128]{2,1,0:T(4,128)S(1)}, f32[2,4,128]{2,1,0:T(4,128)S(1)}, u32[]{:S(2)}, u32[]{:S(2)}) collective-permute-start(f32[2,4,128]{2,1,0:T(4,128)S(1)} %get-tuple-element.42.mine_ref), channel_id=1, source_target_pairs={{0,1},{1,0},{2,3},{3,2},{4,5},{5,4},{6,7},{7,6},{8,9},{9,8},{10,11... | collective-permute-start | bytes 12296 | tf_op jit(solution)/shard_map/ppermute | solution.py:256
  23.4 11.1 %collective-permute-start.9 = (bf16[400,256]{1,0:T(8,128)(2,1)S(1)}, bf16[400,256]{1,0:T(8,128)(2,1)S(1)}, u32[]{:S(2)}, u32[]{:S(2)}) collective-permute-start(bf16[400,256]{1,0:T(8,128)(2,1)S(1)} %get-tuple-element.39), channel_id=1, source_target_pairs={{0,2},{1,3},{2,0},{3,1},{4,6},{5,7},{6,4},{7,5},{8,10},{9,11},{10,... | collective-permute-start | bytes 614408 | tf_op jit(solution)/shard_map/ppermute | solution.py:256
  24.9 3.6 %collective-permute-start.12 = (f32[2,128]{1,0:T(2,128)S(1)}, f32[2,128]{1,0:T(2,128)S(1)}, u32[]{:S(2)}, u32[]{:S(2)}) collective-permute-start(f32[2,128]{1,0:T(2,128)S(1)} %get-tuple-element.43), channel_id=1, source_target_pairs={{0,4},{4,0},{8,12},{12,8},{1,5},{5,1},{9,13},{13,9},{2,6},{6,2},{1... | collective-permute-start | bytes 3080 | tf_op jit(solution)/shard_map/ppermute | solution.py:259
  26.4 8.1 %collective-permute-start.10 = (bf16[400,250]{1,0:T(8,128)(2,1)S(1)}, bf16[400,250]{1,0:T(8,128)(2,1)S(1)}, u32[]{:S(2)}, u32[]{:S(2)}) collective-permute-start(bf16[400,250]{1,0:T(8,128)(2,1)S(1)} %get-tuple-element.40), channel_id=1, source_target_pairs={{0,3},{1,2},{2,1},{3,0},{4,7},{5,6},{6,5},{7,4},{8,11},{9,10},{10,... | collective-permute-start | bytes 600008 | tf_op jit(solution)/shard_map/ppermute | solution.py:256
  28.5 6.0 %collective-permute-start.13 = (bf16[400,250]{1,0:T(8,128)(2,1)S(1)}, bf16[400,250]{1,0:T(8,128)(2,1)S(1)}, u32[]{:S(2)}, u32[]{:S(2)}) collective-permute-start(bf16[400,250]{1,0:T(8,128)(2,1)S(1)} %get-tuple-element.44), channel_id=1, source_target_pairs={{0,1},{1,0},{2,3},{3,2},{4,5},{5,4},{6,7},{7,6},{8,9},{9,8},{10,11... | collective-permute-start | bytes 600008 | tf_op jit(solution)/shard_map/ppermute | solution.py:256
  28.5 4.4 %collective-permute-start.14 = (f32[1,128]{1,0:T(1,128)S(1)}, f32[1,128]{1,0:T(1,128)S(1)}, u32[]{:S(2)}, u32[]{:S(2)}) collective-permute-start(f32[1,128]{1,0:T(1,128)S(1)} %get-tuple-element.47), channel_id=1, source_target_pairs={{0,8},{4,12},{8,0},{12,4},{1,9},{5,13},{9,1},{13,5},{2,10},{6,14},... | collective-permute-start | bytes 1544 | tf_op jit(solution)/shard_map/ppermute | solution.py:259

commit v8 on v6

--- a/solution.py
+++ b/solution.py
@@ -9,7 +9,6 @@
 
 LANES = 128
 STEP = 32
-HELD = 1
 SPARE = 104
 OPT = {'aw': 1, 'bw': 1, 'ar': 2, 'br': 4, 'rel': 0, 'hold': 1, 'c1r': 0}
 GRANT = 16 * 1024 * 1024
@@ -355,7 +354,7 @@
         functools.partial(last_walkers, sources=sources, nocc=nocc, width=width, **sizes),
         (
             struct(half * nocc, padded),
-            struct(half * nocc, padded),
+            struct(half * nocc, width),
             struct(2, nchol + SPARE, LANES, dtype=f32),
             struct(walkers * LANES, wide),
             struct(half * LANES, walkers * LANES),
@@ -373,8 +372,8 @@
     while n:
         energy, send = call(halve, (struct(n, LANES, dtype=f32),) * 2, energy, arrived)
         arrived = turn(send, [(i, i ^ flip) for i in range(nchol)])
-        if flip == HELD:
-            theta_s, _ = lax.optimization_barrier((theta_s, arrived))
+        if flip == 1:
+            first_in = arrived
         n, flip = n // 2, flip * 2
     own, *core = call(
         functools.partial(chip_walkers, nocc=nocc, **sizes),
@@ -383,7 +382,7 @@
         cotan_s,
         theta_s,
     )
-    core = [swap(c, 1) for c in core]
+    core = [swap(c, 1) for c in lax.optimization_barrier((*core, first_in))[:-1]]
     chol_grad, energies = call(
         finish,
         (struct(nocc, gdev, width, dtype=f32), struct(1, 1, dtype=f32)),

time: 35.7 us -> 35.7 us (level)
    ppermute x11, waiting for transfers between devices: 2.25 us -> 3.06 us  [swap(): return lax.ppermute(x, 'walk', [(i, i ^ flip) for i in range(nwalk)])]
    ppermute x5, waiting for transfers between devices: 9.38 us -> 8.65 us  [turn(): return lax.ppermute(x, 'chol', pairs)]
  transfers between devices with their start and end apart: 16 -> 16, of which waited for: 8 -> 9; matrix products, arithmetic and copies ran while one was open for 0% -> 0% of each run, Pallas kernels for 9% -> 9%
where the time goes in v8:
time: 35.7 us; the launch traced here: 35.5 us
  starting transfers between devices  16.6 us (46%)
  waiting for transfers between devices  11.7 us (33%)
  Pallas kernels  6.39 us (18%)
  between operations  0.75 us (2%)
    ppermute x5, starting transfers between devices, turn(): return lax.ppermute(x, 'chol', pairs)  11.6 us
    ppermute x5, waiting for transfers between devices, turn(): return lax.ppermute(x, 'chol', pairs)  8.65 us
    pallas_call x13, Pallas kernels, call(): pl.pallas_call(kernel, out_shape=outs, in_specs=[pl.BlockSpec(memory_spac...  6.39 us
    ppermute x11, starting transfers between devices, swap(): return lax.ppermute(x, 'walk', [(i, i ^ flip) for i in range(nwalk)])  4.99 us
    ppermute x11, waiting for transfers between devices, swap(): return lax.ppermute(x, 'walk', [(i, i ^ flip) for i in range(nwalk)])  3.06 us
  transfers between devices with their start and end apart: 16, of which 9 were waited for; matrix products, arithmetic and copies ran while one was open for 0% of the time, Pallas kernels for 9%

profile of v8, /device:TPU:0, one launch (start us, length us, event | category | flops | bytes accessed | tf_op | source)
XLA Modules:
  0.0 35.5 jit_solution(9074092947566212620)
XLA Ops:
  0.6 0.0 copy-start
  0.6 1.3 %shard_map.59 = (bf16[200,512]{1,0:T(8,128)(2,1)S(1)}, bf16[100,8,250]{2,1,0:T(8,128)(2,1)S(1)}) custom-call(s32[1,100]{1,0:T(1,128)} %bitcast.12, bf16[100,1000]{1,0:T(8,128)(2,1)} %bitcast.11, bf16[100,8,250]{2,1,0:T(8,128)(2,1)} %bitcast.10), custom_call_target="tpu_custom_call" | custom-call | tf_op jit(solution)/shard_map/pallas_call | solution.py:243
  1.9 4.1 %collective-permute-start = (bf16[200,512]{1,0:T(8,128)(2,1)S(1)}, bf16[200,512]{1,0:T(8,128)(2,1)S(1)}, u32[]{:S(2)}, u32[]{:S(2)}) collective-permute-start(bf16[200,512]{1,0:T(8,128)(2,1)S(1)} %get-tuple-element.28.refs_0_), channel_id=1, source_target_pairs={{0,8},{8,12},{12,4},{4,0},{1,9},{9,13},{13,5},{5,1},{2,10},{10,14}... | collective-permute-start | bytes 614408 | tf_op jit(solution)/shard_map/ppermute | solution.py:266
  6.0 0.1 copy.8
  6.1 1.6 %collective-permute-start.5 = (bf16[8,100,250]{2,1,0:T(8,128)(2,1)S(1)}, bf16[8,100,250]{2,1,0:T(8,128)(2,1)S(1)}, u32[]{:S(2)}, u32[]{:S(2)}) collective-permute-start(bf16[8,100,250]{2,1,0:T(8,128)(2,1)S(1)} %bitcast.7), channel_id=1, source_target_pairs={{0,2},{1,3},{2,0},{3,1},{4,6},{5,7},{6,4},{7,5},{8,10},{9,11},{10,... | collective-permute-start | bytes 1200008 | tf_op jit(solution)/shard_map/ppermute | solution.py:263
  7.6 0.0 collective-permute-start.1
  7.6 3.9 %collective-permute-done.refs_1_ = bf16[200,512]{1,0:T(8,128)(2,1)S(1)} collective-permute-done((bf16[200,512]{1,0:T(8,128)(2,1)S(1)}, bf16[200,512]{1,0:T(8,128)(2,1)S(1)}, u32[]{:S(2)}, u32[]{:S(2)}) %collective-permute-start) | collective-permute-done | bytes 204832 | tf_op jit(solution)/shard_map/ppermute | solution.py:266
  11.5 0.1 shard_map.60
  11.6 0.1 collective-permute-start.2
  11.7 3.4 %collective-permute-start.7 = (bf16[200,512]{1,0:T(8,128)(2,1)S(1)}, bf16[200,512]{1,0:T(8,128)(2,1)S(1)}, u32[]{:S(2)}, u32[]{:S(2)}) collective-permute-start(bf16[200,512]{1,0:T(8,128)(2,1)S(1)} %collective-permute-done.refs_1_), channel_id=1, source_target_pairs={{0,8},{8,12},{12,4},{4,0},{1,9},{9,13},{13,5},{5,1},{2,10},{10,14}... | collective-permute-start | bytes 614408 | tf_op jit(solution)/shard_map/ppermute | solution.py:266
  15.2 1.5 %collective-permute-done.1.refs_0_.refs_2_ = bf16[200,512]{1,0:T(8,128)(2,1)S(1)} collective-permute-done((bf16[200,512]{1,0:T(8,128)(2,1)S(1)}, bf16[200,512]{1,0:T(8,128)(2,1)S(1)}, u32[]{:S(2)}, u32[]{:S(2)}) %collective-permute-start.1) | collective-permute-done | bytes 204832 | tf_op jit(solution)/shard_map/ppermute | solution.py:266
  16.6 0.1 shard_map.61
  16.7 0.1 collective-permute-start.3
  16.8 0.0 copy-done
  16.8 0.1 shard_map.62
  16.9 0.5 %collective-permute-start.4 = (bf16[201,500]{1,0:T(8,128)(2,1)S(1)}, bf16[201,500]{1,0:T(8,128)(2,1)S(1)}, u32[]{:S(2)}, u32[]{:S(2)}) collective-permute-start(bf16[201,500]{1,0:T(8,128)(2,1)S(1)} %shard_map.62), channel_id=1, source_target_pairs={{0,1},{1,0},{2,3},{3,2},{4,5},{5,4},{6,7},{7,6},{8,9},{9,8},{10,11... | collective-permute-start | bytes 603008 | tf_op jit(solution)/shard_map/ppermute | solution.py:263
  17.5 0.0 collective-permute-done.5.crossed_ref.same_ref
  17.5 0.1 collective-permute-start.6
  17.6 1.0 %collective-permute-done.4.cross_ref = bf16[201,500]{1,0:T(8,128)(2,1)S(1)} collective-permute-done((bf16[201,500]{1,0:T(8,128)(2,1)S(1)}, bf16[201,500]{1,0:T(8,128)(2,1)S(1)}, u32[]{:S(2)}, u32[]{:S(2)}) %collective-permute-start.4) | collective-permute-done | bytes 201032 | tf_op jit(solution)/shard_map/ppermute | solution.py:263
  18.6 0.5 %collective-permute-done.6.other_ref = bf16[4,100,250]{2,1,0:T(8,128)(2,1)S(1)} collective-permute-done((bf16[4,100,250]{2,1,0:T(8,128)(2,1)S(1)}, bf16[4,100,250]{2,1,0:T(8,128)(2,1)S(1)}, u32[]{:S(2)}, u32[]{:S(2)}) %collective-permute-start.6) | collective-permute-done | bytes 200032 | tf_op jit(solution)/shard_map/ppermute | solution.py:263
  19.0 0.3 shard_map.64
  19.3 0.0 collective-permute-done.3.refs_4_
  19.3 0.0 collective-permute-done.2.refs_3_
  19.4 1.5 %shard_map.65 = (f32[512,256]{1,0:T(8,128)S(1)}, f32[512,256]{1,0:T(8,128)S(1)}, f32[768,512]{1,0:T(8,128)S(1)}, bf16[768,1024]{1,0:T(8,128)(2,1)S(1)}, bf16[512,768]{1,0:T(8,128)(2,1)S(1)}) custom-call(bf16[200,512]{1,0:T(8,128)(2,1)S(1)} %get-tuple-element.28.refs_0_, bf16[200,512]{1,0:T(8,128)(2,1)S(1)} %collective-permute-done.refs_1_, ...), custom_call_target="tpu_custom_call" | custom-call | tf_op jit(solution)/shard_map/pallas_call | solution.py:243
  20.8 0.1 collective-permute-done.7.mine
  20.9 0.2 collective-permute-start.8
  21.1 0.5 %shard_map.66.first_ref = f32[6,128]{1,0:T(8,128)S(1)} custom-call(f32[768,512]{1,0:T(8,128)S(1)} %get-tuple-element.37.tmat_ref), custom_call_target="tpu_custom_call" | custom-call | tf_op jit(solution)/shard_map/pallas_call | solution.py:243
  21.6 0.8 %collective-permute-done.8.theirs = bf16[200,512]{1,0:T(8,128)(2,1)S(1)} collective-permute-done((bf16[200,512]{1,0:T(8,128)(2,1)S(1)}, bf16[200,512]{1,0:T(8,128)(2,1)S(1)}, u32[]{:S(2)}, u32[]{:S(2)}) %collective-permute-start.8) | collective-permute-done | bytes 204832 | tf_op jit(solution)/shard_map/ppermute | solution.py:263
  22.4 0.7 %shard_map.67 = (bf16[400,256]{1,0:T(8,128)(2,1)S(1)}, bf16[400,250]{1,0:T(8,128)(2,1)S(1)}, f32[2,108,128]{2,1,0:T(8,128)S(1)}, bf16[256,1024]{1,0:T(8,128)(2,1)S(1)}, bf16[512,256]{1,0:T(8,128)(2,1)S(1)}) custom-call(bf16[200,512]{1,0:T(8,128)(2,1)S(1)} %collective-permute-done.7.mine, bf16[200,512]{1,0:T(8,128)(2,1)S(1)} %collective-permute-done.8.theirs, ...), custom_call_target="tpu_custom_call" | custom-call | tf_op jit(solution)/shard_map/pallas_call | solution.py:243
  23.1 0.3 collective-permute-start.11
  23.4 1.5 %collective-permute-start.9 = (bf16[400,256]{1,0:T(8,128)(2,1)S(1)}, bf16[400,256]{1,0:T(8,128)(2,1)S(1)}, u32[]{:S(2)}, u32[]{:S(2)}) collective-permute-start(bf16[400,256]{1,0:T(8,128)(2,1)S(1)} %get-tuple-element.41), channel_id=1, source_target_pairs={{0,2},{1,3},{2,0},{3,1},{4,6},{5,7},{6,4},{7,5},{8,10},{9,11},{10,... | collective-permute-start | bytes 614408 | tf_op jit(solution)/shard_map/ppermute | solution.py:263
  24.9 0.2 collective-permute-start.10
  25.1 0.0 collective-permute-done.11.arrived_ref
  25.1 1.5 %collective-permute-start.12 = (f32[2,128]{1,0:T(2,128)S(1)}, f32[2,128]{1,0:T(2,128)S(1)}, u32[]{:S(2)}, u32[]{:S(2)}) collective-permute-start(f32[2,128]{1,0:T(2,128)S(1)} %get-tuple-element.46), channel_id=1, source_target_pairs={{0,4},{4,0},{8,12},{12,8},{1,5},{5,1},{9,13},{13,9},{2,6},{6,2},{1... | collective-permute-start | bytes 3080 | tf_op jit(solution)/shard_map/ppermute | solution.py:266
  26.6 0.7 %shard_map.68 = (f32[4,104,256]{2,1,0:T(8,128)S(1)}, bf16[200,250]{1,0:T(8,128)(2,1)S(1)}, bf16[200,250]{1,0:T(8,128)(2,1)S(1)}) custom-call(bf16[512,768]{1,0:T(8,128)(2,1)S(1)} %get-tuple-element.32.refs_0_, bf16[768,1024]{1,0:T(8,128)(2,1)S(1)} %get-tuple-element.33.refs_1_, bf16[512,256]{1,0:T(8,128)(2,1)S(1)} %get-tuple-element.38.refs_2_, ...), custom_call_target="tpu_custom_call" | custom-call | tf_op jit(solution)/shard_map/pallas_call | solution.py:243
  27.3 1.3 %collective-permute-done.12.arrived_ref = f32[2,128]{1,0:T(2,128)S(1)} collective-permute-done((f32[2,128]{1,0:T(2,128)S(1)}, f32[2,128]{1,0:T(2,128)S(1)}, u32[]{:S(2)}, u32[]{:S(2)}) %collective-permute-start.12) | collective-permute-done | bytes 1056 | tf_op jit(solution)/shard_map/ppermute | solution.py:266
  28.6 0.0 collective-permute-start.13
  28.7 0.5 %collective-permute-start.14 = (bf16[200,250]{1,0:T(8,128)(2,1)S(1)}, bf16[200,250]{1,0:T(8,128)(2,1)S(1)}, u32[]{:S(2)}, u32[]{:S(2)}) collective-permute-start(bf16[200,250]{1,0:T(8,128)(2,1)S(1)} %get-tuple-element.48), channel_id=1, source_target_pairs={{0,1},{1,0},{2,3},{3,2},{4,5},{5,4},{6,7},{7,6},{8,9},{9,8},{10,11... | collective-permute-start | bytes 300008 | tf_op jit(solution)/shard_map/ppermute | solution.py:263
  29.2 2.6 %collective-permute-start.15 = (f32[1,128]{1,0:T(1,128)S(1)}, f32[1,128]{1,0:T(1,128)S(1)}, u32[]{:S(2)}, u32[]{:S(2)}) collective-permute-start(f32[1,128]{1,0:T(1,128)S(1)} %get-tuple-element.51), channel_id=1, source_target_pairs={{0,8},{4,12},{8,0},{12,4},{1,9},{5,13},{9,1},{13,5},{2,10},{6,14},... | collective-permute-start | bytes 1544 | tf_op jit(solution)/shard_map/ppermute | solution.py:266
  31.7 1.9 %collective-permute-done.15.refs_6_ = f32[1,128]{1,0:T(1,128)S(1)} collective-permute-done((f32[1,128]{1,0:T(1,128)S(1)}, f32[1,128]{1,0:T(1,128)S(1)}, u32[]{:S(2)}, u32[]{:S(2)}) %collective-permute-start.15) | collective-permute-done | bytes 544 | tf_op jit(solution)/shard_map/ppermute | solution.py:266
  33.6 0.9 %collective-permute-done.10.refs_2_ = bf16[400,250]{1,0:T(8,128)(2,1)S(1)} collective-permute-done((bf16[400,250]{1,0:T(8,128)(2,1)S(1)}, bf16[400,250]{1,0:T(8,128)(2,1)S(1)}, u32[]{:S(2)}, u32[]{:S(2)}) %collective-permute-start.10) | collective-permute-done | bytes 200032 | tf_op jit(solution)/shard_map/ppermute | solution.py:263
  34.5 0.0 collective-permute-done.9.refs_1_
  34.5 0.0 collective-permute-done.13.refs_3_
  34.5 0.0 collective-permute-done.14.refs_4_
  34.5 1.1 %shard_map.71 = (f32[100,8,250]{2,1,0:T(8,128)}, f32[1,1]{1,0:T(1,128)}) custom-call(f32[4,104,256]{2,1,0:T(8,128)S(1)} %get-tuple-element.40.refs_0_, bf16[400,256]{1,0:T(8,128)(2,1)S(1)} %collective-permute-done.9.refs_1_, bf16[400,250]{1,0:T(8,128)(2,1)S(1)} %collective-permute-done.10.refs_2_, bf16[200,250]{1,0:T(8,128)(2,1)S(1)} %collective-permute-done.13.refs_3_, ...), custom_call_target="tpu_custom_call" | custom-call | tf_op jit(solution)/shard_map/pallas_call | solution.py:243
  (3 shorter events, 0.0 us)
Async XLA Ops:
  0.6 16.2 %copy-start = (s32[1,4]{1,0:T(1,128)S(1)}, s32[1,4]{1,0:T(1,128)}, u32[]{:S(2)}) copy-start(s32[1,4]{1,0:T(1,128)} %code_ref.3) | copy-start | bytes 52
  1.9 9.6 %collective-permute-start = (bf16[200,512]{1,0:T(8,128)(2,1)S(1)}, bf16[200,512]{1,0:T(8,128)(2,1)S(1)}, u32[]{:S(2)}, u32[]{:S(2)}) collective-permute-start(bf16[200,512]{1,0:T(8,128)(2,1)S(1)} %get-tuple-element.28.refs_0_), channel_id=1, source_target_pairs={{0,8},{8,12},{12,4},{4,0},{1,9},{9,13},{13,5},{5,1},{2,10},{10,14}... | collective-permute-start | bytes 614408 | tf_op jit(solution)/shard_map/ppermute | solution.py:266
  6.1 11.4 %collective-permute-start.5 = (bf16[8,100,250]{2,1,0:T(8,128)(2,1)S(1)}, bf16[8,100,250]{2,1,0:T(8,128)(2,1)S(1)}, u32[]{:S(2)}, u32[]{:S(2)}) collective-permute-start(bf16[8,100,250]{2,1,0:T(8,128)(2,1)S(1)} %bitcast.7), channel_id=1, source_target_pairs={{0,2},{1,3},{2,0},{3,1},{4,6},{5,7},{6,4},{7,5},{8,10},{9,11},{10,... | collective-permute-start | bytes 1200008 | tf_op jit(solution)/shard_map/ppermute | solution.py:263
  7.6 9.0 %collective-permute-start.1 = (bf16[200,512]{1,0:T(8,128)(2,1)S(1)}, bf16[200,512]{1,0:T(8,128)(2,1)S(1)}, u32[]{:S(2)}, u32[]{:S(2)}) collective-permute-start(bf16[200,512]{1,0:T(8,128)(2,1)S(1)} %get-tuple-element.28.refs_0_), channel_id=1, source_target_pairs={{8,0},{12,8},{4,12},{0,4},{9,1},{13,9},{5,13},{1,5},{10,2},{14,10}... | collective-permute-start | bytes 614408 | tf_op jit(solution)/shard_map/ppermute | solution.py:266
  11.6 7.7 %collective-permute-start.2 = (bf16[2,202,500]{2,1,0:T(8,128)(2,1)S(1)}, bf16[2,202,500]{2,1,0:T(8,128)(2,1)S(1)}, u32[]{:S(2)}, u32[]{:S(2)}) collective-permute-start(bf16[2,202,500]{2,1,0:T(8,128)(2,1)S(1)} %shard_map.60), channel_id=1, source_target_pairs={{0,1},{1,0},{2,3},{3,2},{4,5},{5,4},{6,7},{7,6},{8,9},{9,8},{10,11... | collective-permute-start | bytes 1212008 | tf_op jit(solution)/shard_map/ppermute | solution.py:263
  11.7 9.2 %collective-permute-start.7 = (bf16[200,512]{1,0:T(8,128)(2,1)S(1)}, bf16[200,512]{1,0:T(8,128)(2,1)S(1)}, u32[]{:S(2)}, u32[]{:S(2)}) collective-permute-start(bf16[200,512]{1,0:T(8,128)(2,1)S(1)} %collective-permute-done.refs_1_), channel_id=1, source_target_pairs={{0,8},{8,12},{12,4},{4,0},{1,9},{9,13},{13,5},{5,1},{2,10},{10,14}... | collective-permute-start | bytes 614408 | tf_op jit(solution)/shard_map/ppermute | solution.py:266
  16.7 2.6 %collective-permute-start.3 = (bf16[204,500]{1,0:T(8,128)(2,1)S(1)}, bf16[204,500]{1,0:T(8,128)(2,1)S(1)}, u32[]{:S(2)}, u32[]{:S(2)}) collective-permute-start(bf16[204,500]{1,0:T(8,128)(2,1)S(1)} %shard_map.61), channel_id=1, source_target_pairs={{0,1},{1,0},{2,3},{3,2},{4,5},{5,4},{6,7},{7,6},{8,9},{9,8},{10,11... | collective-permute-start | bytes 612008 | tf_op jit(solution)/shard_map/ppermute | solution.py:263
  16.9 1.6 %collective-permute-start.4 = (bf16[201,500]{1,0:T(8,128)(2,1)S(1)}, bf16[201,500]{1,0:T(8,128)(2,1)S(1)}, u32[]{:S(2)}, u32[]{:S(2)}) collective-permute-start(bf16[201,500]{1,0:T(8,128)(2,1)S(1)} %shard_map.62), channel_id=1, source_target_pairs={{0,1},{1,0},{2,3},{3,2},{4,5},{5,4},{6,7},{7,6},{8,9},{9,8},{10,11... | collective-permute-start | bytes 603008 | tf_op jit(solution)/shard_map/ppermute | solution.py:263
  17.5 1.5 %collective-permute-start.6 = (bf16[4,100,250]{2,1,0:T(8,128)(2,1)S(1)}, bf16[4,100,250]{2,1,0:T(8,128)(2,1)S(1)}, u32[]{:S(2)}, u32[]{:S(2)}) collective-permute-start(bf16[4,100,250]{2,1,0:T(8,128)(2,1)S(1)} %shard_map.63), channel_id=1, source_target_pairs={{0,1},{1,0},{2,3},{3,2},{4,5},{5,4},{6,7},{7,6},{8,9},{9,8},{10,11... | collective-permute-start | bytes 600008 | tf_op jit(solution)/shard_map/ppermute | solution.py:263
  20.9 1.5 %collective-permute-start.8 = (bf16[200,512]{1,0:T(8,128)(2,1)S(1)}, bf16[200,512]{1,0:T(8,128)(2,1)S(1)}, u32[]{:S(2)}, u32[]{:S(2)}) collective-permute-start(bf16[200,512]{1,0:T(8,128)(2,1)S(1)} %collective-permute-done.7.mine), channel_id=1, source_target_pairs={{0,1},{1,0},{2,3},{3,2},{4,5},{5,4},{6,7},{7,6},{8,9},{9,8},{10,11... | collective-permute-start | bytes 614408 | tf_op jit(solution)/shard_map/ppermute | solution.py:263
  23.1 1.9 %collective-permute-start.11 = (f32[2,108,128]{2,1,0:T(8,128)S(1)}, f32[2,108,128]{2,1,0:T(8,128)S(1)}, u32[]{:S(2)}, u32[]{:S(2)}) collective-permute-start(f32[2,108,128]{2,1,0:T(8,128)S(1)} %get-tuple-element.45.mine_ref), channel_id=1, source_target_pairs={{0,1},{1,0},{2,3},{3,2},{4,5},{5,4},{6,7},{7,6},{8,9},{9,8},{10,11... | collective-permute-start | bytes 331784 | tf_op jit(solution)/shard_map/ppermute | solution.py:263
  23.4 11.1 %collective-permute-start.9 = (bf16[400,256]{1,0:T(8,128)(2,1)S(1)}, bf16[400,256]{1,0:T(8,128)(2,1)S(1)}, u32[]{:S(2)}, u32[]{:S(2)}) collective-permute-start(bf16[400,256]{1,0:T(8,128)(2,1)S(1)} %get-tuple-element.41), channel_id=1, source_target_pairs={{0,2},{1,3},{2,0},{3,1},{4,6},{5,7},{6,4},{7,5},{8,10},{9,11},{10,... | collective-permute-start | bytes 614408 | tf_op jit(solution)/shard_map/ppermute | solution.py:263
  24.9 9.6 %collective-permute-start.10 = (bf16[400,250]{1,0:T(8,128)(2,1)S(1)}, bf16[400,250]{1,0:T(8,128)(2,1)S(1)}, u32[]{:S(2)}, u32[]{:S(2)}) collective-permute-start(bf16[400,250]{1,0:T(8,128)(2,1)S(1)} %get-tuple-element.42), channel_id=1, source_target_pairs={{0,3},{1,2},{2,1},{3,0},{4,7},{5,6},{6,5},{7,4},{8,11},{9,10},{10,... | collective-permute-start | bytes 600008 | tf_op jit(solution)/shard_map/ppermute | solution.py:263
  25.1 3.6 %collective-permute-start.12 = (f32[2,128]{1,0:T(2,128)S(1)}, f32[2,128]{1,0:T(2,128)S(1)}, u32[]{:S(2)}, u32[]{:S(2)}) collective-permute-start(f32[2,128]{1,0:T(2,128)S(1)} %get-tuple-element.46), channel_id=1, source_target_pairs={{0,4},{4,0},{8,12},{12,8},{1,5},{5,1},{9,13},{13,9},{2,6},{6,2},{1... | collective-permute-start | bytes 3080 | tf_op jit(solution)/shard_map/ppermute | solution.py:266
  28.6 5.8 %collective-permute-start.13 = (bf16[200,250]{1,0:T(8,128)(2,1)S(1)}, bf16[200,250]{1,0:T(8,128)(2,1)S(1)}, u32[]{:S(2)}, u32[]{:S(2)}) collective-permute-start(bf16[200,250]{1,0:T(8,128)(2,1)S(1)} %get-tuple-element.47), channel_id=1, source_target_pairs={{0,1},{1,0},{2,3},{3,2},{4,5},{5,4},{6,7},{7,6},{8,9},{9,8},{10,11... | collective-permute-start | bytes 300008 | tf_op jit(solution)/shard_map/ppermute | solution.py:263
  28.7 5.8 %collective-permute-start.14 = (bf16[200,250]{1,0:T(8,128)(2,1)S(1)}, bf16[200,250]{1,0:T(8,128)(2,1)S(1)}, u32[]{:S(2)}, u32[]{:S(2)}) collective-permute-start(bf16[200,250]{1,0:T(8,128)(2,1)S(1)} %get-tuple-element.48), channel_id=1, source_target_pairs={{0,1},{1,0},{2,3},{3,2},{4,5},{5,4},{6,7},{7,6},{8,9},{9,8},{10,11... | collective-permute-start | bytes 300008 | tf_op jit(solution)/shard_map/ppermute | solution.py:263
  29.2 4.4 %collective-permute-start.15 = (f32[1,128]{1,0:T(1,128)S(1)}, f32[1,128]{1,0:T(1,128)S(1)}, u32[]{:S(2)}, u32[]{:S(2)}) collective-permute-start(f32[1,128]{1,0:T(1,128)S(1)} %get-tuple-element.51), channel_id=1, source_target_pairs={{0,8},{4,12},{8,0},{12,4},{1,9},{5,13},{9,1},{13,5},{2,10},{6,14},... | collective-permute-start | bytes 1544 | tf_op jit(solution)/shard_map/ppermute | solution.py:266

commit v9 on v8

--- a/solution.py
+++ b/solution.py
@@ -200,7 +200,7 @@
 def halve(mine_ref, arrived_ref, keep_ref, send_ref):
     ours, theirs = (ref.at[i] if len(ref.shape) == 3 else ref for i, ref in enumerate((mine_ref, arrived_ref)))
     for n in range(keep_ref.shape[0]):
-        for ref, row in ((keep_ref, 2 * n), (send_ref, 2 * n + 1)):
+        for ref, row in ((keep_ref, n), (send_ref, keep_ref.shape[0] + n)):
             ref[n:n + 1, :] = ours[row:row + 1, :] + theirs[row:row + 1, :]
 
 
@@ -368,13 +368,13 @@
         energy,
     )
     same, other = swap(same, 2), swap(other, 3)
-    arrived, n, flip = swap(energy, 1), nchol // 2, 1
+    arrived, n = swap(energy, 1), nchol // 2
     while n:
         energy, send = call(halve, (struct(n, LANES, dtype=f32),) * 2, energy, arrived)
-        arrived = turn(send, [(i, i ^ flip) for i in range(nchol)])
-        if flip == 1:
+        arrived = turn(send, [(i, i ^ n) for i in range(nchol)])
+        if n == nchol // 2:
             first_in = arrived
-        n, flip = n // 2, flip * 2
+        n //= 2
     own, *core = call(
         functools.partial(chip_walkers, nocc=nocc, **sizes),
         (struct(half, rows, padded, dtype=f32),) + (struct(half // 2 * nocc, width),) * 2,

time: 35.7 us -> 35.7 us (level)
  no operation moved by 1% of the time
where the time goes in v9:
time: 35.7 us; the launch traced here: 35.5 us
  starting transfers between devices  16.6 us (46%)
  waiting for transfers between devices  11.7 us (33%)
  Pallas kernels  6.39 us (18%)
  between operations  0.75 us (2%)
    ppermute x5, starting transfers between devices, turn(): return lax.ppermute(x, 'chol', pairs)  11.6 us
    ppermute x5, waiting for transfers between devices, turn(): return lax.ppermute(x, 'chol', pairs)  8.65 us
    pallas_call x13, Pallas kernels, call(): pl.pallas_call(kernel, out_shape=outs, in_specs=[pl.BlockSpec(memory_spac...  6.39 us
    ppermute x11, starting transfers between devices, swap(): return lax.ppermute(x, 'walk', [(i, i ^ flip) for i in range(nwalk)])  4.99 us
    ppermute x11, waiting for transfers between devices, swap(): return lax.ppermute(x, 'walk', [(i, i ^ flip) for i in range(nwalk)])  3.06 us
  transfers between devices with their start and end apart: 16, of which 9 were waited for; matrix products, arithmetic and copies ran while one was open for 0% of the time, Pallas kernels for 9%

profile of v9, /device:TPU:0, one launch (start us, length us, event | category | flops | bytes accessed | tf_op | source)
XLA Modules:
  0.0 35.5 jit_solution(8212301199872994992)
XLA Ops:
  0.6 0.0 copy-start
  0.6 1.3 %shard_map.59 = (bf16[200,512]{1,0:T(8,128)(2,1)S(1)}, bf16[100,8,250]{2,1,0:T(8,128)(2,1)S(1)}) custom-call(s32[1,100]{1,0:T(1,128)} %bitcast.12, bf16[100,1000]{1,0:T(8,128)(2,1)} %bitcast.11, bf16[100,8,250]{2,1,0:T(8,128)(2,1)} %bitcast.10), custom_call_target="tpu_custom_call" | custom-call | tf_op jit(solution)/shard_map/pallas_call | solution.py:243
  1.9 4.1 %collective-permute-start = (bf16[200,512]{1,0:T(8,128)(2,1)S(1)}, bf16[200,512]{1,0:T(8,128)(2,1)S(1)}, u32[]{:S(2)}, u32[]{:S(2)}) collective-permute-start(bf16[200,512]{1,0:T(8,128)(2,1)S(1)} %get-tuple-element.28.refs_0_), channel_id=1, source_target_pairs={{0,8},{8,12},{12,4},{4,0},{1,9},{9,13},{13,5},{5,1},{2,10},{10,14}... | collective-permute-start | bytes 614408 | tf_op jit(solution)/shard_map/ppermute | solution.py:266
  6.0 0.1 copy.8
  6.1 1.6 %collective-permute-start.5 = (bf16[8,100,250]{2,1,0:T(8,128)(2,1)S(1)}, bf16[8,100,250]{2,1,0:T(8,128)(2,1)S(1)}, u32[]{:S(2)}, u32[]{:S(2)}) collective-permute-start(bf16[8,100,250]{2,1,0:T(8,128)(2,1)S(1)} %bitcast.7), channel_id=1, source_target_pairs={{0,2},{1,3},{2,0},{3,1},{4,6},{5,7},{6,4},{7,5},{8,10},{9,11},{10,... | collective-permute-start | bytes 1200008 | tf_op jit(solution)/shard_map/ppermute | solution.py:263
  7.6 0.0 collective-permute-start.1
  7.6 3.9 %collective-permute-done.refs_1_ = bf16[200,512]{1,0:T(8,128)(2,1)S(1)} collective-permute-done((bf16[200,512]{1,0:T(8,128)(2,1)S(1)}, bf16[200,512]{1,0:T(8,128)(2,1)S(1)}, u32[]{:S(2)}, u32[]{:S(2)}) %collective-permute-start) | collective-permute-done | bytes 204832 | tf_op jit(solution)/shard_map/ppermute | solution.py:266
  11.5 0.1 shard_map.60
  11.6 0.1 collective-permute-start.2
  11.7 3.4 %collective-permute-start.7 = (bf16[200,512]{1,0:T(8,128)(2,1)S(1)}, bf16[200,512]{1,0:T(8,128)(2,1)S(1)}, u32[]{:S(2)}, u32[]{:S(2)}) collective-permute-start(bf16[200,512]{1,0:T(8,128)(2,1)S(1)} %collective-permute-done.refs_1_), channel_id=1, source_target_pairs={{0,8},{8,12},{12,4},{4,0},{1,9},{9,13},{13,5},{5,1},{2,10},{10,14}... | collective-permute-start | bytes 614408 | tf_op jit(solution)/shard_map/ppermute | solution.py:266
  15.2 1.5 %collective-permute-done.1.refs_0_.refs_2_ = bf16[200,512]{1,0:T(8,128)(2,1)S(1)} collective-permute-done((bf16[200,512]{1,0:T(8,128)(2,1)S(1)}, bf16[200,512]{1,0:T(8,128)(2,1)S(1)}, u32[]{:S(2)}, u32[]{:S(2)}) %collective-permute-start.1) | collective-permute-done | bytes 204832 | tf_op jit(solution)/shard_map/ppermute | solution.py:266
  16.6 0.1 shard_map.61
  16.7 0.1 collective-permute-start.3
  16.8 0.0 copy-done
  16.8 0.1 shard_map.62
  16.9 0.5 %collective-permute-start.4 = (bf16[201,500]{1,0:T(8,128)(2,1)S(1)}, bf16[201,500]{1,0:T(8,128)(2,1)S(1)}, u32[]{:S(2)}, u32[]{:S(2)}) collective-permute-start(bf16[201,500]{1,0:T(8,128)(2,1)S(1)} %shard_map.62), channel_id=1, source_target_pairs={{0,1},{1,0},{2,3},{3,2},{4,5},{5,4},{6,7},{7,6},{8,9},{9,8},{10,11... | collective-permute-start | bytes 603008 | tf_op jit(solution)/shard_map/ppermute | solution.py:263
  17.5 0.0 collective-permute-done.5.crossed_ref.same_ref
  17.5 0.1 collective-permute-start.6
  17.6 1.0 %collective-permute-done.4.cross_ref = bf16[201,500]{1,0:T(8,128)(2,1)S(1)} collective-permute-done((bf16[201,500]{1,0:T(8,128)(2,1)S(1)}, bf16[201,500]{1,0:T(8,128)(2,1)S(1)}, u32[]{:S(2)}, u32[]{:S(2)}) %collective-permute-start.4) | collective-permute-done | bytes 201032 | tf_op jit(solution)/shard_map/ppermute | solution.py:263
  18.6 0.5 %collective-permute-done.6.other_ref = bf16[4,100,250]{2,1,0:T(8,128)(2,1)S(1)} collective-permute-done((bf16[4,100,250]{2,1,0:T(8,128)(2,1)S(1)}, bf16[4,100,250]{2,1,0:T(8,128)(2,1)S(1)}, u32[]{:S(2)}, u32[]{:S(2)}) %collective-permute-start.6) | collective-permute-done | bytes 200032 | tf_op jit(solution)/shard_map/ppermute | solution.py:263
  19.0 0.3 shard_map.64
  19.3 0.0 collective-permute-done.3.refs_4_
  19.3 0.0 collective-permute-done.2.refs_3_
  19.4 1.5 %shard_map.65 = (f32[512,256]{1,0:T(8,128)S(1)}, f32[512,256]{1,0:T(8,128)S(1)}, f32[768,512]{1,0:T(8,128)S(1)}, bf16[768,1024]{1,0:T(8,128)(2,1)S(1)}, bf16[512,768]{1,0:T(8,128)(2,1)S(1)}) custom-call(bf16[200,512]{1,0:T(8,128)(2,1)S(1)} %get-tuple-element.28.refs_0_, bf16[200,512]{1,0:T(8,128)(2,1)S(1)} %collective-permute-done.refs_1_, ...), custom_call_target="tpu_custom_call" | custom-call | tf_op jit(solution)/shard_map/pallas_call | solution.py:243
  20.8 0.1 collective-permute-done.7.mine
  20.9 0.2 collective-permute-start.8
  21.1 0.5 %shard_map.66.first_ref = f32[6,128]{1,0:T(8,128)S(1)} custom-call(f32[768,512]{1,0:T(8,128)S(1)} %get-tuple-element.37.tmat_ref), custom_call_target="tpu_custom_call" | custom-call | tf_op jit(solution)/shard_map/pallas_call | solution.py:243
  21.6 0.8 %collective-permute-done.8.theirs = bf16[200,512]{1,0:T(8,128)(2,1)S(1)} collective-permute-done((bf16[200,512]{1,0:T(8,128)(2,1)S(1)}, bf16[200,512]{1,0:T(8,128)(2,1)S(1)}, u32[]{:S(2)}, u32[]{:S(2)}) %collective-permute-start.8) | collective-permute-done | bytes 204832 | tf_op jit(solution)/shard_map/ppermute | solution.py:263
  22.4 0.7 %shard_map.67 = (bf16[400,256]{1,0:T(8,128)(2,1)S(1)}, bf16[400,250]{1,0:T(8,128)(2,1)S(1)}, f32[2,108,128]{2,1,0:T(8,128)S(1)}, bf16[256,1024]{1,0:T(8,128)(2,1)S(1)}, bf16[512,256]{1,0:T(8,128)(2,1)S(1)}) custom-call(bf16[200,512]{1,0:T(8,128)(2,1)S(1)} %collective-permute-done.7.mine, bf16[200,512]{1,0:T(8,128)(2,1)S(1)} %collective-permute-done.8.theirs, ...), custom_call_target="tpu_custom_call" | custom-call | tf_op jit(solution)/shard_map/pallas_call | solution.py:243
  23.1 0.3 collective-permute-start.11
  23.4 1.5 %collective-permute-start.9 = (bf16[400,256]{1,0:T(8,128)(2,1)S(1)}, bf16[400,256]{1,0:T(8,128)(2,1)S(1)}, u32[]{:S(2)}, u32[]{:S(2)}) collective-permute-start(bf16[400,256]{1,0:T(8,128)(2,1)S(1)} %get-tuple-element.41), channel_id=1, source_target_pairs={{0,2},{1,3},{2,0},{3,1},{4,6},{5,7},{6,4},{7,5},{8,10},{9,11},{10,... | collective-permute-start | bytes 614408 | tf_op jit(solution)/shard_map/ppermute | solution.py:263
  24.9 0.2 collective-permute-start.10
  25.1 0.0 collective-permute-done.11.arrived_ref
  25.1 2.6 %collective-permute-start.12 = (f32[2,128]{1,0:T(2,128)S(1)}, f32[2,128]{1,0:T(2,128)S(1)}, u32[]{:S(2)}, u32[]{:S(2)}) collective-permute-start(f32[2,128]{1,0:T(2,128)S(1)} %get-tuple-element.46), channel_id=1, source_target_pairs={{0,8},{4,12},{8,0},{12,4},{1,9},{5,13},{9,1},{13,5},{2,10},{6,14},... | collective-permute-start | bytes 3080 | tf_op jit(solution)/shard_map/ppermute | solution.py:266
  27.6 0.7 %shard_map.68 = (f32[4,104,256]{2,1,0:T(8,128)S(1)}, bf16[200,250]{1,0:T(8,128)(2,1)S(1)}, bf16[200,250]{1,0:T(8,128)(2,1)S(1)}) custom-call(bf16[512,768]{1,0:T(8,128)(2,1)S(1)} %get-tuple-element.32.refs_0_, bf16[768,1024]{1,0:T(8,128)(2,1)S(1)} %get-tuple-element.33.refs_1_, bf16[512,256]{1,0:T(8,128)(2,1)S(1)} %get-tuple-element.38.refs_2_, ...), custom_call_target="tpu_custom_call" | custom-call | tf_op jit(solution)/shard_map/pallas_call | solution.py:243
  28.4 1.2 %collective-permute-done.12.arrived_ref = f32[2,128]{1,0:T(2,128)S(1)} collective-permute-done((f32[2,128]{1,0:T(2,128)S(1)}, f32[2,128]{1,0:T(2,128)S(1)}, u32[]{:S(2)}, u32[]{:S(2)}) %collective-permute-start.12) | collective-permute-done | bytes 1056 | tf_op jit(solution)/shard_map/ppermute | solution.py:266
  29.5 0.0 collective-permute-start.13
  29.6 0.5 %collective-permute-start.14 = (bf16[200,250]{1,0:T(8,128)(2,1)S(1)}, bf16[200,250]{1,0:T(8,128)(2,1)S(1)}, u32[]{:S(2)}, u32[]{:S(2)}) collective-permute-start(bf16[200,250]{1,0:T(8,128)(2,1)S(1)} %get-tuple-element.48), channel_id=1, source_target_pairs={{0,1},{1,0},{2,3},{3,2},{4,5},{5,4},{6,7},{7,6},{8,9},{9,8},{10,11... | collective-permute-start | bytes 300008 | tf_op jit(solution)/shard_map/ppermute | solution.py:263
  30.1 1.5 %collective-permute-start.15 = (f32[1,128]{1,0:T(1,128)S(1)}, f32[1,128]{1,0:T(1,128)S(1)}, u32[]{:S(2)}, u32[]{:S(2)}) collective-permute-start(f32[1,128]{1,0:T(1,128)S(1)} %get-tuple-element.51), channel_id=1, source_target_pairs={{0,4},{4,0},{8,12},{12,8},{1,5},{5,1},{9,13},{13,9},{2,6},{6,2},{1... | collective-permute-start | bytes 1544 | tf_op jit(solution)/shard_map/ppermute | solution.py:266
  31.6 2.0 %collective-permute-done.15.refs_6_ = f32[1,128]{1,0:T(1,128)S(1)} collective-permute-done((f32[1,128]{1,0:T(1,128)S(1)}, f32[1,128]{1,0:T(1,128)S(1)}, u32[]{:S(2)}, u32[]{:S(2)}) %collective-permute-start.15) | collective-permute-done | bytes 544 | tf_op jit(solution)/shard_map/ppermute | solution.py:266
  33.6 0.9 %collective-permute-done.10.refs_2_ = bf16[400,250]{1,0:T(8,128)(2,1)S(1)} collective-permute-done((bf16[400,250]{1,0:T(8,128)(2,1)S(1)}, bf16[400,250]{1,0:T(8,128)(2,1)S(1)}, u32[]{:S(2)}, u32[]{:S(2)}) %collective-permute-start.10) | collective-permute-done | bytes 200032 | tf_op jit(solution)/shard_map/ppermute | solution.py:263
  34.5 0.0 collective-permute-done.9.refs_1_
  34.5 0.0 collective-permute-done.13.refs_3_
  34.5 0.0 collective-permute-done.14.refs_4_
  34.5 1.1 %shard_map.71 = (f32[100,8,250]{2,1,0:T(8,128)}, f32[1,1]{1,0:T(1,128)}) custom-call(f32[4,104,256]{2,1,0:T(8,128)S(1)} %get-tuple-element.40.refs_0_, bf16[400,256]{1,0:T(8,128)(2,1)S(1)} %collective-permute-done.9.refs_1_, bf16[400,250]{1,0:T(8,128)(2,1)S(1)} %collective-permute-done.10.refs_2_, bf16[200,250]{1,0:T(8,128)(2,1)S(1)} %collective-permute-done.13.refs_3_, ...), custom_call_target="tpu_custom_call" | custom-call | tf_op jit(solution)/shard_map/pallas_call | solution.py:243
  (3 shorter events, 0.0 us)
Async XLA Ops:
  0.6 16.2 %copy-start = (s32[1,4]{1,0:T(1,128)S(1)}, s32[1,4]{1,0:T(1,128)}, u32[]{:S(2)}) copy-start(s32[1,4]{1,0:T(1,128)} %code_ref.3) | copy-start | bytes 52
  1.9 9.6 %collective-permute-start = (bf16[200,512]{1,0:T(8,128)(2,1)S(1)}, bf16[200,512]{1,0:T(8,128)(2,1)S(1)}, u32[]{:S(2)}, u32[]{:S(2)}) collective-permute-start(bf16[200,512]{1,0:T(8,128)(2,1)S(1)} %get-tuple-element.28.refs_0_), channel_id=1, source_target_pairs={{0,8},{8,12},{12,4},{4,0},{1,9},{9,13},{13,5},{5,1},{2,10},{10,14}... | collective-permute-start | bytes 614408 | tf_op jit(solution)/shard_map/ppermute | solution.py:266
  6.1 11.4 %collective-permute-start.5 = (bf16[8,100,250]{2,1,0:T(8,128)(2,1)S(1)}, bf16[8,100,250]{2,1,0:T(8,128)(2,1)S(1)}, u32[]{:S(2)}, u32[]{:S(2)}) collective-permute-start(bf16[8,100,250]{2,1,0:T(8,128)(2,1)S(1)} %bitcast.7), channel_id=1, source_target_pairs={{0,2},{1,3},{2,0},{3,1},{4,6},{5,7},{6,4},{7,5},{8,10},{9,11},{10,... | collective-permute-start | bytes 1200008 | tf_op jit(solution)/shard_map/ppermute | solution.py:263
  7.6 9.0 %collective-permute-start.1 = (bf16[200,512]{1,0:T(8,128)(2,1)S(1)}, bf16[200,512]{1,0:T(8,128)(2,1)S(1)}, u32[]{:S(2)}, u32[]{:S(2)}) collective-permute-start(bf16[200,512]{1,0:T(8,128)(2,1)S(1)} %get-tuple-element.28.refs_0_), channel_id=1, source_target_pairs={{8,0},{12,8},{4,12},{0,4},{9,1},{13,9},{5,13},{1,5},{10,2},{14,10}... | collective-permute-start | bytes 614408 | tf_op jit(solution)/shard_map/ppermute | solution.py:266
  11.6 7.7 %collective-permute-start.2 = (bf16[2,202,500]{2,1,0:T(8,128)(2,1)S(1)}, bf16[2,202,500]{2,1,0:T(8,128)(2,1)S(1)}, u32[]{:S(2)}, u32[]{:S(2)}) collective-permute-start(bf16[2,202,500]{2,1,0:T(8,128)(2,1)S(1)} %shard_map.60), channel_id=1, source_target_pairs={{0,1},{1,0},{2,3},{3,2},{4,5},{5,4},{6,7},{7,6},{8,9},{9,8},{10,11... | collective-permute-start | bytes 1212008 | tf_op jit(solution)/shard_map/ppermute | solution.py:263
  11.7 9.2 %collective-permute-start.7 = (bf16[200,512]{1,0:T(8,128)(2,1)S(1)}, bf16[200,512]{1,0:T(8,128)(2,1)S(1)}, u32[]{:S(2)}, u32[]{:S(2)}) collective-permute-start(bf16[200,512]{1,0:T(8,128)(2,1)S(1)} %collective-permute-done.refs_1_), channel_id=1, source_target_pairs={{0,8},{8,12},{12,4},{4,0},{1,9},{9,13},{13,5},{5,1},{2,10},{10,14}... | collective-permute-start | bytes 614408 | tf_op jit(solution)/shard_map/ppermute | solution.py:266
  16.7 2.6 %collective-permute-start.3 = (bf16[204,500]{1,0:T(8,128)(2,1)S(1)}, bf16[204,500]{1,0:T(8,128)(2,1)S(1)}, u32[]{:S(2)}, u32[]{:S(2)}) collective-permute-start(bf16[204,500]{1,0:T(8,128)(2,1)S(1)} %shard_map.61), channel_id=1, source_target_pairs={{0,1},{1,0},{2,3},{3,2},{4,5},{5,4},{6,7},{7,6},{8,9},{9,8},{10,11... | collective-permute-start | bytes 612008 | tf_op jit(solution)/shard_map/ppermute | solution.py:263
  16.9 1.6 %collective-permute-start.4 = (bf16[201,500]{1,0:T(8,128)(2,1)S(1)}, bf16[201,500]{1,0:T(8,128)(2,1)S(1)}, u32[]{:S(2)}, u32[]{:S(2)}) collective-permute-start(bf16[201,500]{1,0:T(8,128)(2,1)S(1)} %shard_map.62), channel_id=1, source_target_pairs={{0,1},{1,0},{2,3},{3,2},{4,5},{5,4},{6,7},{7,6},{8,9},{9,8},{10,11... | collective-permute-start | bytes 603008 | tf_op jit(solution)/shard_map/ppermute | solution.py:263
  17.5 1.5 %collective-permute-start.6 = (bf16[4,100,250]{2,1,0:T(8,128)(2,1)S(1)}, bf16[4,100,250]{2,1,0:T(8,128)(2,1)S(1)}, u32[]{:S(2)}, u32[]{:S(2)}) collective-permute-start(bf16[4,100,250]{2,1,0:T(8,128)(2,1)S(1)} %shard_map.63), channel_id=1, source_target_pairs={{0,1},{1,0},{2,3},{3,2},{4,5},{5,4},{6,7},{7,6},{8,9},{9,8},{10,11... | collective-permute-start | bytes 600008 | tf_op jit(solution)/shard_map/ppermute | solution.py:263
  20.9 1.5 %collective-permute-start.8 = (bf16[200,512]{1,0:T(8,128)(2,1)S(1)}, bf16[200,512]{1,0:T(8,128)(2,1)S(1)}, u32[]{:S(2)}, u32[]{:S(2)}) collective-permute-start(bf16[200,512]{1,0:T(8,128)(2,1)S(1)} %collective-permute-done.7.mine), channel_id=1, source_target_pairs={{0,1},{1,0},{2,3},{3,2},{4,5},{5,4},{6,7},{7,6},{8,9},{9,8},{10,11... | collective-permute-start | bytes 614408 | tf_op jit(solution)/shard_map/ppermute | solution.py:263
  23.1 1.9 %collective-permute-start.11 = (f32[2,108,128]{2,1,0:T(8,128)S(1)}, f32[2,108,128]{2,1,0:T(8,128)S(1)}, u32[]{:S(2)}, u32[]{:S(2)}) collective-permute-start(f32[2,108,128]{2,1,0:T(8,128)S(1)} %get-tuple-element.45.mine_ref), channel_id=1, source_target_pairs={{0,1},{1,0},{2,3},{3,2},{4,5},{5,4},{6,7},{7,6},{8,9},{9,8},{10,11... | collective-permute-start | bytes 331784 | tf_op jit(solution)/shard_map/ppermute | solution.py:263
  23.4 11.1 %collective-permute-start.9 = (bf16[400,256]{1,0:T(8,128)(2,1)S(1)}, bf16[400,256]{1,0:T(8,128)(2,1)S(1)}, u32[]{:S(2)}, u32[]{:S(2)}) collective-permute-start(bf16[400,256]{1,0:T(8,128)(2,1)S(1)} %get-tuple-element.41), channel_id=1, source_target_pairs={{0,2},{1,3},{2,0},{3,1},{4,6},{5,7},{6,4},{7,5},{8,10},{9,11},{10,... | collective-permute-start | bytes 614408 | tf_op jit(solution)/shard_map/ppermute | solution.py:263
  24.9 9.6 %collective-permute-start.10 = (bf16[400,250]{1,0:T(8,128)(2,1)S(1)}, bf16[400,250]{1,0:T(8,128)(2,1)S(1)}, u32[]{:S(2)}, u32[]{:S(2)}) collective-permute-start(bf16[400,250]{1,0:T(8,128)(2,1)S(1)} %get-tuple-element.42), channel_id=1, source_target_pairs={{0,3},{1,2},{2,1},{3,0},{4,7},{5,6},{6,5},{7,4},{8,11},{9,10},{10,... | collective-permute-start | bytes 600008 | tf_op jit(solution)/shard_map/ppermute | solution.py:263
  25.1 4.5 %collective-permute-start.12 = (f32[2,128]{1,0:T(2,128)S(1)}, f32[2,128]{1,0:T(2,128)S(1)}, u32[]{:S(2)}, u32[]{:S(2)}) collective-permute-start(f32[2,128]{1,0:T(2,128)S(1)} %get-tuple-element.46), channel_id=1, source_target_pairs={{0,8},{4,12},{8,0},{12,4},{1,9},{5,13},{9,1},{13,5},{2,10},{6,14},... | collective-permute-start | bytes 3080 | tf_op jit(solution)/shard_map/ppermute | solution.py:266
  29.5 4.9 %collective-permute-start.13 = (bf16[200,250]{1,0:T(8,128)(2,1)S(1)}, bf16[200,250]{1,0:T(8,128)(2,1)S(1)}, u32[]{:S(2)}, u32[]{:S(2)}) collective-permute-start(bf16[200,250]{1,0:T(8,128)(2,1)S(1)} %get-tuple-element.47), channel_id=1, source_target_pairs={{0,1},{1,0},{2,3},{3,2},{4,5},{5,4},{6,7},{7,6},{8,9},{9,8},{10,11... | collective-permute-start | bytes 300008 | tf_op jit(solution)/shard_map/ppermute | solution.py:263
  29.6 4.9 %collective-permute-start.14 = (bf16[200,250]{1,0:T(8,128)(2,1)S(1)}, bf16[200,250]{1,0:T(8,128)(2,1)S(1)}, u32[]{:S(2)}, u32[]{:S(2)}) collective-permute-start(bf16[200,250]{1,0:T(8,128)(2,1)S(1)} %get-tuple-element.48), channel_id=1, source_target_pairs={{0,1},{1,0},{2,3},{3,2},{4,5},{5,4},{6,7},{7,6},{8,9},{9,8},{10,11... | collective-permute-start | bytes 300008 | tf_op jit(solution)/shard_map/ppermute | solution.py:263
  30.1 3.5 %collective-permute-start.15 = (f32[1,128]{1,0:T(1,128)S(1)}, f32[1,128]{1,0:T(1,128)S(1)}, u32[]{:S(2)}, u32[]{:S(2)}) collective-permute-start(f32[1,128]{1,0:T(1,128)S(1)} %get-tuple-element.51), channel_id=1, source_target_pairs={{0,4},{4,0},{8,12},{12,8},{1,5},{5,1},{9,13},{13,9},{2,6},{6,2},{1... | collective-permute-start | bytes 1544 | tf_op jit(solution)/shard_map/ppermute | solution.py:266
